TPU v7x, 32 devices: a whole 2x2x4 slice. The times are simulated.
32 devices in a mesh: seq: 16 (over z, y, x), tp: 2 (over core).
Axes of the slice: x: 2, y: 2, z: 4, core: 2. Of those that a mesh axis runs over, the one named last changes fastest.
Arguments:
- patches: bfloat16 [4096, 1152], P('seq'), may hold values from -6 to 6
- lengths: int32 [5], replicated, may hold values from 1 to 1792, as said below
- ln1_gain: float32 [1152], replicated, may hold values from 0.1 to 1.9
- ln1_bias: float32 [1152], replicated, may hold values from -4 to 4
- q_weight: bfloat16 [1152, 1152], P('seq', 'tp'), may hold values from -0.25 to 0.25
- q_bias: float32 [1152], P('tp'), may hold values from -4 to 4
- k_weight: bfloat16 [1152, 1152], P('seq', 'tp'), may hold values from -0.1875 to 0.1875
- v_weight: bfloat16 [1152, 1152], P('seq', 'tp'), may hold values from -0.1875 to 0.1875
- v_bias: float32 [1152], P('tp'), may hold values from -4 to 4
- o_weight: bfloat16 [1152, 1152], P('tp', 'seq'), may hold values from -3 to 3
- o_bias: float32 [1152], replicated, may hold values from -4 to 4
- ln2_gain: float32 [1152], replicated, may hold values from 0.1 to 1.9
- ln2_bias: float32 [1152], replicated, may hold values from -4 to 4
- up_weight: bfloat16 [1152, 4304], P('seq', 'tp'), may hold values from -0.1875 to 0.1875
- up_bias: float32 [4304], P('tp'), may hold values from -4 to 4
- down_weight: bfloat16 [4304, 1152], P('tp', 'seq'), may hold values from -0.09375 to 0.09375
- down_bias: float32 [1152], replicated, may hold values from -4 to 4
- gate_proj: bfloat16 [1152, 14336], P('seq', 'tp'), may hold values from -0.1875 to 0.1875
- up_proj: bfloat16 [1152, 14336], P('seq', 'tp'), may hold values from -0.1875 to 0.1875
- down_proj: bfloat16 [14336, 4096], P('tp', 'seq'), may hold values from -0.046875 to 0.046875
- ctx_gain: float32 [4096], replicated, may hold values from 0.1 to 1.9
- rk_weight: bfloat16 [4096, 384], P('seq', 'tp'), may hold values from -0.09375 to 0.09375
- rv_weight: bfloat16 [4096, 384], P('seq', 'tp'), may hold values from -0.09375 to 0.09375
- latents: float32 [64, 4096], replicated, may hold values from -6 to 6
- lat_gain: float32 [4096], replicated, may hold values from 0.1 to 1.9
- rq_weight: bfloat16 [4096, 1536], P(None, 'tp'), may hold values from -0.1875 to 0.1875
- ro_weight: bfloat16 [1536, 4096], P('tp'), may hold values from -6 to 6
- feat_grad: bfloat16 [4096, 1152], P('seq'), may hold values from -6 to 6
- lat_grad: bfloat16 [64, 4096], replicated, may hold values from -6 to 6
Outputs:
- features: bfloat16 [4096, 1152], P('seq')
- latents_out: float32 [64, 4096], replicated
- patches_grad: bfloat16 [4096, 1152], P('seq')
- latents_grad: float32 [64, 4096], replicated
- ln1_gain_grad: float32 [1152], replicated
- ln1_bias_grad: float32 [1152], replicated
- q_weight_grad: float32 [1152, 1152], P('seq', 'tp')
- q_bias_grad: float32 [1152], P('tp')
- k_weight_grad: float32 [1152, 1152], P('seq', 'tp')
- v_weight_grad: float32 [1152, 1152], P('seq', 'tp')
- v_bias_grad: float32 [1152], P('tp')
- o_weight_grad: float32 [1152, 1152], P('tp', 'seq')
- o_bias_grad: float32 [1152], replicated
- ln2_gain_grad: float32 [1152], replicated
- ln2_bias_grad: float32 [1152], replicated
- up_weight_grad: float32 [1152, 4304], P('seq', 'tp')
- up_bias_grad: float32 [4304], P('tp')
- down_weight_grad: float32 [4304, 1152], P('tp', 'seq')
- down_bias_grad: float32 [1152], replicated
- gate_proj_grad: float32 [1152, 14336], P('seq', 'tp')
- up_proj_grad: float32 [1152, 14336], P('seq', 'tp')
- down_proj_grad: float32 [14336, 4096], P('tp', 'seq')
- ctx_gain_grad: float32 [4096], replicated
- rk_weight_grad: float32 [4096, 384], P('seq', 'tp')
- rv_weight_grad: float32 [4096, 384], P('seq', 'tp')
- lat_gain_grad: float32 [4096], replicated
- rq_weight_grad: float32 [4096, 1536], P('seq', 'tp')
- ro_weight_grad: float32 [1536, 4096], P('tp', 'seq')
Inputs may be any that keep to these rules, and one draw needn't show every extreme that they name: `lengths`: patches of each image; they sum to 4096; the first and the last image have exactly 1792 patches.
All inputs are finite; a program needn't handle non-finite values.
Results may differ from a plain program's by a relative error of at most 0.018.
Values may be sent and summed in bfloat16 or wider, within the bound.
A program may use at most 576 MiB of HBM per device.

v0:
```python
import jax
import jax.numpy as jnp
from jax import lax
from jax.sharding import PartitionSpec as P

HD = 72
RHD = 96
IMGMAX = 4900


EPS = 1e-06


def passed_along(value, axis, steps):
    count = lax.axis_size(axis)
    first, last = (max(0, -steps), min(count, count - steps))
    return lax.ppermute(value, axis, [(source, source + steps) for source in range(first, last)])


def joined(part, axis, combine):
    gathered = jax.tree.map(lambda a: lax.all_gather(a, axis), part)

    def take(source):
        return jax.tree.map(lambda a: lax.dynamic_index_in_dim(a, source, 0, False), gathered)

    return lax.fori_loop(
        1, lax.axis_size(axis), lambda source, state: combine(state, take(source)), take(0)
    )


def layer_norm(value, gain, bias):
    centred = value - jnp.mean(value, axis=-1, keepdims=True)
    return (
        centred * lax.rsqrt(jnp.mean(centred * centred, axis=-1, keepdims=True) + EPS) * gain + bias
    )


def rms_norm(value, gain):
    return value * lax.rsqrt(jnp.mean(value * value, axis=-1, keepdims=True) + EPS) * gain


def gelu_tanh(value):
    return jax.nn.gelu(value, approximate=True)


def product(left, right):
    return jnp.dot(left, right, preferred_element_type=jnp.float32)


def product_nt(left, right):
    return lax.dot_general(
        left, right, (((1,), (1,)), ((), ())), preferred_element_type=jnp.float32
    )


def product_tn(left, right):
    return lax.dot_general(
        left, right, (((0,), (0,)), ((), ())), preferred_element_type=jnp.float32
    )


def image_ids(lengths, positions, total_rows):
    image_ends = jnp.cumsum(lengths)
    counted = jnp.sum((image_ends[None, :] <= positions[:, None]).astype(jnp.int32), axis=1)
    inside = (positions >= 0) & (positions < total_rows)
    return jnp.where(inside, counted, -1)


def split_heads(matrix, count):
    return matrix.reshape(matrix.shape[0], count, -1).transpose(1, 0, 2)


def join_heads(stacked):
    return stacked.transpose(1, 0, 2).reshape(stacked.shape[1], -1)


def neighbour(first, second, offset):
    return passed_along((first, second), "seq", offset)


def returned(first, second, offset):
    return (
        passed_along(first.astype(jnp.bfloat16), "seq", offset).astype(first.dtype),
        passed_along(second.astype(jnp.bfloat16), "seq", offset).astype(second.dtype),
    )


def partial_stats(scores, value_heads):
    peak = jnp.max(scores, axis=-1)
    weights = jnp.exp(scores - peak[..., None])
    total = jnp.sum(weights, axis=-1)
    numer = jnp.einsum(
        "kglt,tkd->kgld", weights, value_heads.astype(jnp.float32), precision=lax.Precision.HIGHEST
    )
    return (peak, total, numer)


def joint_stats(left, right):
    peak = jnp.maximum(left[0], right[0])
    left_scale = jnp.exp(left[0] - peak)
    right_scale = jnp.exp(right[0] - peak)
    total = left[1] * left_scale + right[1] * right_scale
    numer = left[2] * left_scale[..., None] + right[2] * right_scale[..., None]
    return (peak, total, numer)


def on_device(
    patches,
    lengths,
    ln1_gain,
    ln1_bias,
    q_weight,
    q_bias,
    k_weight,
    v_weight,
    v_bias,
    o_weight,
    o_bias,
    ln2_gain,
    ln2_bias,
    up_weight,
    up_bias,
    down_weight,
    down_bias,
    gate_proj,
    up_proj,
    down_proj,
    ctx_gain,
    rk_weight,
    rv_weight,
    latents,
    lat_gain,
    rq_weight,
    ro_weight,
    feat_grad,
    lat_grad,
):
    tok_rows = patches.shape[0]
    seq_count = lax.axis_size("seq")
    seq_place = lax.axis_index("seq")
    total_rows = tok_rows * seq_count
    longest = min(IMGMAX, (seq_count // 2 - 1) * tok_rows)
    reach_blocks = (longest + tok_rows - 2) // tok_rows
    local_heads = q_bias.shape[0] // HD
    kv_heads = rk_weight.shape[1] // RHD
    q_heads = rq_weight.shape[1] // RHD
    group = q_heads // kv_heads
    lat_rows = latents.shape[0]
    scaling = HD ** (-0.5)
    lat_scaling = RHD ** (-0.5)
    first_block = (seq_place == 0).astype(jnp.float32)
    gathered = (
        lax.all_gather(q_weight, "seq", axis=0, tiled=True),
        lax.all_gather(k_weight, "seq", axis=0, tiled=True),
        lax.all_gather(v_weight, "seq", axis=0, tiled=True),
        lax.all_gather(o_weight, "seq", axis=1, tiled=True),
        lax.all_gather(up_weight, "seq", axis=0, tiled=True),
        lax.all_gather(down_weight, "seq", axis=1, tiled=True),
        lax.all_gather(gate_proj, "seq", axis=0, tiled=True),
        lax.all_gather(up_proj, "seq", axis=0, tiled=True),
        lax.all_gather(down_proj, "seq", axis=1, tiled=True),
        lax.all_gather(rk_weight, "seq", axis=0, tiled=True),
        lax.all_gather(rv_weight, "seq", axis=0, tiled=True),
    )
    (
        w_query,
        w_key,
        w_value,
        w_out,
        w_up,
        w_down,
        w_gate_proj,
        w_up_proj,
        w_down_proj,
        w_ctxkey,
        w_ctxval,
    ) = gathered
    input_f32 = patches.astype(jnp.float32)
    normed_in = layer_norm(input_f32, ln1_gain, ln1_bias).astype(jnp.bfloat16)
    queries_low = (product(normed_in, w_query) + q_bias).astype(jnp.bfloat16)
    keys_low = product(normed_in, w_key).astype(jnp.bfloat16)
    values_low = (product(normed_in, w_value) + v_bias).astype(jnp.bfloat16)
    upper_pairs = []
    lower_pairs = []
    upper_pair = (keys_low, values_low)
    lower_pair = (keys_low, values_low)
    for distance in range(1, reach_blocks + 1):
        upper_pair = neighbour(upper_pair[0], upper_pair[1], -1)
        lower_pair = neighbour(lower_pair[0], lower_pair[1], 1)
        upper_pairs.append(upper_pair)
        lower_pairs.append(lower_pair)
    ordered = lower_pairs[::-1] + [(keys_low, values_low)] + upper_pairs
    key_buffer = jnp.concatenate([pair[0] for pair in ordered], axis=0)
    value_buffer = jnp.concatenate([pair[1] for pair in ordered], axis=0)
    own_positions = seq_place * tok_rows + jnp.arange(tok_rows, dtype=jnp.int32)
    query_ids = image_ids(lengths, own_positions, total_rows)
    key_positions = (seq_place - reach_blocks) * tok_rows + jnp.arange(
        (2 * reach_blocks + 1) * tok_rows, dtype=jnp.int32
    )
    key_ids = image_ids(lengths, key_positions, total_rows)
    allowed = query_ids[:, None] == key_ids[None, :]
    query_heads = split_heads(queries_low, local_heads)
    key_heads = split_heads(key_buffer, local_heads)
    value_heads = split_heads(value_buffer, local_heads)

    def head_forward(operands):
        query_one, key_one, value_one = operands
        scores = jnp.where(allowed, product_nt(query_one, key_one) * scaling, -1e30)
        peak = jnp.max(scores, axis=1, keepdims=True)
        exponent = jnp.exp(scores - peak)
        total_exp = jnp.sum(exponent, axis=1, keepdims=True)
        probability = exponent / total_exp
        result = product(probability.astype(jnp.bfloat16), value_one)
        return (result, peak[:, 0] + jnp.log(total_exp[:, 0]))

    head_result, head_lse = lax.map(head_forward, (query_heads, key_heads, value_heads))
    attended_low = join_heads(head_result).astype(jnp.bfloat16)
    attn_sum = lax.psum(product(attended_low, w_out), "tp")
    after_attn = input_f32 + attn_sum + o_bias
    mlp_in = layer_norm(after_attn, ln2_gain, ln2_bias).astype(jnp.bfloat16)
    hidden = product(mlp_in, w_up) + up_bias
    active_low = gelu_tanh(hidden).astype(jnp.bfloat16)
    mlp_sum = lax.psum(product(active_low, w_down).astype(jnp.bfloat16), "tp").astype(jnp.float32)
    after_mlp = after_attn + mlp_sum + down_bias
    features = after_mlp.astype(jnp.bfloat16)
    proj_gate = product(features, w_gate_proj)
    proj_up = product(features, w_up_proj)
    silu_gate = jax.nn.silu(proj_gate)
    proj_hidden = (silu_gate * proj_up).astype(jnp.bfloat16)
    proj_out = lax.psum(product(proj_hidden, w_down_proj).astype(jnp.bfloat16), "tp").astype(
        jnp.float32
    )
    context_low = rms_norm(proj_out, ctx_gain).astype(jnp.bfloat16)
    ctx_keys = product(context_low, w_ctxkey).astype(jnp.bfloat16)
    ctx_values = product(context_low, w_ctxval).astype(jnp.bfloat16)
    lat_normed = rms_norm(latents, lat_gain).astype(jnp.bfloat16)
    lat_queries = product(lat_normed, rq_weight).astype(jnp.bfloat16)
    lat_keys = product(lat_normed, w_ctxkey).astype(jnp.bfloat16)
    lat_values = product(lat_normed, w_ctxval).astype(jnp.bfloat16)
    query_grouped = lat_queries.reshape(lat_rows, kv_heads, group, RHD)
    key_grouped = ctx_keys.reshape(tok_rows, kv_heads, RHD)
    value_grouped = ctx_values.reshape(tok_rows, kv_heads, RHD)
    self_keys = lat_keys.reshape(lat_rows, kv_heads, RHD)
    self_values = lat_values.reshape(lat_rows, kv_heads, RHD)
    lat_scores = (
        jnp.einsum("lkgd,tkd->kglt", query_grouped, key_grouped, preferred_element_type=jnp.float32)
        * lat_scaling
    )
    self_scores = (
        jnp.einsum("lkgd,tkd->kglt", query_grouped, self_keys, preferred_element_type=jnp.float32)
        * lat_scaling
    )
    merged = joined(partial_stats(lat_scores, value_grouped), "seq", joint_stats)
    lat_peak, lat_total, lat_numer = joint_stats(merged, partial_stats(self_scores, self_values))
    lat_lse = lat_peak + jnp.log(lat_total)
    pooled_exact = lat_numer / lat_total[..., None]
    pooled_low = pooled_exact.transpose(2, 0, 1, 3).reshape(lat_rows, -1).astype(jnp.bfloat16)
    lat_mix = product(pooled_low, ro_weight)
    ro_width = ro_weight.shape[1] // seq_count
    ro_columns = lax.dynamic_slice_in_dim(lat_grad, seq_place * ro_width, ro_width, 1)
    ro_weight_grad = product_tn(pooled_low, ro_columns)
    pooled_grad = product_nt(lat_grad, ro_weight).astype(jnp.bfloat16)
    pooled_grouped = pooled_grad.reshape(lat_rows, kv_heads, group, RHD)
    pooled_f32 = pooled_grouped.astype(jnp.float32)
    lat_delta = jnp.sum(pooled_f32.transpose(1, 2, 0, 3) * pooled_exact, axis=-1)

    def score_grads(scores, key_part, value_part):
        probability = jnp.exp(scores - lat_lse[..., None])
        dprob = jnp.einsum(
            "lkgd,tkd->kglt", pooled_grouped, value_part, preferred_element_type=jnp.float32
        )
        dscore = (probability * (dprob - lat_delta[..., None])).astype(jnp.bfloat16)
        query_term = (
            jnp.einsum("kglt,tkd->lkgd", dscore, key_part, preferred_element_type=jnp.float32)
            * lat_scaling
        )
        key_term = (
            jnp.einsum("kglt,lkgd->tkd", dscore, query_grouped, preferred_element_type=jnp.float32)
            * lat_scaling
        ).astype(jnp.bfloat16)
        value_term = jnp.einsum(
            "kglt,lkgd->tkd", probability, pooled_f32, precision=lax.Precision.HIGHEST
        ).astype(jnp.bfloat16)
        return (
            query_term,
            key_term.reshape(key_part.shape[0], -1),
            value_term.reshape(key_part.shape[0], -1),
        )

    ctx_query_term, ctx_keys_grad, ctx_values_grad = score_grads(
        lat_scores, key_grouped, value_grouped
    )
    self_query_term, self_keys_grad, self_values_grad = score_grads(
        self_scores, self_keys, self_values
    )
    query_part = ctx_query_term + first_block * self_query_term
    query_sum = lax.psum(query_part, "seq")
    lat_queries_grad = query_sum.reshape(lat_rows, -1).astype(jnp.bfloat16)
    rq_rows = rq_weight.shape[0] // seq_count
    rq_weight_grad = product_tn(
        lax.dynamic_slice_in_dim(lat_normed, seq_place * rq_rows, rq_rows, 1), lat_queries_grad
    )
    rk_part = product_tn(context_low, ctx_keys_grad) + first_block * product_tn(
        lat_normed, self_keys_grad
    )
    rv_part = product_tn(context_low, ctx_values_grad) + first_block * product_tn(
        lat_normed, self_values_grad
    )
    ctx_part = product_nt(ctx_keys_grad, w_ctxkey) + product_nt(ctx_values_grad, w_ctxval)
    lat_part = (
        product_nt(lat_queries_grad, rq_weight)
        + product_nt(self_keys_grad, w_ctxkey)
        + product_nt(self_values_grad, w_ctxval)
    )
    ctx_back, lat_back, lat_mix_sum = (
        lax.psum(ctx_part.astype(jnp.bfloat16), "tp").astype(jnp.float32),
        lax.psum(lat_part.astype(jnp.bfloat16), "tp").astype(jnp.float32),
        lax.psum(lat_mix.astype(jnp.bfloat16), "tp").astype(jnp.float32),
    )
    latents_out = latents + lat_mix_sum
    lat_pull = jax.vjp(rms_norm, latents, lat_gain)[1]
    lat_in_grad, lat_gain_grad = lat_pull(lat_back)
    latents_grad = lat_grad.astype(jnp.float32) + lat_in_grad
    ctx_pull = jax.vjp(rms_norm, proj_out, ctx_gain)[1]
    proj_out_grad, ctx_gain_part = ctx_pull(ctx_back)
    proj_out_low = proj_out_grad.astype(jnp.bfloat16)
    down_proj_part = product_tn(proj_hidden, proj_out_low)
    hidden_pgrad = product_nt(proj_out_low, w_down_proj)
    silu_pull = jax.vjp(jax.nn.silu, proj_gate)[1]
    gate_grad_low = silu_pull(hidden_pgrad * proj_up)[0].astype(jnp.bfloat16)
    up_grad_low = (hidden_pgrad * silu_gate).astype(jnp.bfloat16)
    gate_proj_part = product_tn(features, gate_grad_low)
    up_proj_part = product_tn(features, up_grad_low)
    proj_in_grad = lax.psum(
        (product_nt(gate_grad_low, w_gate_proj) + product_nt(up_grad_low, w_up_proj)).astype(
            jnp.bfloat16
        ),
        "tp",
    ).astype(jnp.float32)
    mlp_out_grad = feat_grad.astype(jnp.float32) + proj_in_grad
    mlp_out_low = mlp_out_grad.astype(jnp.bfloat16)
    down_part = product_tn(active_low, mlp_out_low)
    down_bias_part = jnp.sum(mlp_out_low.astype(jnp.float32), axis=0)
    active_grad = product_nt(mlp_out_low, w_down)
    gelu_pull = jax.vjp(gelu_tanh, hidden)[1]
    hidden_grad = gelu_pull(active_grad)[0].astype(jnp.bfloat16)
    up_part = product_tn(mlp_in, hidden_grad)
    up_bias_part = jnp.sum(hidden_grad.astype(jnp.float32), axis=0)
    mlp_back = lax.psum(product_nt(hidden_grad, w_up).astype(jnp.bfloat16), "tp").astype(
        jnp.float32
    )
    ln2_pull = jax.vjp(layer_norm, after_attn, ln2_gain, ln2_bias)[1]
    norm_grad, ln2_gain_part, ln2_bias_part = ln2_pull(mlp_back)
    attn_out_grad = mlp_out_grad + norm_grad
    attn_out_low = attn_out_grad.astype(jnp.bfloat16)
    o_part = product_tn(attended_low, attn_out_low)
    o_bias_part = jnp.sum(attn_out_low.astype(jnp.float32), axis=0)
    attended_grad = product_nt(attn_out_low, w_out).astype(jnp.bfloat16)
    grad_heads = split_heads(attended_grad, local_heads)

    def head_backward(operands):
        query_one, key_one, value_one, grad_one, lse_one = operands
        scores = jnp.where(allowed, product_nt(query_one, key_one) * scaling, -1e30)
        probability = jnp.exp(scores - lse_one[:, None])
        dprob = product_nt(grad_one, value_one)
        row_inner = jnp.sum(probability * dprob, axis=1, keepdims=True)
        score_low = (probability * (dprob - row_inner)).astype(jnp.bfloat16)
        query_one_grad = product(score_low, key_one) * scaling
        key_one_grad = product_tn(score_low, query_one) * scaling
        value_one_grad = product_tn(probability.astype(jnp.bfloat16), grad_one)
        return (query_one_grad, key_one_grad, value_one_grad)

    query_hgrad, key_hgrad, value_hgrad = lax.map(
        head_backward, (query_heads, key_heads, value_heads, grad_heads, head_lse)
    )
    key_blocks = join_heads(key_hgrad).reshape(2 * reach_blocks + 1, tok_rows, -1)
    value_blocks = join_heads(value_hgrad).reshape(2 * reach_blocks + 1, tok_rows, -1)
    key_total = key_blocks[reach_blocks]
    value_total = value_blocks[reach_blocks]
    carry_upper = (key_blocks[2 * reach_blocks], value_blocks[2 * reach_blocks])
    carry_lower = (key_blocks[0], value_blocks[0])
    for distance in range(reach_blocks - 1, 0, -1):
        moved_upper = returned(carry_upper[0], carry_upper[1], 1)
        carry_upper = (
            moved_upper[0] + key_blocks[reach_blocks + distance],
            moved_upper[1] + value_blocks[reach_blocks + distance],
        )
        moved_lower = returned(carry_lower[0], carry_lower[1], -1)
        carry_lower = (
            moved_lower[0] + key_blocks[reach_blocks - distance],
            moved_lower[1] + value_blocks[reach_blocks - distance],
        )
    moved_upper = returned(carry_upper[0], carry_upper[1], 1)
    moved_lower = returned(carry_lower[0], carry_lower[1], -1)
    key_total = key_total + moved_upper[0] + moved_lower[0]
    value_total = value_total + moved_upper[1] + moved_lower[1]
    queries_grad = join_heads(query_hgrad).astype(jnp.bfloat16)
    keys_grad = key_total.astype(jnp.bfloat16)
    values_grad = value_total.astype(jnp.bfloat16)
    q_part = product_tn(normed_in, queries_grad)
    k_part = product_tn(normed_in, keys_grad)
    v_part = product_tn(normed_in, values_grad)
    q_bias_part = jnp.sum(queries_grad.astype(jnp.float32), axis=0)
    v_bias_part = jnp.sum(values_grad.astype(jnp.float32), axis=0)
    attn_back = lax.psum(
        (
            product_nt(queries_grad, w_query)
            + product_nt(keys_grad, w_key)
            + product_nt(values_grad, w_value)
        ).astype(jnp.bfloat16),
        "tp",
    ).astype(jnp.float32)
    ln1_pull = jax.vjp(layer_norm, input_f32, ln1_gain, ln1_bias)[1]
    in_grad, ln1_gain_part, ln1_bias_part = ln1_pull(attn_back)
    patches_grad = (attn_out_grad + in_grad).astype(jnp.bfloat16)
    weight_sums = (
        lax.psum_scatter(q_part, "seq", scatter_dimension=0, tiled=True),
        lax.psum_scatter(k_part, "seq", scatter_dimension=0, tiled=True),
        lax.psum_scatter(v_part, "seq", scatter_dimension=0, tiled=True),
        lax.psum_scatter(o_part, "seq", scatter_dimension=1, tiled=True),
        lax.psum_scatter(up_part, "seq", scatter_dimension=0, tiled=True),
        lax.psum_scatter(down_part, "seq", scatter_dimension=1, tiled=True),
        lax.psum_scatter(gate_proj_part, "seq", scatter_dimension=0, tiled=True),
        lax.psum_scatter(up_proj_part, "seq", scatter_dimension=0, tiled=True),
        lax.psum_scatter(down_proj_part, "seq", scatter_dimension=1, tiled=True),
        lax.psum_scatter(rk_part, "seq", scatter_dimension=0, tiled=True),
        lax.psum_scatter(rv_part, "seq", scatter_dimension=0, tiled=True),
    )
    small_sums = lax.psum(
        (
            ln1_gain_part,
            ln1_bias_part,
            q_bias_part,
            v_bias_part,
            o_bias_part,
            ln2_gain_part,
            ln2_bias_part,
            up_bias_part,
            down_bias_part,
            ctx_gain_part,
        ),
        "seq",
    )
    return (
        features,
        latents_out,
        patches_grad,
        latents_grad,
        small_sums[0],
        small_sums[1],
        weight_sums[0],
        small_sums[2],
        weight_sums[1],
        weight_sums[2],
        small_sums[3],
        weight_sums[3],
        small_sums[4],
        small_sums[5],
        small_sums[6],
        weight_sums[4],
        small_sums[7],
        weight_sums[5],
        small_sums[8],
        weight_sums[6],
        weight_sums[7],
        weight_sums[8],
        small_sums[9],
        weight_sums[9],
        weight_sums[10],
        lat_gain_grad,
        rq_weight_grad,
        ro_weight_grad,
    )


def solution(mesh):
    placed = (
        P("seq", None),
        P(),
        P(),
        P(),
        P("seq", "tp"),
        P("tp"),
        P("seq", "tp"),
        P("seq", "tp"),
        P("tp"),
        P("tp", "seq"),
        P(),
        P(),
        P(),
        P("seq", "tp"),
        P("tp"),
        P("tp", "seq"),
        P(),
        P("seq", "tp"),
        P("seq", "tp"),
        P("tp", "seq"),
        P(),
        P("seq", "tp"),
        P("seq", "tp"),
        P(),
        P(),
        P(None, "tp"),
        P("tp", None),
        P("seq", None),
        P(),
    )
    return jax.shard_map(
        on_device,
        mesh=mesh,
        in_specs=placed,
        out_specs=(
            P("seq", None),
            P(),
            P("seq", None),
            P(),
            P(),
            P(),
            P("seq", "tp"),
            P("tp"),
            P("seq", "tp"),
            P("seq", "tp"),
            P("tp"),
            P("tp", "seq"),
            P(),
            P(),
            P(),
            P("seq", "tp"),
            P("tp"),
            P("tp", "seq"),
            P(),
            P("seq", "tp"),
            P("seq", "tp"),
            P("tp", "seq"),
            P(),
            P("seq", "tp"),
            P("seq", "tp"),
            P(),
            P("seq", "tp"),
            P("tp", "seq"),
        ),
        check_vma=False,
    )
```

profile of v0, /device:TPU:14, one launch (start us, length us, event | category | flops | bytes accessed | tf_op | source)
XLA Modules:
  0.0 7626.8 jit_solution(7265729675589362797)
XLA Ops:
  12.2 55.3 all-gather.18.cloned.1.call-done
  75.7 52.4 all-gather.20.cloned.1.call-done
  364.5 50.2 while.48
  419.8 20.5 all-reduce.18.cloned.1.call-done
  442.2 84.1 %all-gather.24.cloned.1.call-done = bf16[1152,2152]{1,0:T(8,128)(2,1)} async-done(((bf16[72,2152]{1,0:T(8,128)(2,1)}), bf16[1152,2152]{1,0:T(8,128)(2,1)}) %all-gather.24.cloned.1.call-update) | async-done | bytes 4958224 | tf_op jit(solution)/shard_map/all_gather | solution.py:157
  532.4 78.5 %all-gather.26.cloned.1.call-done = bf16[2152,1152]{0,1:T(8,128)(2,1)} async-done(((bf16[2152,72]{0,1:T(8,128)(2,1)}), bf16[2152,1152]{0,1:T(8,128)(2,1)}) %all-gather.26.cloned.1.call-update) | async-done | bytes 4958224 | tf_op jit(solution)/shard_map/all_gather | solution.py:158
  637.0 189.0 %all-gather.28.cloned.1.call-done = bf16[1152,7168]{1,0:T(8,128)(2,1)} async-done(((bf16[72,7168]{1,0:T(8,128)(2,1)}), bf16[1152,7168]{1,0:T(8,128)(2,1)}) %all-gather.28.cloned.1.call-update) | async-done | bytes 16515088 | tf_op jit(solution)/shard_map/all_gather | solution.py:159
  838.7 177.4 %all-gather.30.cloned.1.call-done = bf16[1152,7168]{1,0:T(8,128)(2,1)} async-done(((bf16[72,7168]{1,0:T(8,128)(2,1)}), bf16[1152,7168]{1,0:T(8,128)(2,1)}) %all-gather.30.cloned.1.call-update) | async-done | bytes 16515088 | tf_op jit(solution)/shard_map/all_gather | solution.py:160
  1031.7 1172.7 %all-gather.32.cloned.1.call-done = bf16[7168,4096]{1,0:T(8,128)(2,1)} async-done(((bf16[7168,256]{1,0:T(8,128)(2,1)}), bf16[7168,4096]{1,0:T(8,128)(2,1)}) %all-gather.32.cloned.1.call-update) | async-done | bytes 58720272 | tf_op jit(solution)/shard_map/all_gather | solution.py:161
  2204.4 25.0 convolution_convert_fusion
  2236.0 20.1 all-reduce.22.cloned.1.call-done
  2258.2 60.2 all-gather.34.cloned.1.call-done
  2322.3 57.6 all-gather.36.cloned.1.call-done
  2395.6 31.3 all-gather
  2427.8 35.8 all-gather.1
  2464.6 19.0 while.47
  2491.8 27.7 all-reduce.24.cloned.1.call-done
  2524.2 33.0 multiply_convert_fusion.1
  2642.8 94.4 %while.49 = (s32[]{:T(128)}, bf16[8,256,72]{1,2,0:T(8,128)(2,1)S(1)}, f32[8,3840,72]{1,2,0:T(8,128)}, f32[8,3840,72]{1,2,0:T(8,128)}, bf16[8,256,72]{2,1,0:T(8,1...) while((s32[]{:T(128)}, ...), condition=%wide.region_32.33_spmd.clone, body=%wide.region_30.32_spmd.clone.sunk | while | flops 717913856 | bytes 35014784 | solution.py:373
  2971.4 67.0 all-reduce.33
  3114.5 43.2 fusion.183
  3166.7 46.2 reduce-scatter.30.cloned.1.call-done
  3212.9 135.7 %reduce-scatter.32.cloned.1.call-done = f32[256,192]{0,1:T(8,128)} async-done(((f32[4096,192]{0,1:T(8,128)}), f32[256,192]{0,1:T(8,128)}) %reduce-scatter.32.cloned.1.call-update) | async-done | bytes 196624 | tf_op jit(solution)/shard_map/reduce_scatter | solution.py:427
  3348.6 134.8 %reduce-scatter.34.cloned.1.call-done = f32[72,576]{1,0:T(8,128)} async-done(((f32[1152,576]{1,0:T(8,128)}), f32[72,576]{1,0:T(8,128)}) %reduce-scatter.34.cloned.1.call-update) | async-done | bytes 165904
  3483.4 134.6 %reduce-scatter.40.cloned.1.call-done = f32[576,72]{0,1:T(8,128)} async-done(((f32[576,1152]{0,1:T(8,128)}), f32[576,72]{0,1:T(8,128)}) %reduce-scatter.40.cloned.1.call-update) | async-done | bytes 165904
  3618.0 134.8 %reduce-scatter.36.cloned.1.call-done = f32[72,576]{1,0:T(8,128)} async-done(((f32[1152,576]{1,0:T(8,128)}), f32[72,576]{1,0:T(8,128)}) %reduce-scatter.36.cloned.1.call-update) | async-done | bytes 165904
  3752.9 134.4 %reduce-scatter.38.cloned.1.call-done = f32[72,576]{1,0:T(8,128)} async-done(((f32[1152,576]{1,0:T(8,128)}), f32[72,576]{1,0:T(8,128)}) %reduce-scatter.38.cloned.1.call-update) | async-done | bytes 165904
  3887.3 182.0 %reduce-scatter.42.cloned.1.call-done = f32[72,2152]{1,0:T(8,128)} async-done(((f32[1152,2152]{1,0:T(8,128)}), f32[72,2152]{1,0:T(8,128)}) %reduce-scatter.42.cloned.1.call-update) | async-done | bytes 619792
  4069.3 183.1 %reduce-scatter.44.cloned.1.call-done = f32[2152,72]{0,1:T(8,128)} async-done(((f32[2152,1152]{0,1:T(8,128)}), f32[2152,72]{0,1:T(8,128)}) %reduce-scatter.44.cloned.1.call-update) | async-done | bytes 619792
  4252.4 496.1 %reduce-scatter.24.cloned.1.call-done = f32[72,7168]{1,0:T(8,128)} async-done(((f32[1152,7168]{1,0:T(8,128)}), f32[72,7168]{1,0:T(8,128)}) %reduce-scatter.24.cloned.1.call-update) | async-done | bytes 2064400 | tf_op jit(solution)/shard_map/reduce_scatter | solution.py:423
  4748.6 496.3 %reduce-scatter.26.cloned.1.call-done = f32[72,7168]{1,0:T(8,128)} async-done(((f32[1152,7168]{1,0:T(8,128)}), f32[72,7168]{1,0:T(8,128)}) %reduce-scatter.26.cloned.1.call-update) | async-done | bytes 2064400 | tf_op jit(solution)/shard_map/reduce_scatter | solution.py:424
  5244.9 2374.6 %reduce-scatter.28.cloned.1.call-done = f32[7168,256]{1,0:T(8,128)} async-done(((f32[7168,4096]{1,0:T(8,128)}), f32[7168,256]{1,0:T(8,128)}) %reduce-scatter.28.cloned.1.call-update) | async-done | bytes 7340048 | tf_op jit(solution)/shard_map/reduce_scatter | solution.py:425
  (769 shorter events, 924.9 us)
Async XLA Ops:
  7.2 60.2 all-gather.18.cloned.1.call-start
  7.9 120.2 %all-gather.20.cloned.1.call-start = ((), (), s32[]{:S(2)}) async-start(), calls=%async_computation.13 | async-start | bytes 1566720 | tf_op jit(solution)/shard_map/all_gather | solution.py:155
  8.7 280.8 %all-gather.16.cloned.1.call-start = ((), (), s32[]{:S(2)}) async-start(), calls=%async_computation.11 | async-start | bytes 1566720 | tf_op jit(solution)/shard_map/all_gather | solution.py:153
  9.5 405.3 %all-gather.22.cloned.1.call-start = ((), (), s32[]{:S(2)}) async-start(), calls=%async_computation.14 | async-start | bytes 1566720 | tf_op jit(solution)/shard_map/all_gather | solution.py:156
  69.9 66.4 collective-permute-start
  73.5 68.2 collective-permute-start.7
  201.7 238.7 %all-reduce.18.cloned.1.call-start = ((), (), s32[]{:S(2)}) async-start(), calls=%async_computation.15 | async-start | bytes 2359296 | tf_op jit(solution)/shard_map/psum | solution.py:218
  418.2 108.1 %all-gather.24.cloned.1.call-start = ((), (), s32[]{:S(2)}) async-start(), calls=%async_computation.16 | async-start | bytes 5326848 | tf_op jit(solution)/shard_map/all_gather | solution.py:157
  418.8 192.2 %all-gather.26.cloned.1.call-start = ((), (), s32[]{:S(2)}) async-start(), calls=%async_computation.17 | async-start | bytes 5326848 | tf_op jit(solution)/shard_map/all_gather | solution.py:158
  419.6 216.3 %all-reduce.20.cloned.1.call-start = ((), (), s32[]{:S(2)}) async-start(), calls=%async_computation.18 | async-start | bytes 1179648 | tf_op jit(solution)/shard_map/psum | solution.py:223
  616.9 209.1 %all-gather.28.cloned.1.call-start = ((), (), s32[]{:S(2)}) async-start(), calls=%async_computation.19 | async-start | bytes 17547264 | tf_op jit(solution)/shard_map/all_gather | solution.py:159
  617.7 398.4 %all-gather.30.cloned.1.call-start = ((), (), s32[]{:S(2)}) async-start(), calls=%async_computation.20 | async-start | bytes 17547264 | tf_op jit(solution)/shard_map/all_gather | solution.py:160
  618.3 1586.1 %all-gather.32.cloned.1.call-start = ((), (), s32[]{:S(2)}) async-start(), calls=%async_computation.21 | async-start | bytes 62390272 | tf_op jit(solution)/shard_map/all_gather | solution.py:161
  619.0 1637.0 %all-reduce.22.cloned.1.call-start = ((), (), s32[]{:S(2)}) async-start(), calls=%async_computation.22 | async-start | bytes 4194304 | tf_op jit(solution)/shard_map/psum | solution.py:230
  2229.4 89.0 %all-gather.34.cloned.1.call-start = ((), (), s32[]{:S(2)}) async-start(), calls=%async_computation.23 | async-start | bytes 1671168 | tf_op jit(solution)/shard_map/all_gather | solution.py:162
  2230.2 149.8 %all-gather.36.cloned.1.call-start = ((), (), s32[]{:S(2)}) async-start(), calls=%async_computation.24 | async-start | bytes 1671168 | tf_op jit(solution)/shard_map/all_gather | solution.py:163
  2230.8 232.9 %all-gather.38.cloned.1.call-start = ((), (), s32[]{:S(2)}) async-start(), calls=%async_computation.34 | async-start | bytes 4456448 | tf_op jit(solution)/shard_map/all_gather | solution.py:21
  2384.1 135.4 %all-reduce.24.cloned.1.call-start = ((), (), s32[]{:S(2)}) async-start(), calls=%async_computation.25 | async-start | bytes 4194304 | tf_op jit(solution)/shard_map/psum | solution.py:316
  2490.6 112.4 %all-reduce.26.cloned.1.call-start = ((), (), s32[]{:S(2)}) async-start(), calls=%async_computation.26 | async-start | bytes 1179648 | tf_op jit(solution)/shard_map/psum | solution.py:334
  2616.4 347.5 %all-reduce.30.cloned.1.call-start = ((), (), s32[]{:S(2)}) async-start(), calls=%async_computation.28 | async-start | bytes 1179648 | tf_op jit(solution)/shard_map/psum | solution.py:405
  2939.3 222.5 %all-reduce.32.cloned.1.call-start = ((), (), s32[]{:S(2)}) async-start(), calls=%async_computation.41 | async-start | bytes 2097152 | tf_op jit(solution)/shard_map/psum | solution.py:318
  3044.9 168.0 %reduce-scatter.30.cloned.1.call-start = ((), (), s32[]{:S(2)}) async-start(), calls=%async_computation.32 | async-start | bytes 3342336 | tf_op jit(solution)/shard_map/reduce_scatter | solution.py:426
  3048.6 300.0 %reduce-scatter.32.cloned.1.call-start = ((), (), s32[]{:S(2)}) async-start(), calls=%async_computation.33 | async-start | bytes 3342336 | tf_op jit(solution)/shard_map/reduce_scatter | solution.py:427
  3052.6 430.7 %reduce-scatter.34.cloned.1.call-start = ((), (), s32[]{:S(2)}) async-start(), calls=%async_computation.35 | async-start | bytes 3133440
  3056.0 562.0 %reduce-scatter.40.cloned.1.call-start = ((), (), s32[]{:S(2)}) async-start(), calls=%async_computation.38 | async-start | bytes 3133440
  3060.3 692.6 %reduce-scatter.36.cloned.1.call-start = ((), (), s32[]{:S(2)}) async-start(), calls=%async_computation.36 | async-start | bytes 3133440
  3063.7 823.6 %reduce-scatter.38.cloned.1.call-start = ((), (), s32[]{:S(2)}) async-start(), calls=%async_computation.37 | async-start | bytes 3133440
  3067.2 1002.1 %reduce-scatter.42.cloned.1.call-start = ((), (), s32[]{:S(2)}) async-start(), calls=%async_computation.39 | async-start | bytes 10653696
  3075.3 1177.1 %reduce-scatter.44.cloned.1.call-start = ((), (), s32[]{:S(2)}) async-start(), calls=%async_computation.40 | async-start | bytes 10653696
  3083.7 1664.9 %reduce-scatter.24.cloned.1.call-start = ((), (), s32[]{:S(2)}) async-start(), calls=%async_computation.29 | async-start | bytes 35094528 | tf_op jit(solution)/shard_map/reduce_scatter | solution.py:423
  3099.2 2145.7 %reduce-scatter.26.cloned.1.call-start = ((), (), s32[]{:S(2)}) async-start(), calls=%async_computation.30 | async-start | bytes 35094528 | tf_op jit(solution)/shard_map/reduce_scatter | solution.py:424
  3113.8 4505.7 %reduce-scatter.28.cloned.1.call-start = ((), (), s32[]{:S(2)}) async-start(), calls=%async_computation.31 | async-start | bytes 124780544 | tf_op jit(solution)/shard_map/reduce_scatter | solution.py:425
  (195 other events, 6421.7 us)
Sparse Core Ops, SparseCore 0:
  10.7 56.6 all-gather.17
  70.1 57.9 all-gather.19
  130.9 75.3 all-gather.15
  208.8 81.9 all-gather.21
  418.3 22.0 all-reduce.17
  443.2 82.9 all-gather.23
  529.3 81.6 all-gather.25
  617.1 18.7 all-reduce.19
  638.6 187.3 all-gather.27
  828.7 187.3 all-gather.29
  1017.6 1186.7 all-gather.31
  2229.5 26.4 all-reduce.21
  2259.2 59.1 all-gather.33
  2321.3 58.6 all-gather.35
  2384.3 76.7 all-gather.37
  2490.7 28.7 all-reduce.23
  2582.9 20.0 all-reduce.25
  2616.5 20.0 all-reduce.27
  2939.4 24.4 all-reduce.29
  3045.0 30.4 all-reduce.31
  3081.1 131.7 reduce-scatter.29
  3218.4 130.0 reduce-scatter.31
  3354.2 129.1 reduce-scatter.33
  3488.8 129.1 reduce-scatter.39
  3623.6 129.2 reduce-scatter.35
  3758.3 128.9 reduce-scatter.37
  3893.5 175.7 reduce-scatter.41
  4076.6 175.7 reduce-scatter.43
  4259.1 489.4 reduce-scatter.23
  4755.1 489.7 reduce-scatter.25
  5247.8 2371.6 reduce-scatter.27
where the time goes:
time: 7650 us; the launch traced here: 7630 us
  waiting for transfers between devices  6590 us (86%)
  matrix products  421 us (6%)
  starting transfers between devices  283 us (4%)
  blocking collectives  134 us (2%)
  local copies, waits for them, and re-layouts  108 us (1%)
    reduce_scatter x1, waiting for transfers between devices, on_device(): lax.psum_scatter(down_proj_part, 'seq', scatter_dimension=1, tiled=True)  2370 us
    all_gather x1, waiting for transfers between devices, on_device(): lax.all_gather(down_proj, 'seq', axis=1, tiled=True)  1170 us
    unnamed x37, waiting for transfers between devices  911 us
    reduce_scatter x1, waiting for transfers between devices, on_device(): lax.psum_scatter(up_proj_part, 'seq', scatter_dimension=0, tiled=True)  496 us
    reduce_scatter x1, waiting for transfers between devices, on_device(): lax.psum_scatter(gate_proj_part, 'seq', scatter_dimension=0, tiled=True)  496 us
    ppermute x56, starting transfers between devices, passed_along(): lax.ppermute(value, axis, [(source, source + steps) for source in range(f...  280 us
    all_gather x1, waiting for transfers between devices, on_device(): lax.all_gather(gate_proj, 'seq', axis=0, tiled=True)  189 us
    all_gather x1, waiting for transfers between devices, on_device(): lax.all_gather(up_proj, 'seq', axis=0, tiled=True)  177 us
  transfers between devices with their start and end apart: 87, of which 39 were waited for; matrix products, arithmetic and copies ran while one was open for 4% of the time, Pallas kernels for 0%

commit v1 on v0

--- a/solution.py
+++ b/solution.py
@@ -1,4 +1,8 @@
+import functools
+
 import jax
+import jax.experimental.pallas as pl
+import jax.experimental.pallas.tpu as pltpu
 import jax.numpy as jnp
 from jax import lax
 from jax.sharding import PartitionSpec as P
@@ -104,7 +108,7 @@
     return (peak, total, numer)
 
 
-def on_device(
+def weights_travel(
     patches,
     lengths,
     ln1_gain,
@@ -473,6 +477,947 @@
     )
 
 
+MESH = pl.DeviceIdType.MESH
+
+
+def greet(partners):
+    barrier = pltpu.get_barrier_semaphore()
+    for present, device in partners:
+
+        @pl.when(present)
+        def _():
+            pl.semaphore_signal(
+                barrier, inc=1, device_id={"seq": device}, device_id_type=MESH
+            )
+
+    pl.semaphore_wait(barrier, sum(jnp.where(present, 1, 0) for present, _ in partners))
+
+
+def place():
+    me = lax.axis_index("seq")
+    x, y, z = lax.rem(me, 2), lax.rem(lax.div(me, 2), 2), lax.div(me, 4)
+    first = lax.axis_index("tp") == 0
+    a, b = jnp.where(first, x, y), jnp.where(first, y, x)
+    step_a, step_b = jnp.where(first, 1, 2), jnp.where(first, 2, 1)
+    return me, z, a, b, step_a, step_b
+
+
+def neighbours(layers):
+    me, z, a, b, step_a, step_b = place()
+    up, down = z < layers - 1, z > 0
+    return (
+        (up, jnp.where(up, me + 4, me)),
+        (down, jnp.where(down, me - 4, me)),
+        (me >= 0, me + step_a * (1 - 2 * a)),
+        (me >= 0, me + step_b * (1 - 2 * b)),
+    )
+
+
+def gather_kernel(n, x_ref, o_ref, sent, landed, local):
+    layers = n // 4
+    me, z, a, b, step_a, step_b = place()
+    partners = neighbours(layers)
+    (up, to_up), (down, to_down), (_, to_a), (_, to_b) = partners
+    greet(partners)
+    own = pltpu.make_async_copy(x_ref, o_ref.at[me], local)
+    own.start()
+
+    def send(slot, device, way, source=None):
+        return pltpu.make_async_remote_copy(
+            src_ref=o_ref.at[slot] if source is None else source,
+            dst_ref=o_ref.at[slot],
+            send_sem=sent.at[way, slot],
+            recv_sem=landed.at[slot],
+            device_id={"seq": device},
+            device_id_type=MESH,
+        )
+
+    @pl.when(up)
+    def _():
+        send(me, to_up, 0, x_ref).start()
+
+    @pl.when(down)
+    def _():
+        send(me, to_down, 1, x_ref).start()
+
+    send(me, to_b, 3, x_ref).start()
+    send(me, to_a, 2, x_ref).start()
+    for distance in range(1, layers):
+
+        @pl.when(z >= distance)
+        def _():
+            slot = me - 4 * distance
+            send(slot, to_a, 2).wait_recv()
+
+            @pl.when(up)
+            def _():
+                send(slot, to_up, 0).start()
+
+            send(slot, to_b, 3).start()
+            send(slot, to_a, 2).start()
+
+        @pl.when(z + distance < layers)
+        def _():
+            slot = me + 4 * distance
+            send(slot, to_a, 2).wait_recv()
+
+            @pl.when(down)
+            def _():
+                send(slot, to_down, 1).start()
+
+            send(slot, to_b, 3).start()
+            send(slot, to_a, 2).start()
+
+    for distance in range(layers):
+
+        @pl.when(z >= distance)
+        def _():
+            slot = to_a - 4 * distance
+            send(slot, to_b, 3).wait_recv()
+            send(slot, to_b, 3).start()
+
+        if distance:
+
+            @pl.when(z + distance < layers)
+            def _():
+                slot = to_a + 4 * distance
+                send(slot, to_b, 3).wait_recv()
+                send(slot, to_b, 3).start()
+
+    def at(layer, of_a, of_b):
+        return layer * 4 + of_a * step_a + of_b * step_b
+
+    def arrive(layer, _):
+        send(at(layer, 0, 1 - b), to_b, 3).wait_recv()
+        send(at(layer, 1, 1 - b), to_b, 3).wait_recv()
+        return 0
+
+    lax.fori_loop(0, layers, arrive, 0)
+    own.wait()
+
+    def drain(layer, _):
+        slot = at(layer, a, b)
+        send(slot, to_a, 2).wait_send()
+        send(slot, to_b, 3).wait_send()
+        send(at(layer, 1 - a, b), to_b, 3).wait_send()
+
+        @pl.when((layer <= z) & up)
+        def _():
+            send(slot, to_up, 0).wait_send()
+
+        @pl.when((layer >= z) & down)
+        def _():
+            send(slot, to_down, 1).wait_send()
+
+        return 0
+
+    lax.fori_loop(0, layers, drain, 0)
+
+
+def gathered_blocks(x, collective_id):
+    n = lax.axis_size("seq")
+    return pl.pallas_call(
+        functools.partial(gather_kernel, n),
+        out_shape=jax.ShapeDtypeStruct((n,) + x.shape, x.dtype),
+        in_specs=[pl.BlockSpec(memory_space=pl.ANY)],
+        out_specs=pl.BlockSpec(memory_space=pl.ANY),
+        scratch_shapes=[
+            pltpu.SemaphoreType.DMA((4, n)),
+            pltpu.SemaphoreType.DMA((n,)),
+            pltpu.SemaphoreType.DMA(()),
+        ],
+        compiler_params=pltpu.CompilerParams(
+            collective_id=collective_id, has_side_effects=True
+        ),
+    )(x)
+
+
+def scatter_kernel(n, chunks, p_ref, o_ref, from_b, from_a, from_down, from_up, *semaphores):
+    layers = n // 4
+    me, z, a, b, step_a, step_b = place()
+    partners = neighbours(layers)
+    (up, to_up), (down, to_down), (_, to_a), (_, to_b) = partners
+    b_sent, b_landed, a_sent, a_landed, u_sent, u_landed, d_sent, d_landed = semaphores
+    greet(partners)
+
+    def at(layer, of_a, of_b):
+        return layer * 4 + of_a * step_a + of_b * step_b
+
+    def copy(source, target, sent, landed, device):
+        return pltpu.make_async_remote_copy(
+            src_ref=source,
+            dst_ref=target,
+            send_sem=sent,
+            recv_sem=landed,
+            device_id={"seq": device},
+            device_id_type=MESH,
+        )
+
+    def over_b(c, of_a, layer):
+        return copy(
+            p_ref.at[c, at(layer, of_a, 1 - b)],
+            from_b.at[c, of_a, layer],
+            b_sent.at[c, of_a, layer],
+            b_landed.at[c, of_a, layer],
+            to_b,
+        )
+
+    def over_a(c, layer):
+        return copy(
+            p_ref.at[c, at(layer, 1 - a, b)],
+            from_a.at[c, layer],
+            a_sent.at[c, layer],
+            a_landed.at[c, layer],
+            to_a,
+        )
+
+    def upward(c, layer):
+        return copy(
+            p_ref.at[c, at(layer, a, b)],
+            from_down.at[c, layer],
+            u_sent.at[c, layer],
+            u_landed.at[c, layer],
+            to_up,
+        )
+
+    def downward(c, layer):
+        return copy(
+            p_ref.at[c, at(layer, a, b)],
+            from_up.at[c, layer],
+            d_sent.at[c, layer],
+            d_landed.at[c, layer],
+            to_down,
+        )
+
+    def each_layer(body):
+        lax.fori_loop(0, layers, lambda layer, _: (body(layer), 0)[1], 0)
+
+    def send_b(c):
+        each_layer(lambda layer: over_b(c, 1 - a, layer).start())
+        each_layer(lambda layer: over_b(c, a, layer).start())
+
+    def send_a(c):
+        def body(layer):
+            over_b(c, 1 - a, layer).wait_recv()
+            slot = at(layer, 1 - a, b)
+            p_ref[c, slot] = p_ref[c, slot] + from_b[c, 1 - a, layer]
+            over_a(c, layer).start()
+
+        each_layer(body)
+
+    def join_line(c):
+        def body(layer):
+            over_b(c, a, layer).wait_recv()
+            over_a(c, layer).wait_recv()
+            slot = at(layer, a, b)
+            p_ref[c, slot] = p_ref[c, slot] + from_b[c, a, layer] + from_a[c, layer]
+
+            @pl.when((layer > z) & (z == 0))
+            def _():
+                upward(c, layer).start()
+
+            @pl.when((layer < z) & (z == layers - 1))
+            def _():
+                downward(c, layer).start()
+
+        each_layer(body)
+
+    def pass_up(c):
+        def body(layer):
+            @pl.when(layer > z)
+            def _():
+                upward(c, layer).wait_recv()
+                slot = at(layer, a, b)
+                p_ref[c, slot] = p_ref[c, slot] + from_down[c, layer]
+                upward(c, layer).start()
+
+        each_layer(body)
+
+    def pass_down(c):
+        def body(layer):
+            @pl.when(layer < z)
+            def _():
+                downward(c, layer).wait_recv()
+                slot = at(layer, a, b)
+                p_ref[c, slot] = p_ref[c, slot] + from_up[c, layer]
+                downward(c, layer).start()
+
+        each_layer(body)
+
+    def finish(c):
+        @pl.when(down)
+        def _():
+            upward(c, z).wait_recv()
+            p_ref[c, me] = p_ref[c, me] + from_down[c, z]
+
+        @pl.when(up)
+        def _():
+            downward(c, z).wait_recv()
+            p_ref[c, me] = p_ref[c, me] + from_up[c, z]
+
+        o_ref[c] = p_ref[c, me]
+
+    def when_chunk(step, stage):
+        @pl.when((step >= 0) & (step < chunks))
+        def _():
+            stage(jnp.clip(step, 0, chunks - 1))
+
+    send_b(0)
+
+    def step(t, _):
+        when_chunk(t + 1, send_b)
+        when_chunk(t, send_a)
+        when_chunk(t - 1, join_line)
+        inner = (z > 0) & (z < layers - 1)
+
+        @pl.when(inner)
+        def _():
+            when_chunk(t - 1 - z, pass_up)
+            when_chunk(t - layers + z, pass_down)
+
+        when_chunk(t - layers, finish)
+        return 0
+
+    lax.fori_loop(0, chunks + layers, step, 0)
+
+    def drain(c, _):
+        def body(layer):
+            over_b(c, 0, layer).wait_send()
+            over_b(c, 1, layer).wait_send()
+            over_a(c, layer).wait_send()
+
+            @pl.when(layer > z)
+            def _():
+                upward(c, layer).wait_send()
+
+            @pl.when(layer < z)
+            def _():
+                downward(c, layer).wait_send()
+
+        each_layer(body)
+        return 0
+
+    lax.fori_loop(0, chunks, drain, 0)
+
+
+def scattered_sum(terms, collective_id):
+    chunks, n = terms.shape[:2]
+    layers, block = n // 4, terms.shape[2:]
+
+    def slots(*count):
+        return pltpu.VMEM((chunks,) + count + block, terms.dtype)
+
+    def semaphores(*count):
+        return pltpu.SemaphoreType.DMA((chunks,) + count)
+
+    return pl.pallas_call(
+        functools.partial(scatter_kernel, n, chunks),
+        out_shape=jax.ShapeDtypeStruct((chunks,) + block, terms.dtype),
+        in_specs=[pl.BlockSpec(memory_space=pltpu.VMEM)],
+        out_specs=pl.BlockSpec(memory_space=pltpu.VMEM),
+        scratch_shapes=[slots(2, layers)]
+        + [slots(layers)] * 3
+        + [semaphores(2, layers)] * 2
+        + [semaphores(layers)] * 6,
+        compiler_params=pltpu.CompilerParams(
+            collective_id=collective_id, has_side_effects=True, vmem_limit_bytes=60 * 2**20
+        ),
+    )(terms)
+
+
+def exchange_kernel(group, spread, x_ref, o_ref, sent, landed, local):
+    me = lax.axis_index("seq")
+    base = lax.div(me, group) * group
+    mine = me - base
+    barrier = pltpu.get_barrier_semaphore()
+    for step in range(1, group):
+        pl.semaphore_signal(
+            barrier,
+            inc=1,
+            device_id={"seq": base + lax.rem(mine + step, group)},
+            device_id_type=MESH,
+        )
+    pl.semaphore_wait(barrier, group - 1)
+    own = pltpu.make_async_copy(x_ref if spread else x_ref.at[mine], o_ref.at[mine], local)
+    own.start()
+    copies = []
+    for step in range(1, group):
+        other = lax.rem(mine + step, group)
+        copies.append(
+            pltpu.make_async_remote_copy(
+                src_ref=x_ref if spread else x_ref.at[other],
+                dst_ref=o_ref.at[mine],
+                send_sem=sent.at[step],
+                recv_sem=landed.at[step],
+                device_id={"seq": base + other},
+                device_id_type=MESH,
+            )
+        )
+        copies[-1].start()
+    own.wait()
+    for copy in copies:
+        copy.wait()
+
+
+def exchanged(x, collective_id, group=None, spread=False):
+    group = lax.axis_size("seq") if group is None else group
+    shape = (group,) + x.shape if spread else x.shape
+    return pl.pallas_call(
+        functools.partial(exchange_kernel, group, spread),
+        out_shape=jax.ShapeDtypeStruct(shape, x.dtype),
+        in_specs=[pl.BlockSpec(memory_space=pl.ANY)],
+        out_specs=pl.BlockSpec(memory_space=pl.ANY),
+        scratch_shapes=[
+            pltpu.SemaphoreType.DMA((group,)),
+            pltpu.SemaphoreType.DMA((group,)),
+            pltpu.SemaphoreType.DMA(()),
+        ],
+        compiler_params=pltpu.CompilerParams(
+            collective_id=collective_id, has_side_effects=True
+        ),
+    )(x)
+
+
+def summed(x, collective_id):
+    n = lax.axis_size("seq")
+    shares = exchanged(x.reshape(n, -1, x.shape[1]), collective_id)
+    total = jnp.sum(shares, axis=0)
+    return exchanged(total, collective_id + 1, spread=True).reshape(x.shape)
+
+
+def swapped(value):
+    return lax.ppermute(value, "tp", [(0, 1), (1, 0)])
+
+
+def rounded(value):
+    return lax.reduce_precision(value, 8, 7)
+
+
+def paired(value):
+    kept = rounded(value)
+    return kept + swapped(kept.astype(jnp.bfloat16)).astype(jnp.float32)
+
+
+def in_order(mine, other, axis):
+    first = lax.axis_index("tp") == 0
+    return jnp.concatenate(
+        [jnp.where(first, mine, other), jnp.where(first, other, mine)], axis=axis
+    )
+
+
+def attend_kernel(scaling, q_ref, k_ref, v_ref, qid_ref, kid_ref, o_ref, lse_ref):
+    scores = product_nt(q_ref[...], k_ref[...]) * scaling
+    scores = jnp.where(qid_ref[...] == kid_ref[...], scores, -1e30)
+    peak = jnp.max(scores, axis=1, keepdims=True)
+    weights = jnp.exp(scores - peak)
+    total = jnp.sum(weights, axis=1, keepdims=True)
+    probability = (weights / total).astype(jnp.bfloat16)
+    o_ref[...] = product(probability, v_ref[...]).astype(o_ref.dtype)
+    lse_ref[...] = peak + jnp.log(total)
+
+
+def attend_back_kernel(
+    scaling, q_ref, k_ref, v_ref, g_ref, qid_ref, kid_ref, lse_ref, dq_ref, dk_ref, dv_ref
+):
+    @pl.when(pl.program_id(0) == 0)
+    def _():
+        dk_ref[...] = jnp.zeros_like(dk_ref)
+        dv_ref[...] = jnp.zeros_like(dv_ref)
+
+    scores = product_nt(q_ref[...], k_ref[...]) * scaling
+    scores = jnp.where(qid_ref[...] == kid_ref[...], scores, -1e30)
+    probability = jnp.exp(scores - lse_ref[...])
+    dprob = product_nt(g_ref[...], v_ref[...])
+    inner = jnp.sum(probability * dprob, axis=1, keepdims=True)
+    low = (probability * (dprob - inner)).astype(jnp.bfloat16)
+    dq_ref[...] = product(low, k_ref[...]) * scaling
+    dk_ref[...] += product_tn(low, q_ref[...]) * scaling
+    dv_ref[...] += product_tn(probability.astype(jnp.bfloat16), g_ref[...])
+
+
+def attention_calls(queries, window, width, tile, scaling):
+    tiled = lambda columns: pl.BlockSpec((tile, columns), lambda i: (i, 0))
+    whole = lambda rows, columns: pl.BlockSpec((rows, columns), lambda i: (0, 0))
+    params = pltpu.CompilerParams(vmem_limit_bytes=56 * 2**20)
+    forward = pl.pallas_call(
+        functools.partial(attend_kernel, scaling),
+        grid=(queries // tile,),
+        in_specs=[
+            tiled(width),
+            whole(window, width),
+            whole(window, width),
+            tiled(1),
+            whole(1, window),
+        ],
+        out_specs=[tiled(width), tiled(1)],
+        out_shape=[
+            jax.ShapeDtypeStruct((queries, width), jnp.bfloat16),
+            jax.ShapeDtypeStruct((queries, 1), jnp.float32),
+        ],
+        compiler_params=params,
+        cost_estimate=pl.CostEstimate(
+            flops=4 * queries * window * width,
+            bytes_accessed=2 * (2 * window + 2 * queries) * 128,
+            transcendentals=queries * window,
+        ),
+    )
+    backward = pl.pallas_call(
+        functools.partial(attend_back_kernel, scaling),
+        grid=(queries // tile,),
+        in_specs=[
+            tiled(width),
+            whole(window, width),
+            whole(window, width),
+            tiled(width),
+            tiled(1),
+            whole(1, window),
+            tiled(1),
+        ],
+        out_specs=[tiled(width), whole(window, width), whole(window, width)],
+        out_shape=[
+            jax.ShapeDtypeStruct((queries, width), jnp.float32),
+            jax.ShapeDtypeStruct((window, width), jnp.float32),
+            jax.ShapeDtypeStruct((window, width), jnp.float32),
+        ],
+        compiler_params=params,
+        cost_estimate=pl.CostEstimate(
+            flops=10 * queries * window * width,
+            bytes_accessed=2 * (6 * window + 4 * queries) * 128,
+            transcendentals=queries * window,
+        ),
+    )
+    return forward, backward
+
+
+def padded_columns(matrix, width):
+    return jnp.pad(matrix, ((0, 0), (0, width - matrix.shape[1])))
+
+
+def tokens_travel(
+    patches,
+    lengths,
+    ln1_gain,
+    ln1_bias,
+    q_weight,
+    q_bias,
+    k_weight,
+    v_weight,
+    v_bias,
+    o_weight,
+    o_bias,
+    ln2_gain,
+    ln2_bias,
+    up_weight,
+    up_bias,
+    down_weight,
+    down_bias,
+    gate_proj,
+    up_proj,
+    down_proj,
+    ctx_gain,
+    rk_weight,
+    rv_weight,
+    latents,
+    lat_gain,
+    rq_weight,
+    ro_weight,
+    feat_grad,
+    lat_grad,
+):
+    low = jnp.bfloat16
+    rows, width = patches.shape
+    half = rows // 2
+    n = lax.axis_size("seq")
+    me = lax.axis_index("seq")
+    core = lax.axis_index("tp")
+    total_rows = rows * n
+    longest = min(IMGMAX, (n // 2 - 1) * rows)
+    heads = q_bias.shape[0] // HD
+    part = me // heads
+    queries = total_rows // 2
+    window = total_rows - longest
+    window_start = part * longest
+    query_start = part * (queries - longest)
+    scaling = HD ** (-0.5)
+    kv_heads = rk_weight.shape[1] // RHD
+    q_heads = rq_weight.shape[1] // RHD
+    group = q_heads // kv_heads
+    lat_rows = latents.shape[0]
+    lat_scaling = RHD ** (-0.5)
+    first_block = (me == 0).astype(jnp.float32)
+    shard = q_weight.shape[0]
+    hidden_units = up_bias.shape[0]
+    hidden_pad = -(-hidden_units // 128) * 128
+    proj_units = gate_proj.shape[1] // n
+    out_width = down_proj.shape[1] * n
+
+    def my_half(value):
+        return lax.dynamic_slice_in_dim(value, core * half, half, 0)
+
+    vision_shard = jnp.concatenate(
+        [
+            padded_columns(up_weight, hidden_pad),
+            padded_columns(down_weight.T, hidden_pad),
+            o_weight.T,
+            q_weight,
+            k_weight,
+            v_weight,
+        ],
+        axis=1,
+    )
+    vision = lax.all_gather(vision_shard, "seq", axis=0, tiled=True)
+    w_up = vision[:, :hidden_units]
+    w_down_t = vision[:, hidden_pad : hidden_pad + hidden_units]
+    at = 2 * hidden_pad
+    own_width = heads * HD
+    w_out_t, w_query, w_key, w_value = (
+        vision[:, at + i * own_width : at + (i + 1) * own_width] for i in range(4)
+    )
+    w_ctx = lax.all_gather(
+        jnp.concatenate([rk_weight, rv_weight], axis=1), "seq", axis=0, tiled=True
+    )
+    ctx_width = rk_weight.shape[1]
+    w_ctxkey, w_ctxval = w_ctx[:, :ctx_width], w_ctx[:, ctx_width:]
+
+    input_f32 = patches.astype(jnp.float32)
+    normed_in = layer_norm(input_f32, ln1_gain, ln1_bias).astype(low)
+    head_shard = jnp.concatenate(
+        [split_heads(w, heads) for w in (q_weight, k_weight, v_weight)], axis=2
+    )
+    head_weight = exchanged(jnp.concatenate([head_shard] * 2, axis=0), 1).reshape(width, 3 * HD)
+    normed_half = gathered_blocks(my_half(normed_in), 2)
+    normed_half = lax.dynamic_slice_in_dim(normed_half, window_start // rows, window // rows, 0)
+    normed_window = in_order(
+        normed_half[:, None], swapped(normed_half)[:, None], 1
+    ).reshape(window, width)
+    head = me - part * heads
+    q_bias_one = lax.dynamic_slice_in_dim(q_bias, head * HD, HD, 0)
+    v_bias_one = lax.dynamic_slice_in_dim(v_bias, head * HD, HD, 0)
+    bias_one = jnp.concatenate([q_bias_one, jnp.zeros_like(q_bias_one), v_bias_one])
+    qkv = (product(normed_window, head_weight) + bias_one).astype(low)
+    query_one = lax.dynamic_slice_in_dim(qkv[:, :HD], query_start, queries, 0)
+    key_one = qkv[:, HD : 2 * HD]
+    value_one = qkv[:, 2 * HD :]
+    key_ids = image_ids(
+        lengths, window_start + jnp.arange(window, dtype=jnp.int32), total_rows
+    )
+    query_ids = lax.dynamic_slice_in_dim(key_ids, query_start, queries, 0)[:, None]
+    key_ids = key_ids[None, :]
+    attend, attend_back = attention_calls(queries, window, HD, rows, scaling)
+    attended_one, lse_one = attend(query_one, key_one, value_one, query_ids, key_ids)
+    attended_low = join_heads(exchanged(attended_one.reshape(heads, rows, HD), 3, group=heads))
+
+    def to_units(matrix):
+        blocks = matrix.reshape(shard, n, proj_units).transpose(1, 0, 2)
+        return lax.all_to_all(blocks, "seq", 0, 0).reshape(width, proj_units)
+
+    gate_mine, up_mine = to_units(gate_proj), to_units(up_proj)
+    down_mine = (
+        lax.all_to_all(down_proj.reshape(n, proj_units, -1), "seq", 0, 0)
+        .transpose(1, 0, 2)
+        .reshape(proj_units, out_width)
+    )
+    w_gate = jnp.concatenate([gate_mine, swapped(gate_mine)], axis=1)
+    w_up_proj = jnp.concatenate([up_mine, swapped(up_mine)], axis=1)
+    w_down_proj = jnp.concatenate([down_mine, swapped(down_mine)], axis=0)
+
+    attn_part = product_nt(attended_low, w_out_t)
+    attn_sum = attn_part + swapped(attn_part)
+    after_attn = input_f32 + attn_sum + o_bias
+    mlp_in = layer_norm(after_attn, ln2_gain, ln2_bias).astype(low)
+    hidden = product(mlp_in, w_up) + up_bias
+    active_low = gelu_tanh(hidden).astype(low)
+    after_mlp = after_attn + paired(product_nt(active_low, w_down_t)) + down_bias
+    features = after_mlp.astype(low)
+
+    features_all = gathered_blocks(my_half(features), 4).reshape(n * half, width)
+    proj_gate = product(features_all, w_gate)
+    proj_up = product(features_all, w_up_proj)
+    silu_gate = jax.nn.silu(proj_gate)
+    proj_hidden = (silu_gate * proj_up).astype(low)
+
+    def chunked(terms, chunks):
+        return terms.reshape(n, half, chunks, -1).transpose(2, 0, 1, 3)
+
+    def joined_chunks(sums):
+        return sums.transpose(1, 0, 2).reshape(half, -1)
+
+    out_chunks = out_width // 512
+    out_terms = jnp.stack(
+        [
+            product(proj_hidden, w_down_proj[:, c * 512 : (c + 1) * 512]).astype(low)
+            for c in range(out_chunks)
+        ]
+    ).reshape(out_chunks, n, half, 512)
+    proj_out_low = joined_chunks(scattered_sum(out_terms, 5))
+    proj_out_half = proj_out_low.astype(jnp.float32)
+    proj_out = in_order(proj_out_low, swapped(proj_out_low), 0).astype(jnp.float32)
+
+    context_low = rms_norm(proj_out, ctx_gain).astype(low)
+    ctx_keys = product(context_low, w_ctxkey).astype(low)
+    ctx_values = product(context_low, w_ctxval).astype(low)
+    lat_normed = rms_norm(latents, lat_gain).astype(low)
+    lat_queries = product(lat_normed, rq_weight).astype(low)
+    lat_keys = product(lat_normed, w_ctxkey).astype(low)
+    lat_values = product(lat_normed, w_ctxval).astype(low)
+    query_grouped = lat_queries.reshape(lat_rows, kv_heads, group, RHD)
+    key_grouped = ctx_keys.reshape(rows, kv_heads, RHD)
+    value_grouped = ctx_values.reshape(rows, kv_heads, RHD)
+    self_keys = lat_keys.reshape(lat_rows, kv_heads, RHD)
+    self_values = lat_values.reshape(lat_rows, kv_heads, RHD)
+    lat_scores = (
+        jnp.einsum("lkgd,tkd->kglt", query_grouped, key_grouped, preferred_element_type=jnp.float32)
+        * lat_scaling
+    )
+    self_scores = (
+        jnp.einsum("lkgd,tkd->kglt", query_grouped, self_keys, preferred_element_type=jnp.float32)
+        * lat_scaling
+    )
+    stats = partial_stats(lat_scores, value_grouped)
+    packed = jnp.concatenate([stats[2], stats[0][..., None], stats[1][..., None]], axis=-1)
+    packed = jnp.pad(packed.reshape(n, -1, RHD + 2), ((0, 0), (0, 0), (0, 126 - RHD)))
+    shares = exchanged(packed, 6)
+    share_peak = jnp.max(shares[..., RHD], axis=0)
+    share_scale = jnp.exp(shares[..., RHD] - share_peak)
+    share_sums = jnp.sum(shares * share_scale[..., None], axis=0)
+    share_sums = jnp.where(
+        jnp.arange(128) == RHD, share_peak[:, None], share_sums
+    )
+    merged = exchanged(share_sums, 7, spread=True).reshape(kv_heads, group, lat_rows, 128)
+    lat_peak, lat_total, lat_numer = joint_stats(
+        (merged[..., RHD], merged[..., RHD + 1], merged[..., :RHD]),
+        partial_stats(self_scores, self_values),
+    )
+    lat_lse = lat_peak + jnp.log(lat_total)
+    pooled_exact = lat_numer / lat_total[..., None]
+    pooled_low = pooled_exact.transpose(2, 0, 1, 3).reshape(lat_rows, -1).astype(low)
+    lat_mix = product(pooled_low, ro_weight)
+    ro_width = ro_weight.shape[1] // n
+    ro_columns = lax.dynamic_slice_in_dim(lat_grad, me * ro_width, ro_width, 1)
+    ro_weight_grad = product_tn(pooled_low, ro_columns)
+    pooled_grad = product_nt(lat_grad, ro_weight).astype(low)
+    pooled_grouped = pooled_grad.reshape(lat_rows, kv_heads, group, RHD)
+    pooled_f32 = pooled_grouped.astype(jnp.float32)
+    lat_delta = jnp.sum(pooled_f32.transpose(1, 2, 0, 3) * pooled_exact, axis=-1)
+
+    def score_grads(scores, key_part, value_part):
+        probability = jnp.exp(scores - lat_lse[..., None])
+        dprob = jnp.einsum(
+            "lkgd,tkd->kglt", pooled_grouped, value_part, preferred_element_type=jnp.float32
+        )
+        dscore = (probability * (dprob - lat_delta[..., None])).astype(low)
+        query_term = (
+            jnp.einsum("kglt,tkd->lkgd", dscore, key_part, preferred_element_type=jnp.float32)
+            * lat_scaling
+        )
+        key_term = (
+            jnp.einsum("kglt,lkgd->tkd", dscore, query_grouped, preferred_element_type=jnp.float32)
+            * lat_scaling
+        ).astype(low)
+        value_term = jnp.einsum(
+            "kglt,lkgd->tkd", probability, pooled_f32, precision=lax.Precision.HIGHEST
+        ).astype(low)
+        return (
+            query_term,
+            key_term.reshape(key_part.shape[0], -1),
+            value_term.reshape(key_part.shape[0], -1),
+        )
+
+    ctx_query_term, ctx_keys_grad, ctx_values_grad = score_grads(
+        lat_scores, key_grouped, value_grouped
+    )
+    self_query_term, self_keys_grad, self_values_grad = score_grads(
+        self_scores, self_keys, self_values
+    )
+    ctx_part = product_nt(ctx_keys_grad, w_ctxkey) + product_nt(ctx_values_grad, w_ctxval)
+    ctx_kept = rounded(my_half(ctx_part))
+    ctx_sent = lax.dynamic_slice_in_dim(ctx_part, (1 - core) * half, half, 0).astype(low)
+    ctx_back = ctx_kept + swapped(ctx_sent).astype(jnp.float32)
+    ctx_pull = jax.vjp(rms_norm, proj_out_half, ctx_gain)[1]
+    proj_out_grad, ctx_gain_part = ctx_pull(ctx_back)
+    proj_out_grads = gathered_blocks(proj_out_grad.astype(low), 8).reshape(n * half, out_width)
+
+    query_part = ctx_query_term + first_block * self_query_term
+    query_sum = summed(query_part.reshape(lat_rows, -1), 9)
+    lat_queries_grad = query_sum.astype(low)
+    rq_rows = rq_weight.shape[0] // n
+    rq_weight_grad = product_tn(
+        lax.dynamic_slice_in_dim(lat_normed, me * rq_rows, rq_rows, 1), lat_queries_grad
+    )
+    ctx_grads = jnp.concatenate([ctx_keys_grad, ctx_values_grad], axis=1)
+    self_grads = jnp.concatenate([self_keys_grad, self_values_grad], axis=1)
+    r_part = product_tn(context_low, ctx_grads) + first_block * product_tn(lat_normed, self_grads)
+    r_grad = lax.psum_scatter(r_part.astype(low), "seq", scatter_dimension=0, tiled=True).astype(
+        jnp.float32
+    )
+    lat_part = (
+        product_nt(lat_queries_grad, rq_weight)
+        + product_nt(self_keys_grad, w_ctxkey)
+        + product_nt(self_values_grad, w_ctxval)
+    )
+    lat_back, lat_mix_sum = paired(lat_part), paired(lat_mix)
+    latents_out = latents + lat_mix_sum
+    lat_pull = jax.vjp(rms_norm, latents, lat_gain)[1]
+    lat_in_grad, lat_gain_grad = lat_pull(lat_back)
+    latents_grad = lat_grad.astype(jnp.float32) + lat_in_grad
+
+    hidden_pgrad = product_nt(proj_out_grads, w_down_proj)
+    silu_pull = jax.vjp(jax.nn.silu, proj_gate)[1]
+    gate_grad_low = silu_pull(hidden_pgrad * proj_up)[0].astype(low)
+    up_grad_low = (hidden_pgrad * silu_gate).astype(low)
+    feat_terms = (product_nt(gate_grad_low, w_gate) + product_nt(up_grad_low, w_up_proj)).astype(low)
+    feat_half = joined_chunks(scattered_sum(chunked(feat_terms, width // 384), 11))
+    proj_in_grad = in_order(feat_half, swapped(feat_half), 0).astype(jnp.float32)
+
+    def unit_grads(left, right, axis):
+        mine = lax.slice_in_dim(left, 0, proj_units, axis=1) if axis == 0 else left
+        other = lax.slice_in_dim(left, proj_units, 2 * proj_units, axis=1) if axis == 0 else left
+        mine_r = right if axis == 0 else lax.slice_in_dim(right, 0, proj_units, axis=1)
+        other_r = right if axis == 0 else lax.slice_in_dim(right, proj_units, 2 * proj_units, axis=1)
+        sent = swapped(product_tn(other, other_r).astype(low))
+        return (product_tn(mine, mine_r) + sent.astype(jnp.float32)).astype(low)
+
+    def to_rows(grad):
+        blocks = lax.all_to_all(grad.reshape(n, shard, proj_units), "seq", 0, 0)
+        return blocks.transpose(1, 0, 2).reshape(shard, n * proj_units).astype(jnp.float32)
+
+    gate_proj_grad = to_rows(unit_grads(features_all, gate_grad_low, 1))
+    up_proj_grad = to_rows(unit_grads(features_all, up_grad_low, 1))
+    down_blocks = unit_grads(proj_hidden, proj_out_grads, 0)
+    down_blocks = down_blocks.reshape(proj_units, n, -1).transpose(1, 0, 2)
+    down_proj_grad = (
+        lax.all_to_all(down_blocks, "seq", 0, 0)
+        .reshape(n * proj_units, -1)
+        .astype(jnp.float32)
+    )
+
+    mlp_out_grad = feat_grad.astype(jnp.float32) + proj_in_grad
+    mlp_out_low = mlp_out_grad.astype(low)
+    down_part_t = product_tn(mlp_out_low, active_low)
+    down_bias_part = jnp.sum(mlp_out_low.astype(jnp.float32), axis=0)
+    active_grad = product(mlp_out_low, w_down_t)
+    gelu_pull = jax.vjp(gelu_tanh, hidden)[1]
+    hidden_grad = gelu_pull(active_grad)[0].astype(low)
+    up_part = product_tn(mlp_in, hidden_grad)
+    up_bias_part = jnp.sum(hidden_grad.astype(jnp.float32), axis=0)
+    mlp_back = paired(product_nt(hidden_grad, w_up))
+    ln2_pull = jax.vjp(layer_norm, after_attn, ln2_gain, ln2_bias)[1]
+    norm_grad, ln2_gain_part, ln2_bias_part = ln2_pull(mlp_back)
+    attn_out_grad = mlp_out_grad + norm_grad
+    attn_out_low = attn_out_grad.astype(low)
+    o_part_t = product_tn(attn_out_low, attended_low)
+    o_bias_part = jnp.sum(attn_out_low.astype(jnp.float32), axis=0)
+    vision_part = jnp.concatenate(
+        [
+            padded_columns(up_part.astype(low), hidden_pad),
+            padded_columns(down_part_t.astype(low), hidden_pad),
+            o_part_t.astype(low),
+        ],
+        axis=1,
+    )
+    vision_grad = lax.psum_scatter(vision_part, "seq", scatter_dimension=0, tiled=True).astype(
+        jnp.float32
+    )
+    up_weight_grad = vision_grad[:, :hidden_units]
+    down_weight_grad = vision_grad[:, hidden_pad : hidden_pad + hidden_units].T
+    o_weight_grad = vision_grad[:, 2 * hidden_pad :].T
+
+    attended_grad = product(attn_out_low, w_out_t).astype(low)
+    grad_one = exchanged(split_heads(attended_grad, heads), 12, group=heads).reshape(queries, HD)
+    dq, dk, dv = attend_back(
+        query_one, key_one, value_one, grad_one, query_ids, key_ids, lse_one
+    )
+    dq_window = lax.dynamic_update_slice_in_dim(
+        jnp.zeros((window, HD), jnp.float32), dq, query_start, 0
+    )
+    dqkv = jnp.concatenate([dq_window, dk, dv], axis=1)
+    dqkv_low = dqkv.astype(low)
+    head_grad = product_tn(normed_window, dqkv_low).astype(low).reshape(n, shard, 3 * HD)
+    head_grads = exchanged(head_grad, 13).astype(jnp.float32)
+    head_grads = head_grads[:heads] + head_grads[heads:]
+    q_weight_grad, k_weight_grad, v_weight_grad = (
+        join_heads(head_grads[:, :, i * HD : (i + 1) * HD]) for i in range(3)
+    )
+    bias_row = jnp.sum(dqkv_low.astype(jnp.float32), axis=0)
+    bias_rows = jnp.zeros((heads, 3 * HD), jnp.float32)
+    bias_rows = lax.dynamic_update_slice_in_dim(bias_rows, bias_row[None], head, 0)
+    blocks = dqkv.reshape(window // rows, rows, 3 * HD)
+    other_block = jnp.where(part == 0, blocks[-1], blocks[0]).astype(low)
+    across = lax.ppermute(
+        other_block, "seq", [(i, (i + heads) % n) for i in range(n)]
+    ).astype(jnp.float32)
+    own_blocks = lax.dynamic_slice_in_dim(blocks, part, heads, 0)
+    edge = jnp.where(part == 0, heads - 1, 0)
+    own_blocks = own_blocks + jnp.where(
+        (jnp.arange(heads) == edge)[:, None, None], across[None], 0.0
+    )
+    token_grads = exchanged(own_blocks.astype(low), 14, group=heads)
+    queries_grad, keys_grad, values_grad = (
+        join_heads(token_grads[:, :, i * HD : (i + 1) * HD]) for i in range(3)
+    )
+    attn_back = paired(
+        product_nt(queries_grad, w_query)
+        + product_nt(keys_grad, w_key)
+        + product_nt(values_grad, w_value)
+    )
+    ln1_pull = jax.vjp(layer_norm, input_f32, ln1_gain, ln1_bias)[1]
+    in_grad, ln1_gain_part, ln1_bias_part = ln1_pull(attn_back)
+    patches_grad = (attn_out_grad + in_grad).astype(low)
+
+    smalls = (
+        ln1_gain_part,
+        ln1_bias_part,
+        bias_rows[:, :HD].reshape(-1),
+        bias_rows[:, 2 * HD :].reshape(-1),
+        o_bias_part,
+        ln2_gain_part,
+        ln2_bias_part,
+        up_bias_part,
+        down_bias_part,
+        ctx_gain_part,
+    )
+    joined_smalls = jnp.concatenate(smalls)
+    length = joined_smalls.shape[0]
+    per_device = -(-length // (n * 1024)) * 1024
+    joined_smalls = jnp.pad(joined_smalls, (0, n * per_device - length))
+    small_sum = summed(joined_smalls.reshape(n * per_device // 128, 128), 15).reshape(-1)
+    small_sums, begin = [], 0
+    for small in smalls:
+        small_sums.append(small_sum[begin : begin + small.shape[0]])
+        begin += small.shape[0]
+    ctx_gain_grad = small_sums[9] + swapped(small_sums[9])
+    return (
+        features,
+        latents_out,
+        patches_grad,
+        latents_grad,
+        small_sums[0],
+        small_sums[1],
+        q_weight_grad,
+        small_sums[2],
+        k_weight_grad,
+        v_weight_grad,
+        small_sums[3],
+        o_weight_grad,
+        small_sums[4],
+        small_sums[5],
+        small_sums[6],
+        up_weight_grad,
+        small_sums[7],
+        down_weight_grad,
+        small_sums[8],
+        gate_proj_grad,
+        up_proj_grad,
+        down_proj_grad,
+        ctx_gain_grad,
+        r_grad[:, :ctx_width],
+        r_grad[:, ctx_width:],
+        lat_gain_grad,
+        rq_weight_grad,
+        ro_weight_grad,
+    )
+
+
 def solution(mesh):
     placed = (
         P("seq", None),
@@ -505,8 +1450,9 @@
         P("seq", None),
         P(),
     )
+    few = mesh.shape["tp"] == 2 and mesh.shape["seq"] == 16
     return jax.shard_map(
-        on_device,
+        tokens_travel if few else weights_travel,
         mesh=mesh,
         in_specs=placed,
         out_specs=(

time: 7650 us -> 1700 us (0.22)
  waiting for transfers between devices: 6590 us -> 308 us
  Pallas kernels: 0 us -> 842 us
  starting transfers between devices: 283 us -> 68.3 us
  matrix products: 421 us -> 227 us
  blocking collectives: 134 us -> 0 us
    reduce_scatter x5 -> x1, waiting for transfers between devices: 3550 us -> 0.01 us  [tokens_travel(): lax.psum_scatter(r_part.astype(low), 'seq', scatter_dimension=0, tiled=True)]
    all_gather x12 -> x2, waiting for transfers between devices: 1930 us -> 0.04 us  [the longest x1 0.02 us: tokens_travel(): vision = lax.all_gather(vision_shard, 'seq', axis=0, tiled=True)]
    pallas_call x0 -> x18, Pallas kernels: none -> 842 us  [the longest x3 326 us: gathered_blocks(): pl.pallas_call(functools.partial(gather_kernel, n), out_shape=jax.ShapeDt...]
    unnamed x37 -> x5, waiting for transfers between devices: 911 us -> 104 us
    ppermute x56 -> x18, starting transfers between devices: 280 us -> 5.34 us  [the longest x17 2.92 us: swapped(): return lax.ppermute(value, 'tp', [(0, 1), (1, 0)])]
    psum x8 -> x0, waiting for transfers between devices: 129 us -> none  [the longest x1 27.7 us: on_device(): lax.psum(ctx_part.astype(jnp.bfloat16), 'tp').astype(jnp.float32)]
    all_to_all x0 -> x6, waiting for transfers between devices: none -> 86 us  [the longest x2 43.9 us: to_units(): return lax.all_to_all(blocks, 'seq', 0, 0).reshape(width, proj_units)]
  transfers between devices with their start and end apart: 87 -> 28, of which waited for: 39 -> 4; matrix products, arithmetic and copies ran while one was open for 4% -> 24% of each run, Pallas kernels for 0% -> 48%
where the time goes in v1:
time: 1700 us; the launch traced here: 1690 us
  Pallas kernels  842 us (50%)
  waiting for transfers between devices  308 us (18%)
  matrix products  227 us (13%)
  local copies, waits for them, and re-layouts  143 us (8%)
  other arithmetic  87.2 us (5%)
  starting transfers between devices  68.3 us (4%)
  between operations  17 us (1%)
    pallas_call x3, Pallas kernels, gathered_blocks(): pl.pallas_call(functools.partial(gather_kernel, n), out_shape=jax.ShapeDt...  326 us
    pallas_call x11, Pallas kernels, exchanged(): pl.pallas_call(functools.partial(exchange_kernel, group, spread), out_sha...  252 us
    pallas_call x2, Pallas kernels, scattered_sum(): pl.pallas_call(functools.partial(scatter_kernel, n, chunks), out_shape=ja...  228 us
    ppermute x1, waiting for transfers between devices, tokens_travel(): lax.ppermute(other_block, 'seq', [(i, (i + heads) % n) for i in range(n)])  118 us
    unnamed x5, waiting for transfers between devices  104 us
    dot_general x15, matrix products, product_nt(): lax.dot_general(left, right, (((1,), (1,)), ((), ())), preferred_element_...  75 us
    dot_general x20, matrix products, product(): return jnp.dot(left, right, preferred_element_type=jnp.float32)  73.5 us
    dot_general x14, matrix products, product_tn(): lax.dot_general(left, right, (((0,), (0,)), ((), ())), preferred_element_...  69.8 us
  transfers between devices with their start and end apart: 28, of which 4 were waited for; matrix products, arithmetic and copies ran while one was open for 24% of the time, Pallas kernels for 48%

profile of v1, /device:TPU:14, one launch (start us, length us, event | category | flops | bytes accessed | tf_op | source)
XLA Modules:
  0.0 1692.6 jit_solution(12694908053589437069)
XLA Ops:
  26.5 43.9 %all-to-all-done = bf16[16,72,448]{2,1,0:T(8,128)(2,1)S(1)} async-done(((bf16[16,72,448]{2,1,0:T(8,128)(2,1)}), bf16[16,72,448]{2,1,0:T(8,128)(2,1)S(1)}, u32[]{:S(2)}, u32[]{:S(2)}) %all-to-all-start) | async-done | bytes 1032224 | tf_op jit(solution)/shard_map/all_to_all | solution.py:1112
  77.6 129.3 %shard_map.492 = bf16[16,128,1152]{2,1,0:T(8,128)(2,1)} custom-call(bf16[128,1152]{1,0:T(8,128)(2,1)} %fusion.124.x_ref), custom_call_target="tpu_custom_call" | custom-call | tf_op jit(solution)/shard_map/pallas_call | solution.py:619
  208.0 30.1 %all-to-all-start.2 = ((bf16[16,448,256]{2,1,0:T(8,128)(2,1)}), bf16[16,448,256]{2,1,0:T(8,128)(2,1)}, u32[]{:S(2)}, u32[]{:S(2)}) async-start(bf16[16,448,256]{2,1,0:T(8,128)(2,1)} %bitcast.312), calls=%async_computation.2 | async-start | bytes 7340032 | tf_op jit(solution)/shard_map/all_to_all | solution.py:1116
  246.2 116.6 %shard_map.493 = bf16[16,72,216]{2,1,0:T(8,128)(2,1)} custom-call(bf16[16,72,216]{2,1,0:T(8,128)(2,1)} %maximum_maximum_fusion.x_ref), custom_call_target="tpu_custom_call" | custom-call | tf_op jit(solution)/shard_map/pallas_call | solution.py:865
  374.3 14.6 shard_map.494
  388.8 14.8 shard_map.495
  455.8 45.5 %shard_map.496 = bf16[16,128,1152]{2,1,0:T(8,128)(2,1)} custom-call(bf16[128,1152]{1,0:T(8,128)(2,1)} %constant_dynamic-slice_fusion.x_ref), custom_call_target="tpu_custom_call" | custom-call | tf_op jit(solution)/shard_map/pallas_call | solution.py:619
  501.4 11.0 fusion.82
  512.4 12.1 multiply_convert_fusion.1
  559.6 165.2 %shard_map.497 = bf16[8,128,512]{2,1,0:T(8,128)(2,1)} custom-call(bf16[8,16,128,512]{3,2,1,0:T(8,128)(2,1)} %constant_dynamic-update-slice_fusion.2.p_ref), custom_call_target="tpu_custom_call" | custom-call | tf_op jit(solution)/shard_map/pallas_call | solution.py:813
  748.3 13.4 shard_map.498
  766.6 10.2 shard_map.499
  796.0 10.1 shard_map.505
  807.7 10.8 shard_map.506
  842.1 150.8 %shard_map.500 = bf16[16,128,4096]{2,1,0:T(8,128)(2,1)} custom-call(bf16[128,4096]{1,0:T(8,128)(2,1)} %fusion.45.x_ref), custom_call_target="tpu_custom_call" | custom-call | tf_op jit(solution)/shard_map/pallas_call | solution.py:619
  992.9 13.1 convolution_convert_fusion.2
  1006.0 31.3 %fusion.7 = (bf16[2048,896]{0,1:T(8,128)(2,1)}, bf16[2048,896]{0,1:T(8,128)(2,1)}) fusion(f32[2048,896]{0,1:T(8,128)} %fusion.82, f32[2048,896]{0,1:T(8,128)} %get-tuple-element.271, bf16[2048,4096]{1,0:T(8,128)(2,1)} %bitcast.288, bf16[896,4096]{1,0:T(8,128)(2,1)} %copy-done.29), kind=kOutput, calls=%fused_computation.14 | convolution fusion | flops 15058075648 | bytes 46137344 | tf_op jit(solution)/shard_map/dot_general | solution.py:55
  1037.3 7.9 fusion.80
  1051.3 8.3 add_convert_fusion
  1059.6 10.9 reshape.477
  1076.6 63.3 %shard_map.501 = bf16[3,128,384]{2,1,0:T(8,128)(2,1)} custom-call(bf16[3,16,128,384]{3,2,1,0:T(8,128)(2,1)} %bitcast.282), custom_call_target="tpu_custom_call" | custom-call | tf_op jit(solution)/shard_map/pallas_call | solution.py:813
  1174.3 7.3 all-to-all-start.4
  1181.7 29.7 %fusion.4 = bf16[1152,4928]{0,1:T(8,128)(2,1)} fusion(bf16[1152,2152]{0,1:T(8,128)(2,1)} %convolution_convert_fusion, bf16[1152,2152]{0,1:T(8,128)(2,1)} %convolution_convert_fusion.1, bf16[1152,576]{0,1:T(8,128)(2,1)S(1)} %convolution_convert_fusion.3), kind=kLoop, calls=%fused_computation.7 | loop fusion | flops 68124672 | bytes 22597632 | tf_op jit(solution)/shard_map/concatenate | solution.py:1310
  1214.5 10.9 shard_map.502
  1239.8 12.5 add_convert_fusion.1
  1254.4 42.1 %all-to-all-done.3 = bf16[16,72,448]{2,1,0:T(8,128)(2,1)S(1)} async-done(((bf16[16,72,448]{2,1,0:T(8,128)(2,1)}), bf16[16,72,448]{2,1,0:T(8,128)(2,1)S(1)}, u32[]{:S(2)}, u32[]{:S(2)}) %all-to-all-start.3) | async-done | bytes 1032224 | tf_op jit(solution)/shard_map/all_to_all | solution.py:1281
  1303.0 21.7 %shard_map.503 = (f32[2048,72]{1,0:T(8,128)}, f32[2304,72]{1,0:T(8,128)}, f32[2304,72]{1,0:T(8,128)}) custom-call(bf16[2048,72]{1,0:T(8,128)(2,1)} %constant_dynamic-slice_fusion.1.q_ref, bf16[2304,72]{1,0:T(8,128)(2,1)} %get-tuple-element.236.k_ref, bf16[2304,72]{1,0:T(8,128)(2,1)} %get-tuple-element.235.v_ref, bf16[2048,72]{1,0:T(8,128)(2,1)} %bitcast.346, ...), custom_call_target="tpu_custom_call" | custom-call | flops 3397386240 | bytes 5636096 | tf_op jit(solution)/shard_map/pallas_call | solution.py:1327
  1335.1 117.6 %collective-permute-done.11 = bf16[256,216]{1,0:T(8,128)(2,1)S(1)} collective-permute-done((bf16[256,216]{1,0:T(8,128)(2,1)S(1)}, bf16[256,216]{1,0:T(8,128)(2,1)S(1)}, u32[]{:S(2)}, u32[]{:S(2)}) %collective-permute-start.11) | collective-permute-done | bytes 110624 | tf_op jit(solution)/shard_map/ppermute | solution.py:1346
  1455.6 20.0 %shard_map.504 = bf16[8,256,216]{2,1,0:T(8,128)(2,1)} custom-call(bf16[8,256,216]{2,1,0:T(8,128)(2,1)} %add_convert_fusion.3.x_ref), custom_call_target="tpu_custom_call" | custom-call | tf_op jit(solution)/shard_map/pallas_call | solution.py:865
  1488.7 28.3 %shard_map.509 = bf16[16,72,216]{2,1,0:T(8,128)(2,1)} custom-call(bf16[16,72,216]{2,1,0:T(8,128)(2,1)} %bitcast.318), custom_call_target="tpu_custom_call" | custom-call | tf_op jit(solution)/shard_map/pallas_call | solution.py:865
  1542.4 9.0 shard_map.508
  1575.9 104.4 %all-reduce.9.cloned.1.call-done = bf16[1152,4928]{0,1:T(8,128)(2,1)} async-done(((bf16[1152,4928]{0,1:T(8,128)(2,1)}), bf16[1152,4928]{0,1:T(8,128)(2,1)}) %all-reduce.9.cloned.1.call-update) | async-done | bytes 11354128
  (499 shorter events, 358.5 us)
Async XLA Ops:
  7.2 397.7 %all-gather.3.cloned.1.call-start = ((), (), s32[]{:S(2)}) async-start(), calls=%async_computation.7 | async-start | bytes 16293888 | tf_op jit(solution)/shard_map/all_gather | solution.py:1068
  15.1 55.2 %all-to-all-start = ((bf16[16,72,448]{2,1,0:T(8,128)(2,1)}), bf16[16,72,448]{2,1,0:T(8,128)(2,1)S(1)}, u32[]{:S(2)}, u32[]{:S(2)}) async-start(bf16[16,72,448]{2,1,0:T(8,128)(2,1)} %bitcast.278), calls=%async_computation | async-start | bytes 2359296 | tf_op jit(solution)/shard_map/all_to_all | solution.py:1112
  70.3 431.0 %copy-start.17 = (bf16[16,72,448]{2,1,0:T(8,128)(2,1)}, bf16[16,72,448]{2,1,0:T(8,128)(2,1)S(1)}, u32[]{:S(2)}) copy-start(bf16[16,72,448]{2,1,0:T(8,128)(2,1)S(1)} %all-to-all-done) | copy-start | bytes 3096580
  70.4 136.5 %all-to-all-start.1 = ((bf16[16,72,448]{2,1,0:T(8,128)(2,1)}), bf16[16,72,448]{2,1,0:T(8,128)(2,1)S(1)}, u32[]{:S(2)}, u32[]{:S(2)}) async-start(bf16[16,72,448]{2,1,0:T(8,128)(2,1)} %bitcast.309), calls=%async_computation.1 | async-start | bytes 2359296 | tf_op jit(solution)/shard_map/all_to_all | solution.py:1112
  76.2 130.7 %copy-start.70 = (f32[256]{0:T(256)}, f32[256]{0:T(256)S(1)}, u32[]{:S(2)}) copy-start(f32[256]{0:T(256)S(1)} %broadcast_multiply_fusion.1) | copy-start | bytes 3076
  208.0 204.8 %all-to-all-start.2 = ((bf16[16,448,256]{2,1,0:T(8,128)(2,1)}), bf16[16,448,256]{2,1,0:T(8,128)(2,1)}, u32[]{:S(2)}, u32[]{:S(2)}) async-start(bf16[16,448,256]{2,1,0:T(8,128)(2,1)} %bitcast.312), calls=%async_computation.2 | async-start | bytes 7340032 | tf_op jit(solution)/shard_map/all_to_all | solution.py:1116
  238.1 488.1 %all-gather.5.cloned.1.call-start = ((), (), s32[]{:S(2)}) async-start(), calls=%async_computation.8 | async-start | bytes 3342336 | tf_op jit(solution)/shard_map/all_gather | solution.py:1076
  241.8 123.7 %collective-permute-start = (bf16[9,128,1152]{2,1,0:T(8,128)(2,1)}, bf16[9,128,1152]{2,1,0:T(8,128)(2,1)}, u32[]{:S(2)}, u32[]{:S(2)}) collective-permute-start(bf16[9,128,1152]{2,1,0:T(8,128)(2,1)} %constant_dynamic-slice_fusion.2), channel_id=1, source_target_pairs={{0,1},{1,0},{2,3},{3,2},{4,5},{5,4},{6,7},{7,6},{8,9},{9,8},{10,11... | collective-permute-start | bytes 7962632 | tf_op jit(solution)/shard_map/ppermute | solution.py:889
  242.5 1324.9 %reduce-scatter.3.cloned.1.call-start = ((), (), s32[]{:S(2)}) async-start(), calls=%async_computation.9 | async-start | bytes 3342336 | tf_op jit(solution)/shard_map/reduce_scatter | solution.py:1250
  408.1 26.3 %collective-permute-start.1 = (f32[256,1152]{1,0:T(8,128)}, f32[256,1152]{1,0:T(8,128)}, u32[]{:S(2)}, u32[]{:S(2)}) collective-permute-start(f32[256,1152]{1,0:T(8,128)} %fusion.71), channel_id=1, source_target_pairs={{0,1},{1,0},{2,3},{3,2},{4,5},{5,4},{6,7},{7,6},{8,9},{9,8},{10,11... | collective-permute-start | bytes 3538952 | tf_op jit(solution)/shard_map/ppermute | solution.py:889
  409.9 19.3 %collective-permute-start.3 = (bf16[1152,448]{0,1:T(8,128)(2,1)}, bf16[1152,448]{0,1:T(8,128)(2,1)}, u32[]{:S(2)}, u32[]{:S(2)}) collective-permute-start(bf16[1152,448]{0,1:T(8,128)(2,1)} %copy.333), channel_id=1, source_target_pairs={{0,1},{1,0},{2,3},{3,2},{4,5},{5,4},{6,7},{7,6},{8,9},{9,8},{10,11... | collective-permute-start | bytes 3096584 | tf_op jit(solution)/shard_map/ppermute | solution.py:889
  412.7 18.8 %collective-permute-start.4 = (bf16[1152,448]{0,1:T(8,128)(2,1)}, bf16[1152,448]{0,1:T(8,128)(2,1)}, u32[]{:S(2)}, u32[]{:S(2)}) collective-permute-start(bf16[1152,448]{0,1:T(8,128)(2,1)} %copy.336), channel_id=1, source_target_pairs={{0,1},{1,0},{2,3},{3,2},{4,5},{5,4},{6,7},{7,6},{8,9},{9,8},{10,11... | collective-permute-start | bytes 3096584 | tf_op jit(solution)/shard_map/ppermute | solution.py:889
  417.1 32.5 %collective-permute-start.5 = (bf16[448,4096]{1,0:T(8,128)(2,1)}, bf16[448,4096]{1,0:T(8,128)(2,1)}, u32[]{:S(2)}, u32[]{:S(2)}) collective-permute-start(bf16[448,4096]{1,0:T(8,128)(2,1)} %bitcast.117), channel_id=1, source_target_pairs={{0,1},{1,0},{2,3},{3,2},{4,5},{5,4},{6,7},{7,6},{8,9},{9,8},{10,11... | collective-permute-start | bytes 11010056 | tf_op jit(solution)/shard_map/ppermute | solution.py:889
  421.7 309.5 %copy-start.26 = (bf16[64,2,4,96]{3,2,1,0:T(4,128)(2,1)}, bf16[64,2,4,96]{3,2,1,0:T(4,128)(2,1)S(1)}, u32[]{:S(2)}) copy-start(bf16[64,2,4,96]{3,2,1,0:T(4,128)(2,1)S(1)} %reshape.436) | copy-start | bytes 294916
  447.0 5.1 collective-permute-start.2
  559.6 166.6 %copy-start.13 = (bf16[64,4096]{1,0:T(8,128)(2,1)S(1)}, bf16[64,4096]{1,0:T(8,128)(2,1)}, u32[]{:S(2)}) copy-start(bf16[64,4096]{1,0:T(8,128)(2,1)} %copy-done.12) | copy-start | bytes 1572868
  726.1 6.9 collective-permute-start.6
  832.4 2.5 collective-permute-start.13
  832.5 4.3 collective-permute-start.7
  834.7 4.0 collective-permute-start.8
  1141.4 7.5 collective-permute-start.9
  1148.1 91.6 %collective-permute-start.16 = (bf16[448,4096]{1,0:T(8,128)(2,1)}, bf16[448,4096]{1,0:T(8,128)(2,1)}, u32[]{:S(2)}, u32[]{:S(2)}) collective-permute-start(bf16[448,4096]{1,0:T(8,128)(2,1)} %convolution_convert_fusion.2), channel_id=1, source_target_pairs={{0,1},{1,0},{2,3},{3,2},{4,5},{5,4},{6,7},{7,6},{8,9},{9,8},{10,11... | collective-permute-start | bytes 11010056 | tf_op jit(solution)/shard_map/ppermute | solution.py:889
  1148.4 19.2 %collective-permute-start.15 = (bf16[1152,448]{0,1:T(8,128)(2,1)S(1)}, bf16[1152,448]{0,1:T(8,128)(2,1)S(1)}, u32[]{:S(2)}, u32[]{:S(2)}) collective-permute-start(bf16[1152,448]{0,1:T(8,128)(2,1)S(1)} %copy-done.87), channel_id=1, source_target_pairs={{0,1},{1,0},{2,3},{3,2},{4,5},{5,4},{6,7},{7,6},{8,9},{9,8},{10,11... | collective-permute-start | bytes 3096584 | tf_op jit(solution)/shard_map/ppermute | solution.py:889
  1148.6 76.8 %collective-permute-start.14 = (bf16[1152,448]{0,1:T(8,128)(2,1)}, bf16[1152,448]{0,1:T(8,128)(2,1)}, u32[]{:S(2)}, u32[]{:S(2)}) collective-permute-start(bf16[1152,448]{0,1:T(8,128)(2,1)} %convolution_convert_fusion.13), channel_id=1, source_target_pairs={{0,1},{1,0},{2,3},{3,2},{4,5},{5,4},{6,7},{7,6},{8,9},{9,8},{10,11... | collective-permute-start | bytes 3096584 | tf_op jit(solution)/shard_map/ppermute | solution.py:889
  1155.8 8.8 collective-permute-start.10
  1174.3 58.5 %all-to-all-start.4 = ((bf16[16,72,448]{2,1,0:T(8,128)(2,1)}), bf16[16,72,448]{2,1,0:T(8,128)(2,1)}, u32[]{:S(2)}, u32[]{:S(2)}) async-start(bf16[16,72,448]{2,1,0:T(8,128)(2,1)} %bitcast.310), calls=%async_computation.4 | async-start | bytes 2359296 | tf_op jit(solution)/shard_map/all_to_all | solution.py:1281
  1181.6 498.7 %all-reduce.9.cloned.1.call-start = ((), (), s32[]{:S(2)}) async-start(), calls=%async_computation.10 | async-start | bytes 22708224
  1232.8 63.8 %all-to-all-start.3 = ((bf16[16,72,448]{2,1,0:T(8,128)(2,1)}), bf16[16,72,448]{2,1,0:T(8,128)(2,1)S(1)}, u32[]{:S(2)}, u32[]{:S(2)}) async-start(bf16[16,72,448]{2,1,0:T(8,128)(2,1)} %bitcast.311), calls=%async_computation.3 | async-start | bytes 2359296 | tf_op jit(solution)/shard_map/all_to_all | solution.py:1281
  1297.6 272.5 %all-to-all-start.5 = ((bf16[16,448,256]{2,1,0:T(8,128)(2,1)}), bf16[16,448,256]{2,1,0:T(8,128)(2,1)}, u32[]{:S(2)}, u32[]{:S(2)}) async-start(bf16[16,448,256]{2,1,0:T(8,128)(2,1)} %bitcast.290), calls=%async_computation.5 | async-start | bytes 7340032 | tf_op jit(solution)/shard_map/all_to_all | solution.py:1289
  1327.8 124.9 %collective-permute-start.11 = (bf16[256,216]{1,0:T(8,128)(2,1)S(1)}, bf16[256,216]{1,0:T(8,128)(2,1)S(1)}, u32[]{:S(2)}, u32[]{:S(2)}) collective-permute-start(bf16[256,216]{1,0:T(8,128)(2,1)S(1)} %fusion.128), channel_id=1, source_target_pairs={{0,16},{2,18},{4,20},{6,22},{8,24},{10,26},{12,28},{14,30},{16,0},... | collective-permute-start | bytes 331784 | tf_op jit(solution)/shard_map/ppermute | solution.py:1346
  1486.2 42.7 %collective-permute-start.12 = (bf16[256,1152]{1,0:T(8,128)(2,1)}, bf16[256,1152]{1,0:T(8,128)(2,1)S(1)}, u32[]{:S(2)}, u32[]{:S(2)}) collective-permute-start(bf16[256,1152]{1,0:T(8,128)(2,1)} %get-tuple-element.282), channel_id=1, source_target_pairs={{0,1},{1,0},{2,3},{3,2},{4,5},{5,4},{6,7},{7,6},{8,9},{9,8},{10,11... | collective-permute-start | bytes 1769480 | tf_op jit(solution)/shard_map/ppermute | solution.py:889
  1552.3 4.9 collective-permute-start.17
  (103 other events, 1305.7 us)
Sparse Core Ops, SparseCore 0:
  12.2 283.5 all-gather.2
  299.0 103.8 all-gather.4
  793.6 140.0 reduce-scatter.2
  1225.6 454.7 all-reduce.8

commit v2 on v1

--- a/solution.py
+++ b/solution.py
@@ -513,105 +513,131 @@
     )
 
 
-def gather_kernel(n, x_ref, o_ref, sent, landed, local):
-    layers = n // 4
-    me, z, a, b, step_a, step_b = place()
-    partners = neighbours(layers)
-    (up, to_up), (down, to_down), (_, to_a), (_, to_b) = partners
-    greet(partners)
-    own = pltpu.make_async_copy(x_ref, o_ref.at[me], local)
-    own.start()
-
-    def send(slot, device, way, source=None):
+class Arrivals:
+    def __init__(self, n, x_ref, slots, sent, landed, local):
+        self.n, self.layers = n, n // 4
+        self.x_ref, self.slots, self.sent, self.landed = x_ref, slots, sent, landed
+        self.me, self.z, self.a, self.b, self.step_a, self.step_b = place()
+        self.partners = neighbours(self.layers)
+        (self.up, self.to_up), (self.down, self.to_down) = self.partners[:2]
+        self.to_a, self.to_b = self.partners[2][1], self.partners[3][1]
+        self.own = pltpu.make_async_copy(x_ref, slots.at[self.me], local)
+
+    def at(self, layer, of_a, of_b):
+        return layer * 4 + of_a * self.step_a + of_b * self.step_b
+
+    def send(self, slot, device, way, source=None):
         return pltpu.make_async_remote_copy(
-            src_ref=o_ref.at[slot] if source is None else source,
-            dst_ref=o_ref.at[slot],
-            send_sem=sent.at[way, slot],
-            recv_sem=landed.at[slot],
+            src_ref=self.slots.at[slot] if source is None else source,
+            dst_ref=self.slots.at[slot],
+            send_sem=self.sent.at[way, slot],
+            recv_sem=self.landed.at[slot],
             device_id={"seq": device},
             device_id_type=MESH,
         )
 
-    @pl.when(up)
-    def _():
-        send(me, to_up, 0, x_ref).start()
-
-    @pl.when(down)
-    def _():
-        send(me, to_down, 1, x_ref).start()
-
-    send(me, to_b, 3, x_ref).start()
-    send(me, to_a, 2, x_ref).start()
-    for distance in range(1, layers):
-
-        @pl.when(z >= distance)
+    def layer(self, k):
+        z, last = self.z, self.layers - 1
+        both = 2 * jnp.minimum(z, last - z)
+        step = (k + 1) // 2
+        near = jnp.where(k % 2 == 1, z - step, z + step)
+        far = jnp.where(z < last - z, k, last - k)
+        return jnp.where(k <= both, near, far)
+
+    def block(self, i):
+        last = 2 * self.layers - 1
+        over_b = i // (2 * self.layers)
+        j = i - over_b * 2 * self.layers
+        over_a = jnp.where((j > 0) & ((j % 2 == 0) | (j == last)), 1, 0)
+        nearness = jnp.where(over_a == 1, jnp.maximum(j - 1, 0) // 2, (j + 1) // 2)
+        layer = self.layer(nearness)
+        of_a = jnp.where(over_a == 1, 1 - self.a, self.a)
+        of_b = jnp.where(over_b == 1, 1 - self.b, self.b)
+        return layer, over_a, over_b, self.at(layer, of_a, of_b)
+
+    def start(self, beside=None):
+        if beside is None:
+            greet(self.partners)
+        else:
+            beside.greet()
+        self.own.start()
+        me, x_ref = self.me, self.x_ref
+
+        @pl.when(self.up)
         def _():
-            slot = me - 4 * distance
-            send(slot, to_a, 2).wait_recv()
-
-            @pl.when(up)
+            self.send(me, self.to_up, 0, x_ref).start()
+
+        @pl.when(self.down)
+        def _():
+            self.send(me, self.to_down, 1, x_ref).start()
+
+        self.send(me, self.to_b, 3, x_ref).start()
+        self.send(me, self.to_a, 2, x_ref).start()
+        self.own.wait()
+
+    def take(self, i):
+        layer, over_a, over_b, slot = self.block(i)
+
+        @pl.when(i > 0)
+        def _():
+            self.send(slot, self.to_b, 3).wait_recv()
+
+        @pl.when((i > 0) & (over_b == 0))
+        def _():
+            @pl.when(over_a == 0)
             def _():
-                send(slot, to_up, 0).start()
-
-            send(slot, to_b, 3).start()
-            send(slot, to_a, 2).start()
-
-        @pl.when(z + distance < layers)
-        def _():
-            slot = me + 4 * distance
-            send(slot, to_a, 2).wait_recv()
-
-            @pl.when(down)
+                @pl.when((layer < self.z) & self.up)
+                def _():
+                    self.send(slot, self.to_up, 0).start()
+
+                @pl.when((layer > self.z) & self.down)
+                def _():
+                    self.send(slot, self.to_down, 1).start()
+
+                self.send(slot, self.to_a, 2).start()
+
+            self.send(slot, self.to_b, 3).start()
+
+        return slot
+
+    def drain(self):
+        def body(layer, _):
+            slot = self.at(layer, self.a, self.b)
+            self.send(slot, self.to_a, 2).wait_send()
+            self.send(slot, self.to_b, 3).wait_send()
+            self.send(self.at(layer, 1 - self.a, self.b), self.to_b, 3).wait_send()
+
+            @pl.when((layer <= self.z) & self.up)
             def _():
-                send(slot, to_down, 1).start()
-
-            send(slot, to_b, 3).start()
-            send(slot, to_a, 2).start()
-
-    for distance in range(layers):
-
-        @pl.when(z >= distance)
-        def _():
-            slot = to_a - 4 * distance
-            send(slot, to_b, 3).wait_recv()
-            send(slot, to_b, 3).start()
-
-        if distance:
-
-            @pl.when(z + distance < layers)
+                self.send(slot, self.to_up, 0).wait_send()
+
+            @pl.when((layer >= self.z) & self.down)
             def _():
-                slot = to_a + 4 * distance
-                send(slot, to_b, 3).wait_recv()
-                send(slot, to_b, 3).start()
-
-    def at(layer, of_a, of_b):
-        return layer * 4 + of_a * step_a + of_b * step_b
-
-    def arrive(layer, _):
-        send(at(layer, 0, 1 - b), to_b, 3).wait_recv()
-        send(at(layer, 1, 1 - b), to_b, 3).wait_recv()
+                self.send(slot, self.to_down, 1).wait_send()
+
+            return 0
+
+        lax.fori_loop(0, self.layers, body, 0)
+
+
+def gather_semaphores(n):
+    return [
+        pltpu.SemaphoreType.DMA((4, n)),
+        pltpu.SemaphoreType.DMA((n,)),
+        pltpu.SemaphoreType.DMA(()),
+    ]
+
+
+def gather_kernel(n, x_ref, o_ref, *semaphores):
+    arrivals = Arrivals(n, x_ref, o_ref, *semaphores)
+    arrivals.start()
+
+    def body(i, _):
+        arrivals.take(i)
         return 0
 
-    lax.fori_loop(0, layers, arrive, 0)
-    own.wait()
-
-    def drain(layer, _):
-        slot = at(layer, a, b)
-        send(slot, to_a, 2).wait_send()
-        send(slot, to_b, 3).wait_send()
-        send(at(layer, 1 - a, b), to_b, 3).wait_send()
-
-        @pl.when((layer <= z) & up)
-        def _():
-            send(slot, to_up, 0).wait_send()
-
-        @pl.when((layer >= z) & down)
-        def _():
-            send(slot, to_down, 1).wait_send()
-
-        return 0
-
-    lax.fori_loop(0, layers, drain, 0)
+    lax.fori_loop(0, n, body, 0)
+    arrivals.drain()
 
 
 def gathered_blocks(x, collective_id):
@@ -621,18 +647,352 @@
         out_shape=jax.ShapeDtypeStruct((n,) + x.shape, x.dtype),
         in_specs=[pl.BlockSpec(memory_space=pl.ANY)],
         out_specs=pl.BlockSpec(memory_space=pl.ANY),
-        scratch_shapes=[
-            pltpu.SemaphoreType.DMA((4, n)),
-            pltpu.SemaphoreType.DMA((n,)),
-            pltpu.SemaphoreType.DMA(()),
-        ],
+        scratch_shapes=gather_semaphores(n),
         compiler_params=pltpu.CompilerParams(
             collective_id=collective_id, has_side_effects=True
         ),
     )(x)
 
 
-def scatter_kernel(n, chunks, p_ref, o_ref, from_b, from_a, from_down, from_up, *semaphores):
+def gather_beside_kernel(n, x_ref, y_ref, o_ref, y_out, sent, landed, local, *semaphores):
+    beside = Beside(n, 1, ((y_ref, y_out),), sent, landed, local)
+    arrivals = Arrivals(n, x_ref, o_ref, *semaphores)
+    arrivals.start(beside)
+
+    def body(i, _):
+        arrivals.take(i)
+        beside.start(i)
+        return 0
+
+    lax.fori_loop(0, n, body, 0)
+    beside.finish()
+    arrivals.drain()
+
+
+def gathered_beside(x, y, collective_id):
+    n = lax.axis_size("seq")
+    anywhere = pl.BlockSpec(memory_space=pl.ANY)
+    return pl.pallas_call(
+        functools.partial(gather_beside_kernel, n),
+        out_shape=[
+            jax.ShapeDtypeStruct((n,) + x.shape, x.dtype),
+            jax.ShapeDtypeStruct(y.shape, y.dtype),
+        ],
+        in_specs=[anywhere] * 2,
+        out_specs=[anywhere] * 2,
+        scratch_shapes=[pltpu.SemaphoreType.DMA((1, n))] * 2
+        + [pltpu.SemaphoreType.DMA((1,))]
+        + gather_semaphores(n),
+        compiler_params=pltpu.CompilerParams(
+            collective_id=collective_id, has_side_effects=True
+        ),
+    )(x, y)
+
+
+def pair_rows(pair):
+    return pair.reshape(pair.shape[0] * pair.shape[1], pair.shape[2])
+
+
+def units_kernel(
+    n,
+    x_ref,
+    w_gate_ref,
+    w_up_ref,
+    slots,
+    gate_ref,
+    up_ref,
+    hidden_ref,
+    x_buf,
+    gate_buf,
+    up_buf,
+    hidden_buf,
+    load_sem,
+    store_sem,
+    *semaphores,
+):
+    arrivals = Arrivals(n, x_ref, slots, *semaphores)
+    arrivals.start()
+    kept = ((gate_ref, gate_buf), (up_ref, up_buf), (hidden_ref, hidden_buf))
+
+    def stores(pair):
+        buf = pair % 2
+        return [
+            pltpu.make_async_copy(
+                held.at[buf, i], out.at[arrivals.block(2 * pair + i)[3]], store_sem.at[buf, i, j]
+            )
+            for i in range(2)
+            for j, (out, held) in enumerate(kept)
+        ]
+
+    def body(pair, _):
+        buf = pair % 2
+        loads = [
+            pltpu.make_async_copy(
+                slots.at[arrivals.take(2 * pair + i)], x_buf.at[i], load_sem.at[i]
+            )
+            for i in range(2)
+        ]
+        for load in loads:
+            load.start()
+        for load in loads:
+            load.wait()
+
+        @pl.when(pair >= 2)
+        def _():
+            for store in stores(pair - 2):
+                store.wait()
+
+        x = pair_rows(x_buf[...])
+        shape = gate_buf.shape[1:]
+        gate = product(x, w_gate_ref[...])
+        up = product(x, w_up_ref[...])
+        gate_buf[buf] = gate.reshape(shape)
+        up_buf[buf] = up.reshape(shape)
+        hidden_buf[buf] = (gate * jax.nn.sigmoid(gate) * up).astype(jnp.bfloat16).reshape(shape)
+        for store in stores(pair):
+            store.start()
+        return 0
+
+    lax.fori_loop(0, n // 2, body, 0)
+    for pair in (n // 2 - 2, n // 2 - 1):
+        for store in stores(pair):
+            store.wait()
+    arrivals.drain()
+
+
+def gathered_units(x, w_gate, w_up, collective_id):
+    n = lax.axis_size("seq")
+    rows, units = x.shape[0], w_gate.shape[1]
+    exact = jax.ShapeDtypeStruct((n, rows, units), jnp.float32)
+    low = jax.ShapeDtypeStruct((n, rows, units), jnp.bfloat16)
+    anywhere = pl.BlockSpec(memory_space=pl.ANY)
+    return pl.pallas_call(
+        functools.partial(units_kernel, n),
+        out_shape=[jax.ShapeDtypeStruct((n,) + x.shape, x.dtype), exact, exact, low],
+        in_specs=[anywhere] + [pl.BlockSpec(memory_space=pltpu.VMEM)] * 2,
+        out_specs=[anywhere] * 4,
+        scratch_shapes=[
+            pltpu.VMEM((2,) + x.shape, x.dtype),
+            pltpu.VMEM((2, 2, rows, units), jnp.float32),
+            pltpu.VMEM((2, 2, rows, units), jnp.float32),
+            pltpu.VMEM((2, 2, rows, units), jnp.bfloat16),
+            pltpu.SemaphoreType.DMA((2,)),
+            pltpu.SemaphoreType.DMA((2, 2, 3)),
+        ]
+        + gather_semaphores(n),
+        compiler_params=pltpu.CompilerParams(
+            collective_id=collective_id, has_side_effects=True, vmem_limit_bytes=60 * 2**20
+        ),
+    )(x, w_gate, w_up)
+
+
+def units_back_kernel(
+    n,
+    x_ref,
+    w_gate_ref,
+    w_up_ref,
+    w_down_ref,
+    features_ref,
+    gate_ref,
+    up_ref,
+    slots,
+    terms_ref,
+    dunits_ref,
+    ddown_ref,
+    x_buf,
+    features_buf,
+    gate_buf,
+    up_buf,
+    terms_buf,
+    hidden_grad,
+    gate_sum,
+    up_sum,
+    down_sum,
+    down_buf,
+    units_buf,
+    load_sem,
+    store_sem,
+    down_sem,
+    units_sem,
+    *semaphores,
+):
+    arrivals = Arrivals(n, x_ref, slots, *semaphores)
+    arrivals.start()
+    gate_sum[...] = jnp.zeros_like(gate_sum)
+    up_sum[...] = jnp.zeros_like(up_sum)
+    down_sum[...] = jnp.zeros_like(down_sum)
+    out_width = w_down_ref.shape[1]
+    tile = 1024
+    chunks, chunk = terms_ref.shape[0], terms_ref.shape[3]
+
+    def stores(pair):
+        return [
+            pltpu.make_async_copy(
+                terms_buf.at[i, :, pl.ds(c * chunk, chunk)],
+                terms_ref.at[c, arrivals.block(2 * pair + i)[3]],
+                store_sem.at[i, c],
+            )
+            for i in range(2)
+            for c in range(chunks)
+        ]
+
+    def loads(pair):
+        return [
+            pltpu.make_async_copy(
+                source.at[arrivals.block(2 * pair + i)[3]],
+                held.at[pair % 2, i] if j < 2 else held.at[i],
+                load_sem.at[pair % 2, i, j],
+            )
+            for i in range(2)
+            for j, (source, held) in enumerate(
+                ((slots, x_buf), (features_ref, features_buf), (gate_ref, gate_buf), (up_ref, up_buf))
+            )
+        ]
+
+    def take_pair(pair):
+        arrivals.take(2 * pair)
+        arrivals.take(2 * pair + 1)
+        for load in loads(pair):
+            load.start()
+
+    take_pair(0)
+
+    def body(pair, _):
+        buf = pair % 2
+        for load in loads(pair):
+            load.wait()
+        hidden_grad[...] = jnp.zeros_like(hidden_grad)
+
+        def back_tile(t, _):
+            columns = pl.ds(pl.multiple_of(t * tile, tile), tile)
+            hidden_grad[...] += product_nt(
+                pair_rows(x_buf[buf, :, :, columns]), w_down_ref[:, columns]
+            )
+            return 0
+
+        lax.fori_loop(0, out_width // tile, back_tile, 0)
+        gate, up, grad = pair_rows(gate_buf[...]), pair_rows(up_buf[...]), hidden_grad[...]
+        share = jax.nn.sigmoid(gate)
+        silu = gate * share
+        gate_low = (grad * up * (share * (1.0 + gate * (1.0 - share)))).astype(jnp.bfloat16)
+        up_low = (grad * silu).astype(jnp.bfloat16)
+        hidden_t = (silu * up).astype(jnp.bfloat16).T
+        terms = product_nt(gate_low, w_gate_ref[...]) + product_nt(up_low, w_up_ref[...])
+
+        @pl.when(pair >= 1)
+        def _():
+            for store in stores(pair - 1):
+                store.wait()
+
+        terms_buf[...] = terms.astype(jnp.bfloat16).reshape(terms_buf.shape)
+        for store in stores(pair):
+            store.start()
+
+        @pl.when(pair + 1 < n // 2)
+        def _():
+            take_pair(pair + 1)
+
+        features_t = pair_rows(features_buf[buf]).T
+        for begin in range(0, gate_low.shape[1], 256):
+            columns = slice(begin, begin + 256)
+            gate_sum[:, columns] += product(features_t, gate_low[:, columns])
+            up_sum[:, columns] += product(features_t, up_low[:, columns])
+
+        def down_tile(t, _):
+            columns = pl.ds(pl.multiple_of(t * tile, tile), tile)
+            down_sum[:, columns] += product(hidden_t, pair_rows(x_buf[buf, :, :, columns]))
+            return 0
+
+        lax.fori_loop(0, out_width // tile, down_tile, 0)
+        return 0
+
+    lax.fori_loop(0, n // 2, body, 0)
+    share = out_width // n
+
+    def down_store(j):
+        return pltpu.make_async_copy(
+            down_buf.at[j % 2], ddown_ref.at[j], down_sem.at[j % 2]
+        )
+
+    def down_out(j, _):
+        @pl.when(j >= 2)
+        def _():
+            down_store(j - 2).wait()
+
+        columns = pl.ds(pl.multiple_of(j * share, share), share)
+        down_buf[j % 2] = down_sum[:, columns].astype(jnp.bfloat16)
+        down_store(j).start()
+        return 0
+
+    lax.fori_loop(0, n, down_out, 0)
+
+    def units_store(j):
+        return pltpu.make_async_copy(units_buf.at[j % 2], dunits_ref.at[j], units_sem.at[j % 2])
+
+    def units_out(j, _):
+        @pl.when(j >= 2)
+        def _():
+            units_store(j - 2).wait()
+
+        owned = units_buf.shape[2]
+        owner = pl.ds(pl.multiple_of(j * owned, 8), owned)
+        for i, total in enumerate((gate_sum, up_sum)):
+            units_buf[j % 2, i] = total[owner].astype(jnp.bfloat16)
+        units_store(j).start()
+        return 0
+
+    lax.fori_loop(0, n, units_out, 0)
+    units_store(n - 2).wait()
+    units_store(n - 1).wait()
+    down_store(n - 2).wait()
+    down_store(n - 1).wait()
+    for store in stores(n // 2 - 1):
+        store.wait()
+    arrivals.drain()
+
+
+def gathered_back(x, w_gate, w_up, w_down, features, gate, up, chunks, collective_id):
+    n = lax.axis_size("seq")
+    rows, out_width = x.shape
+    width, units = w_gate.shape
+    low, exact = jnp.bfloat16, jnp.float32
+    anywhere = pl.BlockSpec(memory_space=pl.ANY)
+    in_vmem = pl.BlockSpec(memory_space=pltpu.VMEM)
+    return pl.pallas_call(
+        functools.partial(units_back_kernel, n),
+        out_shape=[
+            jax.ShapeDtypeStruct((n,) + x.shape, low),
+            jax.ShapeDtypeStruct((chunks, n, rows, width // chunks), low),
+            jax.ShapeDtypeStruct((n, 2, width // n, units), low),
+            jax.ShapeDtypeStruct((n, units, out_width // n), low),
+        ],
+        in_specs=[anywhere] + [in_vmem] * 3 + [anywhere] * 3,
+        out_specs=[anywhere] * 4,
+        scratch_shapes=[
+            pltpu.VMEM((2, 2, rows, out_width), low),
+            pltpu.VMEM((2, 2, rows, width), low),
+            pltpu.VMEM((2, rows, units), exact),
+            pltpu.VMEM((2, rows, units), exact),
+            pltpu.VMEM((2, rows, width), low),
+            pltpu.VMEM((2 * rows, units), exact),
+            pltpu.VMEM((width, units), exact),
+            pltpu.VMEM((width, units), exact),
+            pltpu.VMEM((units, out_width), exact),
+            pltpu.VMEM((2, units, out_width // n), low),
+            pltpu.VMEM((2, 2, width // n, units), low),
+            pltpu.SemaphoreType.DMA((2, 2, 4)),
+            pltpu.SemaphoreType.DMA((2, chunks)),
+            pltpu.SemaphoreType.DMA((2,)),
+            pltpu.SemaphoreType.DMA((2,)),
+        ]
+        + gather_semaphores(n),
+        compiler_params=pltpu.CompilerParams(
+            collective_id=collective_id, has_side_effects=True, vmem_limit_bytes=60 * 2**20
+        ),
+    )(x, w_gate, w_up, w_down, features, gate, up)
+
+
+def scatter_kernel(n, chunks, p_ref, o_ref, from_b, from_a, from_down, from_up, *semaphores, fill=None):
     layers = n // 4
     me, z, a, b, step_a, step_b = place()
     partners = neighbours(layers)
@@ -762,10 +1122,15 @@
         def _():
             stage(jnp.clip(step, 0, chunks - 1))
 
-    send_b(0)
+    def fill_and_send(c):
+        if fill is not None:
+            fill(c)
+        send_b(c)
+
+    fill_and_send(0)
 
     def step(t, _):
-        when_chunk(t + 1, send_b)
+        when_chunk(t + 1, fill_and_send)
         when_chunk(t, send_a)
         when_chunk(t - 1, join_line)
         inner = (z > 0) & (z < layers - 1)
@@ -800,89 +1165,276 @@
     lax.fori_loop(0, chunks, drain, 0)
 
 
+def scatter_scratch(chunks, n, block, dtype):
+    layers = n // 4
+
+    def slots(*count):
+        return pltpu.VMEM((chunks,) + count + block, dtype)
+
+    def semaphores(*count):
+        return pltpu.SemaphoreType.DMA((chunks,) + count)
+
+    return (
+        [slots(2, layers)]
+        + [slots(layers)] * 3
+        + [semaphores(2, layers)] * 2
+        + [semaphores(layers)] * 6
+    )
+
+
 def scattered_sum(terms, collective_id):
     chunks, n = terms.shape[:2]
-    layers, block = n // 4, terms.shape[2:]
-
-    def slots(*count):
-        return pltpu.VMEM((chunks,) + count + block, terms.dtype)
-
-    def semaphores(*count):
-        return pltpu.SemaphoreType.DMA((chunks,) + count)
-
+    block = terms.shape[2:]
     return pl.pallas_call(
         functools.partial(scatter_kernel, n, chunks),
         out_shape=jax.ShapeDtypeStruct((chunks,) + block, terms.dtype),
         in_specs=[pl.BlockSpec(memory_space=pltpu.VMEM)],
         out_specs=pl.BlockSpec(memory_space=pltpu.VMEM),
-        scratch_shapes=[slots(2, layers)]
-        + [slots(layers)] * 3
-        + [semaphores(2, layers)] * 2
-        + [semaphores(layers)] * 6,
+        scratch_shapes=scatter_scratch(chunks, n, block, terms.dtype),
         compiler_params=pltpu.CompilerParams(
             collective_id=collective_id, has_side_effects=True, vmem_limit_bytes=60 * 2**20
         ),
     )(terms)
 
 
-def exchange_kernel(group, spread, x_ref, o_ref, sent, landed, local):
+def down_kernel(n, chunks, hidden_ref, w_down_ref, o_ref, p_ref, *scratch):
+    cols = w_down_ref.shape[1] // chunks
+
+    def fill(c):
+        columns = pl.ds(pl.multiple_of(c * cols, cols), cols)
+
+        def body(pair, _):
+            owners = pl.ds(2 * pair, 2)
+            terms = product(pair_rows(hidden_ref[owners]), w_down_ref[:, columns])
+            p_ref[c, owners] = terms.astype(p_ref.dtype).reshape(2, -1, cols)
+            return 0
+
+        lax.fori_loop(0, n // 2, body, 0)
+
+    scatter_kernel(n, chunks, p_ref, o_ref, *scratch, fill=fill)
+
+
+def scattered_down(hidden, w_down, chunks, collective_id):
+    n, rows = hidden.shape[:2]
+    block = (rows, w_down.shape[1] // chunks)
+    return pl.pallas_call(
+        functools.partial(down_kernel, n, chunks),
+        out_shape=jax.ShapeDtypeStruct((chunks,) + block, hidden.dtype),
+        in_specs=[pl.BlockSpec(memory_space=pltpu.VMEM)] * 2,
+        out_specs=pl.BlockSpec(memory_space=pltpu.VMEM),
+        scratch_shapes=[pltpu.VMEM((chunks, n) + block, hidden.dtype)]
+        + scatter_scratch(chunks, n, block, hidden.dtype),
+        compiler_params=pltpu.CompilerParams(
+            collective_id=collective_id, has_side_effects=True, vmem_limit_bytes=60 * 2**20
+        ),
+    )(hidden, w_down)
+
+
+class Beside:
+    def __init__(self, n, per_step, pairs, sent, landed, local):
+        self.n, self.per_step, self.pairs = n, per_step, pairs
+        self.sent, self.landed = sent, landed
+        self.me = lax.axis_index("seq")
+        self.own = [
+            pltpu.make_async_copy(source.at[self.me], target.at[self.me], local.at[j])
+            for j, (source, target) in enumerate(pairs)
+        ]
+
+    def greet(self):
+        barrier = pltpu.get_barrier_semaphore()
+        for step in range(1, self.n):
+            pl.semaphore_signal(
+                barrier,
+                inc=1,
+                device_id={"seq": lax.rem(self.me + step, self.n)},
+                device_id_type=MESH,
+            )
+        pl.semaphore_wait(barrier, self.n - 1)
+        for own in self.own:
+            own.start()
+
+    def copies(self, step):
+        other = lax.rem(self.me + step, self.n)
+        return [
+            pltpu.make_async_remote_copy(
+                src_ref=source.at[other],
+                dst_ref=target.at[self.me],
+                send_sem=self.sent.at[j, step],
+                recv_sem=self.landed.at[j, step],
+                device_id={"seq": other},
+                device_id_type=MESH,
+            )
+            for j, (source, target) in enumerate(self.pairs)
+        ]
+
+    def start(self, t):
+        for i in range(self.per_step):
+            step = t * self.per_step + i + 1
+
+            @pl.when(step < self.n)
+            def _():
+                for copy in self.copies(jnp.minimum(step, self.n - 1)):
+                    copy.start()
+
+    def finish(self):
+        def body(step, _):
+            for copy in self.copies(step):
+                copy.wait()
+            return 0
+
+        lax.fori_loop(1, self.n, body, 0)
+        for own in self.own:
+            own.wait()
+
+
+def vision_kernel(n, chunks, spans, left_ref, right_ref, o_ref, p_ref, *scratch):
+    cols = right_ref.shape[1] // chunks
+    shard = left_ref.shape[1] // n
+
+    def fill(c):
+        def body(t, _):
+            tile = c * (cols // 128) + t
+            source = sum(jnp.where(tile >= span, 1, 0) for span in spans[1:])
+            columns = pl.ds(pl.multiple_of(tile * 128, 128), 128)
+            terms = product(left_ref[source], right_ref[:, columns])
+            p_ref[c, :, :, pl.ds(pl.multiple_of(t * 128, 128), 128)] = terms.reshape(
+                n, shard, 128
+            ).astype(p_ref.dtype)
+            return 0
+
+        lax.fori_loop(0, cols // 128, body, 0)
+
+    scatter_kernel(n, chunks, p_ref, o_ref, *scratch, fill=fill)
+
+
+def scattered_vision(left, right, spans, chunks, collective_id):
+    n = lax.axis_size("seq")
+    block = (left.shape[1] // n, right.shape[1] // chunks)
+    return pl.pallas_call(
+        functools.partial(vision_kernel, n, chunks, spans),
+        out_shape=jax.ShapeDtypeStruct((chunks,) + block, left.dtype),
+        in_specs=[pl.BlockSpec(memory_space=pltpu.VMEM)] * 2,
+        out_specs=pl.BlockSpec(memory_space=pltpu.VMEM),
+        scratch_shapes=[pltpu.VMEM((chunks, n) + block, left.dtype)]
+        + scatter_scratch(chunks, n, block, left.dtype),
+        compiler_params=pltpu.CompilerParams(
+            collective_id=collective_id, has_side_effects=True, vmem_limit_bytes=60 * 2**20
+        ),
+    )(left, right)
+
+
+def exchange_kernel(n, groups, *refs):
+    count = len(groups)
+    sources, targets = refs[:count], refs[count : 2 * count]
+    sent, landed, local = refs[2 * count :]
     me = lax.axis_index("seq")
-    base = lax.div(me, group) * group
-    mine = me - base
     barrier = pltpu.get_barrier_semaphore()
-    for step in range(1, group):
+    for step in range(1, n):
         pl.semaphore_signal(
-            barrier,
-            inc=1,
-            device_id={"seq": base + lax.rem(mine + step, group)},
+            barrier, inc=1, device_id={"seq": lax.rem(me + step, n)}, device_id_type=MESH
+        )
+    pl.semaphore_wait(barrier, n - 1)
+    copies = []
+    for j, group in enumerate(groups):
+        base = lax.div(me, group) * group
+        mine = me - base
+        copies.append(
+            pltpu.make_async_copy(sources[j].at[mine], targets[j].at[mine], local.at[j])
+        )
+        copies[-1].start()
+        for step in range(1, group):
+            other = lax.rem(mine + step, group)
+            copies.append(
+                pltpu.make_async_remote_copy(
+                    src_ref=sources[j].at[other],
+                    dst_ref=targets[j].at[mine],
+                    send_sem=sent.at[j, step],
+                    recv_sem=landed.at[j, step],
+                    device_id={"seq": base + other},
+                    device_id_type=MESH,
+                )
+            )
+            copies[-1].start()
+    for copy in copies:
+        copy.wait()
+
+
+def exchanged(arrays, collective_id):
+    n = lax.axis_size("seq")
+    count = len(arrays)
+    groups = tuple(x.shape[0] for x in arrays)
+    return pl.pallas_call(
+        functools.partial(exchange_kernel, n, groups),
+        out_shape=[jax.ShapeDtypeStruct(x.shape, x.dtype) for x in arrays],
+        in_specs=[pl.BlockSpec(memory_space=pl.ANY)] * count,
+        out_specs=[pl.BlockSpec(memory_space=pl.ANY)] * count,
+        scratch_shapes=[pltpu.SemaphoreType.DMA((count, n))] * 2
+        + [pltpu.SemaphoreType.DMA((count,))],
+        compiler_params=pltpu.CompilerParams(
+            collective_id=collective_id, has_side_effects=True
+        ),
+    )(*arrays)
+
+
+def reduce_kernel(n, combine, x_ref, o_ref, shares, total, sent, landed, sent_on, landed_on):
+    me = lax.axis_index("seq")
+    barrier = pltpu.get_barrier_semaphore()
+    others = [lax.rem(me + step, n) for step in range(1, n)]
+    for other in others:
+        pl.semaphore_signal(barrier, inc=1, device_id={"seq": other}, device_id_type=MESH)
+    pl.semaphore_wait(barrier, n - 1)
+
+    def copy(step, source, target, sent, landed):
+        return pltpu.make_async_remote_copy(
+            src_ref=source,
+            dst_ref=target,
+            send_sem=sent.at[step],
+            recv_sem=landed.at[step],
+            device_id={"seq": others[step - 1]},
             device_id_type=MESH,
         )
-    pl.semaphore_wait(barrier, group - 1)
-    own = pltpu.make_async_copy(x_ref if spread else x_ref.at[mine], o_ref.at[mine], local)
-    own.start()
-    copies = []
-    for step in range(1, group):
-        other = lax.rem(mine + step, group)
-        copies.append(
-            pltpu.make_async_remote_copy(
-                src_ref=x_ref if spread else x_ref.at[other],
-                dst_ref=o_ref.at[mine],
-                send_sem=sent.at[step],
-                recv_sem=landed.at[step],
-                device_id={"seq": base + other},
-                device_id_type=MESH,
-            )
-        )
-        copies[-1].start()
-    own.wait()
-    for copy in copies:
-        copy.wait()
-
-
-def exchanged(x, collective_id, group=None, spread=False):
-    group = lax.axis_size("seq") if group is None else group
-    shape = (group,) + x.shape if spread else x.shape
+
+    there = [copy(i, x_ref.at[others[i - 1]], shares.at[me], sent, landed) for i in range(1, n)]
+    for move in there:
+        move.start()
+    shares[me] = x_ref[me]
+    for move in there:
+        move.wait()
+    total[...] = combine(shares[...])
+    back = [copy(i, total, o_ref.at[me], sent_on, landed_on) for i in range(1, n)]
+    for move in back:
+        move.start()
+    o_ref[me] = total[...]
+    for move in back:
+        move.wait()
+
+
+def reduced(x, combine, collective_id):
+    n = x.shape[0]
     return pl.pallas_call(
-        functools.partial(exchange_kernel, group, spread),
-        out_shape=jax.ShapeDtypeStruct(shape, x.dtype),
-        in_specs=[pl.BlockSpec(memory_space=pl.ANY)],
-        out_specs=pl.BlockSpec(memory_space=pl.ANY),
-        scratch_shapes=[
-            pltpu.SemaphoreType.DMA((group,)),
-            pltpu.SemaphoreType.DMA((group,)),
-            pltpu.SemaphoreType.DMA(()),
-        ],
+        functools.partial(reduce_kernel, n, combine),
+        out_shape=jax.ShapeDtypeStruct(x.shape, x.dtype),
+        in_specs=[pl.BlockSpec(memory_space=pltpu.VMEM)],
+        out_specs=pl.BlockSpec(memory_space=pltpu.VMEM),
+        scratch_shapes=[pltpu.VMEM(x.shape, x.dtype), pltpu.VMEM(x.shape[1:], x.dtype)]
+        + [pltpu.SemaphoreType.DMA((n,))] * 4,
         compiler_params=pltpu.CompilerParams(
             collective_id=collective_id, has_side_effects=True
         ),
     )(x)
 
 
-def summed(x, collective_id):
-    n = lax.axis_size("seq")
-    shares = exchanged(x.reshape(n, -1, x.shape[1]), collective_id)
-    total = jnp.sum(shares, axis=0)
-    return exchanged(total, collective_id + 1, spread=True).reshape(x.shape)
+def added(shares):
+    return jnp.sum(shares, axis=0)
+
+
+def softmax_shares(shares):
+    column = lax.broadcasted_iota(jnp.int32, shares.shape, 2)
+    at_peak = column == RHD
+    peak = jnp.max(jnp.where(at_peak, shares, -jnp.inf), axis=2, keepdims=True)
+    top = jnp.max(peak, axis=0, keepdims=True)
+    sums = jnp.sum(shares * jnp.exp(peak - top), axis=0)
+    return jnp.where(at_peak[0], top[0], sums)
 
 
 def swapped(value):
@@ -1049,76 +1601,89 @@
     hidden_units = up_bias.shape[0]
     hidden_pad = -(-hidden_units // 128) * 128
     proj_units = gate_proj.shape[1] // n
+    own_width = heads * HD
+    unit_lanes = -(-proj_units // 128) * 128
     out_width = down_proj.shape[1] * n
 
     def my_half(value):
         return lax.dynamic_slice_in_dim(value, core * half, half, 0)
+
+    input_f32 = patches.astype(jnp.float32)
+    normed_in = layer_norm(input_f32, ln1_gain, ln1_bias).astype(low)
+    lanes = -(-HD // 128) * 128
+
+    def wide(heads_of):
+        return jnp.pad(heads_of, [(0, 0)] * (heads_of.ndim - 1) + [(0, lanes - HD)])
+
+    def compact(parts):
+        joined = jnp.concatenate([p[..., :HD] for p in parts], axis=-1)
+        room = -(-joined.shape[-1] // 128) * 128 - joined.shape[-1]
+        return jnp.pad(joined, [(0, 0)] * (joined.ndim - 1) + [(0, room)])
+
+    head_shard = compact([split_heads(w, heads) for w in (q_weight, k_weight, v_weight)])
+    normed_half, head_weight = gathered_beside(
+        my_half(normed_in), jnp.concatenate([head_shard] * 2, axis=0), 2
+    )
+
+    unit_weights = jnp.stack([gate_proj, up_proj]).reshape(2, shard, n, proj_units)
+    unit_weights = jnp.pad(unit_weights, ((0, 0),) * 3 + ((0, unit_lanes - proj_units),))
+    ctx_width = rk_weight.shape[1]
+    ctx_shard = jnp.concatenate([rk_weight, rv_weight], axis=1)
+    unit_weights, normed_half, head_weight, ctx_shard = lax.optimization_barrier(
+        (unit_weights.transpose(2, 0, 1, 3), normed_half, head_weight, ctx_shard)
+    )
+    w_ctx = lax.all_gather(ctx_shard, "seq", axis=0, tiled=True)
+    w_ctxkey, w_ctxval = w_ctx[:, :ctx_width], w_ctx[:, ctx_width:]
+    unit_weights = lax.all_to_all(unit_weights, "seq", 0, 0)
+    normed_half = lax.dynamic_slice_in_dim(normed_half, window_start // rows, window // rows, 0)
+    normed_window = in_order(
+        normed_half[:, None], swapped(normed_half)[:, None], 1
+    ).reshape(window, width)
+    head_weight = head_weight.reshape(width, -1)
+    head_weight = jnp.concatenate(
+        [wide(head_weight[:, i * HD : (i + 1) * HD]) for i in range(3)], axis=1
+    )
+    head = me - part * heads
+    q_bias_one = lax.dynamic_slice_in_dim(q_bias, head * HD, HD, 0)
+    v_bias_one = lax.dynamic_slice_in_dim(v_bias, head * HD, HD, 0)
+    bias_one = jnp.concatenate(
+        [wide(q_bias_one), jnp.zeros((lanes,), jnp.float32), wide(v_bias_one)]
+    )
+    qkv = (product(normed_window, head_weight) + bias_one).astype(low)
+    query_one = lax.dynamic_slice_in_dim(qkv[:, :lanes], query_start, queries, 0)
+    key_one = qkv[:, lanes : 2 * lanes]
+    value_one = qkv[:, 2 * lanes :]
+    key_ids = image_ids(
+        lengths, window_start + jnp.arange(window, dtype=jnp.int32), total_rows
+    )
+    query_ids = lax.dynamic_slice_in_dim(key_ids, query_start, queries, 0)[:, None]
+    key_ids = key_ids[None, :]
+    attend, attend_back = attention_calls(queries, window, lanes, rows, scaling)
+    attended_one, lse_one = attend(query_one, key_one, value_one, query_ids, key_ids)
+    attended_low = join_heads(
+        exchanged([attended_one.reshape(heads, rows, lanes)], 3)[0][:, :, :HD]
+    )
 
     vision_shard = jnp.concatenate(
         [
             padded_columns(up_weight, hidden_pad),
             padded_columns(down_weight.T, hidden_pad),
             o_weight.T,
-            q_weight,
-            k_weight,
-            v_weight,
         ],
         axis=1,
     )
-    vision = lax.all_gather(vision_shard, "seq", axis=0, tiled=True)
+    unit_weights, vision_shard, attended_low, down_proj = lax.optimization_barrier(
+        (unit_weights, vision_shard, attended_low, down_proj)
+    )
+    vision, down_mine = gathered_beside(vision_shard, down_proj.reshape(n, proj_units, -1), 17)
+    vision = vision.reshape(width, -1)
+    down_mine = down_mine.transpose(1, 0, 2).reshape(proj_units, out_width)
     w_up = vision[:, :hidden_units]
     w_down_t = vision[:, hidden_pad : hidden_pad + hidden_units]
-    at = 2 * hidden_pad
-    own_width = heads * HD
-    w_out_t, w_query, w_key, w_value = (
-        vision[:, at + i * own_width : at + (i + 1) * own_width] for i in range(4)
-    )
-    w_ctx = lax.all_gather(
-        jnp.concatenate([rk_weight, rv_weight], axis=1), "seq", axis=0, tiled=True
-    )
-    ctx_width = rk_weight.shape[1]
-    w_ctxkey, w_ctxval = w_ctx[:, :ctx_width], w_ctx[:, ctx_width:]
-
-    input_f32 = patches.astype(jnp.float32)
-    normed_in = layer_norm(input_f32, ln1_gain, ln1_bias).astype(low)
-    head_shard = jnp.concatenate(
-        [split_heads(w, heads) for w in (q_weight, k_weight, v_weight)], axis=2
-    )
-    head_weight = exchanged(jnp.concatenate([head_shard] * 2, axis=0), 1).reshape(width, 3 * HD)
-    normed_half = gathered_blocks(my_half(normed_in), 2)
-    normed_half = lax.dynamic_slice_in_dim(normed_half, window_start // rows, window // rows, 0)
-    normed_window = in_order(
-        normed_half[:, None], swapped(normed_half)[:, None], 1
-    ).reshape(window, width)
-    head = me - part * heads
-    q_bias_one = lax.dynamic_slice_in_dim(q_bias, head * HD, HD, 0)
-    v_bias_one = lax.dynamic_slice_in_dim(v_bias, head * HD, HD, 0)
-    bias_one = jnp.concatenate([q_bias_one, jnp.zeros_like(q_bias_one), v_bias_one])
-    qkv = (product(normed_window, head_weight) + bias_one).astype(low)
-    query_one = lax.dynamic_slice_in_dim(qkv[:, :HD], query_start, queries, 0)
-    key_one = qkv[:, HD : 2 * HD]
-    value_one = qkv[:, 2 * HD :]
-    key_ids = image_ids(
-        lengths, window_start + jnp.arange(window, dtype=jnp.int32), total_rows
-    )
-    query_ids = lax.dynamic_slice_in_dim(key_ids, query_start, queries, 0)[:, None]
-    key_ids = key_ids[None, :]
-    attend, attend_back = attention_calls(queries, window, HD, rows, scaling)
-    attended_one, lse_one = attend(query_one, key_one, value_one, query_ids, key_ids)
-    attended_low = join_heads(exchanged(attended_one.reshape(heads, rows, HD), 3, group=heads))
-
-    def to_units(matrix):
-        blocks = matrix.reshape(shard, n, proj_units).transpose(1, 0, 2)
-        return lax.all_to_all(blocks, "seq", 0, 0).reshape(width, proj_units)
-
-    gate_mine, up_mine = to_units(gate_proj), to_units(up_proj)
-    down_mine = (
-        lax.all_to_all(down_proj.reshape(n, proj_units, -1), "seq", 0, 0)
-        .transpose(1, 0, 2)
-        .reshape(proj_units, out_width)
-    )
-    w_gate = jnp.concatenate([gate_mine, swapped(gate_mine)], axis=1)
-    w_up_proj = jnp.concatenate([up_mine, swapped(up_mine)], axis=1)
+    w_out_t = vision[:, 2 * hidden_pad :]
+    unit_weights = unit_weights.transpose(1, 0, 2, 3).reshape(2, width, unit_lanes)
+    w_gate, w_up_proj = jnp.concatenate([unit_weights, swapped(unit_weights)], axis=2)
+    down_mine = jnp.pad(down_mine, ((0, unit_lanes - proj_units), (0, 0)))
     w_down_proj = jnp.concatenate([down_mine, swapped(down_mine)], axis=0)
 
     attn_part = product_nt(attended_low, w_out_t)
@@ -1130,28 +1695,21 @@
     after_mlp = after_attn + paired(product_nt(active_low, w_down_t)) + down_bias
     features = after_mlp.astype(low)
 
-    features_all = gathered_blocks(my_half(features), 4).reshape(n * half, width)
-    proj_gate = product(features_all, w_gate)
-    proj_up = product(features_all, w_up_proj)
-    silu_gate = jax.nn.silu(proj_gate)
-    proj_hidden = (silu_gate * proj_up).astype(low)
-
-    def chunked(terms, chunks):
-        return terms.reshape(n, half, chunks, -1).transpose(2, 0, 1, 3)
+    features_all, proj_gate, proj_up, proj_hidden = gathered_units(
+        my_half(features), w_gate, w_up_proj, 4
+    )
 
     def joined_chunks(sums):
         return sums.transpose(1, 0, 2).reshape(half, -1)
 
-    out_chunks = out_width // 512
-    out_terms = jnp.stack(
-        [
-            product(proj_hidden, w_down_proj[:, c * 512 : (c + 1) * 512]).astype(low)
-            for c in range(out_chunks)
-        ]
-    ).reshape(out_chunks, n, half, 512)
-    proj_out_low = joined_chunks(scattered_sum(out_terms, 5))
+    out_chunks = out_width // 256
+    proj_out_low = joined_chunks(scattered_down(proj_hidden, w_down_proj, out_chunks, 5))
     proj_out_half = proj_out_low.astype(jnp.float32)
     proj_out = in_order(proj_out_low, swapped(proj_out_low), 0).astype(jnp.float32)
+    qkv_shard, _ = lax.optimization_barrier(
+        (jnp.concatenate([q_weight, k_weight, v_weight], axis=1), proj_out_low)
+    )
+    w_qkv = lax.all_gather(qkv_shard, "seq", axis=0, tiled=True)
 
     context_low = rms_norm(proj_out, ctx_gain).astype(low)
     ctx_keys = product(context_low, w_ctxkey).astype(low)
@@ -1176,14 +1734,7 @@
     stats = partial_stats(lat_scores, value_grouped)
     packed = jnp.concatenate([stats[2], stats[0][..., None], stats[1][..., None]], axis=-1)
     packed = jnp.pad(packed.reshape(n, -1, RHD + 2), ((0, 0), (0, 0), (0, 126 - RHD)))
-    shares = exchanged(packed, 6)
-    share_peak = jnp.max(shares[..., RHD], axis=0)
-    share_scale = jnp.exp(shares[..., RHD] - share_peak)
-    share_sums = jnp.sum(shares * share_scale[..., None], axis=0)
-    share_sums = jnp.where(
-        jnp.arange(128) == RHD, share_peak[:, None], share_sums
-    )
-    merged = exchanged(share_sums, 7, spread=True).reshape(kv_heads, group, lat_rows, 128)
+    merged = reduced(packed, softmax_shares, 6).reshape(kv_heads, group, lat_rows, 128)
     lat_peak, lat_total, lat_numer = joint_stats(
         (merged[..., RHD], merged[..., RHD + 1], merged[..., :RHD]),
         partial_stats(self_scores, self_values),
@@ -1191,10 +1742,6 @@
     lat_lse = lat_peak + jnp.log(lat_total)
     pooled_exact = lat_numer / lat_total[..., None]
     pooled_low = pooled_exact.transpose(2, 0, 1, 3).reshape(lat_rows, -1).astype(low)
-    lat_mix = product(pooled_low, ro_weight)
-    ro_width = ro_weight.shape[1] // n
-    ro_columns = lax.dynamic_slice_in_dim(lat_grad, me * ro_width, ro_width, 1)
-    ro_weight_grad = product_tn(pooled_low, ro_columns)
     pooled_grad = product_nt(lat_grad, ro_weight).astype(low)
     pooled_grouped = pooled_grad.reshape(lat_rows, kv_heads, group, RHD)
     pooled_f32 = pooled_grouped.astype(jnp.float32)
@@ -1235,113 +1782,81 @@
     ctx_back = ctx_kept + swapped(ctx_sent).astype(jnp.float32)
     ctx_pull = jax.vjp(rms_norm, proj_out_half, ctx_gain)[1]
     proj_out_grad, ctx_gain_part = ctx_pull(ctx_back)
-    proj_out_grads = gathered_blocks(proj_out_grad.astype(low), 8).reshape(n * half, out_width)
+    _, feat_terms, unit_grads, down_grads = gathered_back(
+        proj_out_grad.astype(low),
+        w_gate,
+        w_up_proj,
+        w_down_proj,
+        features_all,
+        proj_gate,
+        proj_up,
+        width // 128,
+        8,
+    )
 
     query_part = ctx_query_term + first_block * self_query_term
-    query_sum = summed(query_part.reshape(lat_rows, -1), 9)
-    lat_queries_grad = query_sum.astype(low)
-    rq_rows = rq_weight.shape[0] // n
-    rq_weight_grad = product_tn(
-        lax.dynamic_slice_in_dim(lat_normed, me * rq_rows, rq_rows, 1), lat_queries_grad
-    )
     ctx_grads = jnp.concatenate([ctx_keys_grad, ctx_values_grad], axis=1)
     self_grads = jnp.concatenate([self_keys_grad, self_values_grad], axis=1)
     r_part = product_tn(context_low, ctx_grads) + first_block * product_tn(lat_normed, self_grads)
     r_grad = lax.psum_scatter(r_part.astype(low), "seq", scatter_dimension=0, tiled=True).astype(
         jnp.float32
     )
-    lat_part = (
-        product_nt(lat_queries_grad, rq_weight)
-        + product_nt(self_keys_grad, w_ctxkey)
-        + product_nt(self_values_grad, w_ctxval)
-    )
-    lat_back, lat_mix_sum = paired(lat_part), paired(lat_mix)
-    latents_out = latents + lat_mix_sum
-    lat_pull = jax.vjp(rms_norm, latents, lat_gain)[1]
-    lat_in_grad, lat_gain_grad = lat_pull(lat_back)
-    latents_grad = lat_grad.astype(jnp.float32) + lat_in_grad
-
-    hidden_pgrad = product_nt(proj_out_grads, w_down_proj)
-    silu_pull = jax.vjp(jax.nn.silu, proj_gate)[1]
-    gate_grad_low = silu_pull(hidden_pgrad * proj_up)[0].astype(low)
-    up_grad_low = (hidden_pgrad * silu_gate).astype(low)
-    feat_terms = (product_nt(gate_grad_low, w_gate) + product_nt(up_grad_low, w_up_proj)).astype(low)
-    feat_half = joined_chunks(scattered_sum(chunked(feat_terms, width // 384), 11))
+
+    feat_half = joined_chunks(scattered_sum(feat_terms, 11))
+
     proj_in_grad = in_order(feat_half, swapped(feat_half), 0).astype(jnp.float32)
-
-    def unit_grads(left, right, axis):
-        mine = lax.slice_in_dim(left, 0, proj_units, axis=1) if axis == 0 else left
-        other = lax.slice_in_dim(left, proj_units, 2 * proj_units, axis=1) if axis == 0 else left
-        mine_r = right if axis == 0 else lax.slice_in_dim(right, 0, proj_units, axis=1)
-        other_r = right if axis == 0 else lax.slice_in_dim(right, proj_units, 2 * proj_units, axis=1)
-        sent = swapped(product_tn(other, other_r).astype(low))
-        return (product_tn(mine, mine_r) + sent.astype(jnp.float32)).astype(low)
-
-    def to_rows(grad):
-        blocks = lax.all_to_all(grad.reshape(n, shard, proj_units), "seq", 0, 0)
-        return blocks.transpose(1, 0, 2).reshape(shard, n * proj_units).astype(jnp.float32)
-
-    gate_proj_grad = to_rows(unit_grads(features_all, gate_grad_low, 1))
-    up_proj_grad = to_rows(unit_grads(features_all, up_grad_low, 1))
-    down_blocks = unit_grads(proj_hidden, proj_out_grads, 0)
-    down_blocks = down_blocks.reshape(proj_units, n, -1).transpose(1, 0, 2)
-    down_proj_grad = (
-        lax.all_to_all(down_blocks, "seq", 0, 0)
-        .reshape(n * proj_units, -1)
-        .astype(jnp.float32)
-    )
+    def core_sum(mine, other):
+        return (mine.astype(jnp.float32) + swapped(other).astype(jnp.float32)).astype(low)
+
+    down_blocks = core_sum(
+        down_grads[:, :proj_units], down_grads[:, unit_lanes : unit_lanes + proj_units]
+    )
+    unit_blocks = core_sum(unit_grads[..., :unit_lanes], unit_grads[..., unit_lanes:])
+    unit_blocks = unit_blocks.reshape(n, 2 * shard, unit_lanes)
 
     mlp_out_grad = feat_grad.astype(jnp.float32) + proj_in_grad
     mlp_out_low = mlp_out_grad.astype(low)
-    down_part_t = product_tn(mlp_out_low, active_low)
     down_bias_part = jnp.sum(mlp_out_low.astype(jnp.float32), axis=0)
     active_grad = product(mlp_out_low, w_down_t)
     gelu_pull = jax.vjp(gelu_tanh, hidden)[1]
     hidden_grad = gelu_pull(active_grad)[0].astype(low)
-    up_part = product_tn(mlp_in, hidden_grad)
     up_bias_part = jnp.sum(hidden_grad.astype(jnp.float32), axis=0)
     mlp_back = paired(product_nt(hidden_grad, w_up))
     ln2_pull = jax.vjp(layer_norm, after_attn, ln2_gain, ln2_bias)[1]
     norm_grad, ln2_gain_part, ln2_bias_part = ln2_pull(mlp_back)
     attn_out_grad = mlp_out_grad + norm_grad
     attn_out_low = attn_out_grad.astype(low)
-    o_part_t = product_tn(attn_out_low, attended_low)
     o_bias_part = jnp.sum(attn_out_low.astype(jnp.float32), axis=0)
-    vision_part = jnp.concatenate(
+    vision_chunks = 13
+    vision_width = 2 * hidden_pad + own_width
+    vision_cols = -(-vision_width // (vision_chunks * 128)) * 128
+    vision_left = jnp.stack([mlp_in.T, mlp_out_low.T, attn_out_low.T])
+    vision_right = jnp.concatenate(
         [
-            padded_columns(up_part.astype(low), hidden_pad),
-            padded_columns(down_part_t.astype(low), hidden_pad),
-            o_part_t.astype(low),
+            padded_columns(hidden_grad, hidden_pad),
+            padded_columns(active_low, hidden_pad),
+            padded_columns(attended_low, vision_chunks * vision_cols - 2 * hidden_pad),
         ],
         axis=1,
     )
-    vision_grad = lax.psum_scatter(vision_part, "seq", scatter_dimension=0, tiled=True).astype(
-        jnp.float32
-    )
-    up_weight_grad = vision_grad[:, :hidden_units]
-    down_weight_grad = vision_grad[:, hidden_pad : hidden_pad + hidden_units].T
-    o_weight_grad = vision_grad[:, 2 * hidden_pad :].T
+    spans = (0, hidden_pad // 128, 2 * hidden_pad // 128)
+    vision_grad = scattered_vision(vision_left, vision_right, spans, vision_chunks, 18)
 
     attended_grad = product(attn_out_low, w_out_t).astype(low)
-    grad_one = exchanged(split_heads(attended_grad, heads), 12, group=heads).reshape(queries, HD)
+    grad_one = exchanged([wide(split_heads(attended_grad, heads))], 12)[0].reshape(queries, lanes)
     dq, dk, dv = attend_back(
         query_one, key_one, value_one, grad_one, query_ids, key_ids, lse_one
     )
     dq_window = lax.dynamic_update_slice_in_dim(
-        jnp.zeros((window, HD), jnp.float32), dq, query_start, 0
-    )
-    dqkv = jnp.concatenate([dq_window, dk, dv], axis=1)
+        jnp.zeros((window, lanes), jnp.float32), dq, query_start, 0
+    )
+    dqkv = compact([dq_window, dk, dv])
     dqkv_low = dqkv.astype(low)
-    head_grad = product_tn(normed_window, dqkv_low).astype(low).reshape(n, shard, 3 * HD)
-    head_grads = exchanged(head_grad, 13).astype(jnp.float32)
-    head_grads = head_grads[:heads] + head_grads[heads:]
-    q_weight_grad, k_weight_grad, v_weight_grad = (
-        join_heads(head_grads[:, :, i * HD : (i + 1) * HD]) for i in range(3)
-    )
+    head_grad = product_tn(normed_window, dqkv_low).astype(low).reshape(n, shard, -1)
     bias_row = jnp.sum(dqkv_low.astype(jnp.float32), axis=0)
-    bias_rows = jnp.zeros((heads, 3 * HD), jnp.float32)
+    bias_rows = jnp.zeros((heads, dqkv.shape[1]), jnp.float32)
     bias_rows = lax.dynamic_update_slice_in_dim(bias_rows, bias_row[None], head, 0)
-    blocks = dqkv.reshape(window // rows, rows, 3 * HD)
+    blocks = dqkv.reshape(window // rows, rows, -1)
     other_block = jnp.where(part == 0, blocks[-1], blocks[0]).astype(low)
     across = lax.ppermute(
         other_block, "seq", [(i, (i + heads) % n) for i in range(n)]
@@ -1351,14 +1866,16 @@
     own_blocks = own_blocks + jnp.where(
         (jnp.arange(heads) == edge)[:, None, None], across[None], 0.0
     )
-    token_grads = exchanged(own_blocks.astype(low), 14, group=heads)
+    head_grads, token_grads = exchanged([head_grad, own_blocks.astype(low)], 13)
+    head_grads, token_grads, unit_blocks = lax.optimization_barrier(
+        (head_grads, token_grads, unit_blocks)
+    )
+    unit_rows = lax.all_to_all(unit_blocks, "seq", 0, 0)
     queries_grad, keys_grad, values_grad = (
         join_heads(token_grads[:, :, i * HD : (i + 1) * HD]) for i in range(3)
     )
     attn_back = paired(
-        product_nt(queries_grad, w_query)
-        + product_nt(keys_grad, w_key)
-        + product_nt(values_grad, w_value)
+        product_nt(jnp.concatenate([queries_grad, keys_grad, values_grad], axis=1), w_qkv)
     )
     ln1_pull = jax.vjp(layer_norm, input_f32, ln1_gain, ln1_bias)[1]
     in_grad, ln1_gain_part, ln1_bias_part = ln1_pull(attn_back)
@@ -1368,7 +1885,7 @@
         ln1_gain_part,
         ln1_bias_part,
         bias_rows[:, :HD].reshape(-1),
-        bias_rows[:, 2 * HD :].reshape(-1),
+        bias_rows[:, 2 * HD : 3 * HD].reshape(-1),
         o_bias_part,
         ln2_gain_part,
         ln2_bias_part,
@@ -1377,15 +1894,59 @@
         ctx_gain_part,
     )
     joined_smalls = jnp.concatenate(smalls)
+    joined_smalls = jnp.concatenate([joined_smalls, query_part.reshape(-1)])
     length = joined_smalls.shape[0]
     per_device = -(-length // (n * 1024)) * 1024
     joined_smalls = jnp.pad(joined_smalls, (0, n * per_device - length))
-    small_sum = summed(joined_smalls.reshape(n * per_device // 128, 128), 15).reshape(-1)
+    small_sum = reduced(joined_smalls.reshape(n, per_device // 128, 128), added, 15).reshape(-1)
+    (
+        small_sum,
+        down_blocks,
+        unit_rows,
+        vision_grad,
+        head_grads,
+        pooled_late,
+        self_grads,
+    ) = lax.optimization_barrier(
+        (small_sum, down_blocks, unit_rows, vision_grad, head_grads, pooled_low, self_grads)
+    )
+    down_rows = lax.all_to_all(down_blocks, "seq", 0, 0)
+    vision_grad = vision_grad.transpose(1, 0, 2).reshape(shard, -1).astype(jnp.float32)
+    up_weight_grad = vision_grad[:, :hidden_units]
+    down_weight_grad = vision_grad[:, hidden_pad : hidden_pad + hidden_units].T
+    o_weight_grad = vision_grad[:, 2 * hidden_pad : vision_width].T
+    head_grads = head_grads.astype(jnp.float32)
+    head_grads = head_grads[:heads] + head_grads[heads:]
+    q_weight_grad, k_weight_grad, v_weight_grad = (
+        join_heads(head_grads[:, :, i * HD : (i + 1) * HD]) for i in range(3)
+    )
+    lat_mix = product(pooled_late, ro_weight)
+    ro_width = ro_weight.shape[1] // n
+    ro_columns = lax.dynamic_slice_in_dim(lat_grad, me * ro_width, ro_width, 1)
+    ro_weight_grad = product_tn(pooled_late, ro_columns)
     small_sums, begin = [], 0
     for small in smalls:
         small_sums.append(small_sum[begin : begin + small.shape[0]])
         begin += small.shape[0]
     ctx_gain_grad = small_sums[9] + swapped(small_sums[9])
+
+    query_sum = small_sum[begin : begin + query_part.size].reshape(lat_rows, -1)
+    lat_queries_grad = query_sum.astype(low)
+    rq_rows = rq_weight.shape[0] // n
+    rq_weight_grad = product_tn(
+        lax.dynamic_slice_in_dim(lat_normed, me * rq_rows, rq_rows, 1), lat_queries_grad
+    )
+    lat_part = product_nt(lat_queries_grad, rq_weight) + product_nt(self_grads, w_ctx)
+    down_proj_grad = down_rows.reshape(n * proj_units, -1).astype(jnp.float32)
+    unit_rows = unit_rows.reshape(n, 2, shard, unit_lanes)[..., :proj_units]
+    gate_proj_grad, up_proj_grad = (
+        unit_rows.transpose(1, 2, 0, 3).reshape(2, shard, n * proj_units).astype(jnp.float32)
+    )
+    lat_back, lat_mix_sum = paired(lat_part), paired(lat_mix)
+    latents_out = latents + lat_mix_sum
+    lat_pull = jax.vjp(rms_norm, latents, lat_gain)[1]
+    lat_in_grad, lat_gain_grad = lat_pull(lat_back)
+    latents_grad = lat_grad.astype(jnp.float32) + lat_in_grad
     return (
         features,
         latents_out,

time: 1700 us -> 1340 us (0.79)
  waiting for transfers between devices: 308 us -> 33.6 us
  matrix products: 227 us -> 76.3 us
  Pallas kernels: 842 us -> 972 us
  starting transfers between devices: 68.3 us -> 28.6 us
  local copies, waits for them, and re-layouts: 143 us -> 117 us
    pallas_call x14 -> x11, Pallas kernels: 577 us -> 872 us  [the longest x2 215 us: gathered_beside(): pl.pallas_call(functools.partial(gather_beside_kernel, n), out_shape=[jax...]
    pallas_call x2 -> x1, Pallas kernels: 228 us -> 64.9 us  [scattered_sum(): pl.pallas_call(functools.partial(scatter_kernel, n, chunks), out_shape=ja...]
    ppermute x1, waiting for transfers between devices: 118 us -> 2.75 us  [tokens_travel(): lax.ppermute(other_block, 'seq', [(i, (i + heads) % n) for i in range(n)])]
    unnamed x5 -> x3, waiting for transfers between devices: 104 us -> 0.05 us
    dot_general x14 -> x5, matrix products: 69.8 us -> 11 us  [product_tn(): lax.dot_general(left, right, (((0,), (0,)), ((), ())), preferred_element_...]
    all_to_all x6 -> x3, waiting for transfers between devices: 86 us -> 30.5 us  [the longest x1 28.7 us: tokens_travel(): down_rows = lax.all_to_all(down_blocks, 'seq', 0, 0)]
    dot_general x15 -> x9, matrix products: 75 us -> 27.5 us  [product_nt(): lax.dot_general(left, right, (((1,), (1,)), ((), ())), preferred_element_...]
    dot_general x20 -> x10, matrix products: 73.5 us -> 28.1 us  [product(): return jnp.dot(left, right, preferred_element_type=jnp.float32)]
  transfers between devices with their start and end apart: 28 -> 22, of which waited for: 4 -> 4; matrix products, arithmetic and copies ran while one was open for 24% -> 19% of each run, Pallas kernels for 48% -> 57%
where the time goes in v2:
time: 1340 us; the launch traced here: 1330 us
  Pallas kernels  972 us (73%)
  local copies, waits for them, and re-layouts  117 us (9%)
  other arithmetic  88.5 us (7%)
  matrix products  76.3 us (6%)
  waiting for transfers between devices  33.6 us (3%)
  starting transfers between devices  28.6 us (2%)
  between operations  15.8 us (1%)
    pallas_call x2, Pallas kernels, gathered_beside(): pl.pallas_call(functools.partial(gather_beside_kernel, n), out_shape=[jax...  215 us
    pallas_call x1, Pallas kernels, gathered_back(): pl.pallas_call(functools.partial(units_back_kernel, n), out_shape=[jax.Sh...  183 us
    pallas_call x1, Pallas kernels, scattered_down(): pl.pallas_call(functools.partial(down_kernel, n, chunks), out_shape=jax.S...  172 us
    pallas_call x1, Pallas kernels, scattered_vision(): pl.pallas_call(functools.partial(vision_kernel, n, chunks, spans), out_sh...  113 us
    pallas_call x1, Pallas kernels, scattered_sum(): pl.pallas_call(functools.partial(scatter_kernel, n, chunks), out_shape=ja...  64.9 us
    pallas_call x2, Pallas kernels, reduced(): pl.pallas_call(functools.partial(reduce_kernel, n, combine), out_shape=ja...  63.5 us
    pallas_call x1, Pallas kernels, gathered_units(): pl.pallas_call(functools.partial(units_kernel, n), out_shape=[jax.ShapeDt...  62.4 us
    pallas_call x3, Pallas kernels, exchanged(): pl.pallas_call(functools.partial(exchange_kernel, n, groups), out_shape=[...  61.7 us
  transfers between devices with their start and end apart: 22, of which 4 were waited for; matrix products, arithmetic and copies ran while one was open for 19% of the time, Pallas kernels for 57%

profile of v2, /device:TPU:14, one launch (start us, length us, event | category | flops | bytes accessed | tf_op | source)
XLA Modules:
  0.0 1332.2 jit_solution(17014284687675207991)
XLA Ops:
  17.4 55.1 %shard_map.492 = (bf16[16,128,1152]{2,1,0:T(8,128)(2,1)}, bf16[16,72,256]{2,1,0:T(8,128)(2,1)}) custom-call(bf16[128,1152]{1,0:T(8,128)(2,1)} %copy.346.x_ref, bf16[16,72,256]{2,1,0:T(8,128)(2,1)} %pad_maximum_fusion.5.y_ref), custom_call_target="tpu_custom_call" | custom-call | tf_op jit(solution)/shard_map/pallas_call | solution.py:675
  81.6 7.5 all-to-all-start
  109.5 14.6 %shard_map.493 = (bf16[2048,128]{1,0:T(8,128)(2,1)}, f32[2048,1]{1,0:T(8,128)}) custom-call(bf16[2048,128]{1,0:T(8,128)(2,1)} %constant_dynamic-slice_fusion.1.q_ref, bf16[2304,128]{1,0:T(8,128)(2,1)} %get-tuple-element.297.k_ref, bf16[2304,128]{1,0:T(8,128)(2,1)} %get-tuple-element.296.v_ref, s32[2048,1]{1,0:T(8,128)} %copy.349.qid_ref, ...), custom_call_target="tpu_custom_call" | custom-call | flops 2415919104 | bytes 2228224 | tf_op jit(solution)/shard_map/pallas_call | solution.py:1662
  124.0 17.1 %shard_map.494 = bf16[8,256,128]{2,1,0:T(8,128)(2,1)} custom-call(bf16[8,256,128]{2,1,0:T(8,128)(2,1)} %bitcast.308), custom_call_target="tpu_custom_call" | custom-call | tf_op jit(solution)/shard_map/pallas_call | solution.py:1366
  146.4 160.0 %shard_map.495 = (bf16[16,72,4928]{2,1,0:T(8,128)(2,1)}, bf16[16,448,256]{2,1,0:T(8,128)(2,1)}) custom-call(bf16[72,4928]{1,0:T(8,128)(2,1)} %fusion.128.x_ref, bf16[16,448,256]{2,1,0:T(8,128)(2,1)} %bitcast.280), custom_call_target="tpu_custom_call" | custom-call | tf_op jit(solution)/shard_map/pallas_call | solution.py:675
  320.4 3.7 multiply_convert_fusion
  329.1 4.1 fusion.34
  333.2 62.4 %shard_map.496 = (bf16[16,128,1152]{2,1,0:T(8,128)(2,1)}, f32[16,128,1024]{2,1,0:T(8,128)}, f32[16,128,1024]{2,1,0:T(8,128)}, bf16[16,128,1024]{2,1,0:T(8,128)(2,1)}) custom-call(bf16[128,1152]{1,0:T(8,128)(2,1)} %copy.357.x_ref, bf16[1152,1024]{1,0:T(8,128)(2,1)} %get-tuple-element.293.w_gate_ref, bf16[1152,1024]{1,0:T(8,128)(2,1)} %get-tuple-element.292.w_up_ref), custom_call_target="tpu_custom_call" | custom-call | tf_op jit(solution)/shard_map/pallas_call | solution.py:769
  395.6 7.8 pad_maximum_fusion.w_down_ref
  403.4 172.4 %shard_map.497 = bf16[16,128,256]{2,1,0:T(8,128)(2,1)} custom-call(bf16[16,128,1024]{2,1,0:T(8,128)(2,1)} %get-tuple-element.76.hidden_ref, bf16[1024,4096]{1,0:T(8,128)(2,1)} %pad_maximum_fusion.w_down_ref), custom_call_target="tpu_custom_call" | custom-call | tf_op jit(solution)/shard_map/pallas_call | solution.py:1220
  577.4 5.5 convolution_convert_fusion.1
  610.4 28.9 %shard_map.498 = f32[16,32,128]{2,1,0:T(8,128)} custom-call(f32[16,32,128]{2,1,0:T(8,128)} %select_maximum_fusion.2.x_ref), custom_call_target="tpu_custom_call" | custom-call | tf_op jit(solution)/shard_map/pallas_call | solution.py:1414
  657.6 3.6 fusion.46
  664.1 183.0 %shard_map.499 = (bf16[16,128,4096]{2,1,0:T(8,128)(2,1)}, bf16[9,16,128,128]{3,2,1,0:T(8,128)(2,1)}, bf16[16,2,72,1024]{3,2,1,0:T(8,128)(2,1)}, bf16[16,1024,256]{2,1,0:T(8,128)(2,1)}) custom-call(bf16[128,4096]{1,0:T(8,128)(2,1)} %fusion.47.x_ref, bf16[1152,1024]{1,0:T(8,128)(2,1)} %get-tuple-element.293.w_gate_ref, ...), custom_call_target="tpu_custom_call" | custom-call | tf_op jit(solution)/shard_map/pallas_call | solution.py:961
  847.2 64.9 %shard_map.500 = bf16[9,128,128]{2,1,0:T(8,128)(2,1)} custom-call(bf16[9,16,128,128]{3,2,1,0:T(8,128)(2,1)} %get-tuple-element.82.p_ref), custom_call_target="tpu_custom_call" | custom-call | tf_op jit(solution)/shard_map/pallas_call | solution.py:1188
  916.9 6.2 convert_reduce_fusion.1
  923.2 5.6 fusion.209
  935.4 4.3 slice.187
  952.6 15.9 %shard_map.501 = bf16[8,256,128]{2,1,0:T(8,128)(2,1)} custom-call(bf16[8,256,128]{2,1,0:T(8,128)(2,1)} %pad.74.refs_0_), custom_call_target="tpu_custom_call" | custom-call | tf_op jit(solution)/shard_map/pallas_call | solution.py:1366
  968.5 21.4 %shard_map.502 = (f32[2048,128]{1,0:T(8,128)}, f32[2304,128]{1,0:T(8,128)}, f32[2304,128]{1,0:T(8,128)}) custom-call(bf16[2048,128]{1,0:T(8,128)(2,1)} %constant_dynamic-slice_fusion.1.q_ref, bf16[2304,128]{1,0:T(8,128)(2,1)} %get-tuple-element.297.k_ref, bf16[2304,128]{1,0:T(8,128)(2,1)} %get-tuple-element.296.v_ref, bf16[2048,128]{1,0:T(8,128)(2,1)} %bitcast.307, ...), custom_call_target="tpu_custom_call" | custom-call | flops 6039797760 | bytes 5636096 | tf_op jit(solution)/shard_map/pallas_call | solution.py:1847
  1001.2 28.7 %shard_map.503 = (bf16[16,72,256]{2,1,0:T(8,128)(2,1)}, bf16[8,256,256]{2,1,0:T(8,128)(2,1)}) custom-call(bf16[16,72,256]{2,1,0:T(8,128)(2,1)} %bitcast.305, bf16[8,256,256]{2,1,0:T(8,128)(2,1)} %add_convert_fusion.3.refs_1_), custom_call_target="tpu_custom_call" | custom-call | tf_op jit(solution)/shard_map/pallas_call | solution.py:1366
  1029.9 4.5 add_convert_fusion.2
  1034.5 6.2 all-to-all-start.1
  1055.0 4.5 fusion.210
  1060.8 6.2 add_convert_fusion
  1074.5 9.0 concatenate.83
  1084.2 34.6 %shard_map.504 = f32[16,32,128]{2,1,0:T(8,128)} custom-call(f32[16,32,128]{2,1,0:T(8,128)} %bitcast.293), custom_call_target="tpu_custom_call" | custom-call | tf_op jit(solution)/shard_map/pallas_call | solution.py:1414
  1121.7 113.4 %shard_map.505 = bf16[13,72,384]{2,1,0:T(8,128)(2,1)} custom-call(bf16[3,1152,256]{2,1,0:T(8,128)(2,1)} %pad_maximum_fusion.4.left_ref, bf16[256,4992]{1,0:T(8,128)(2,1)} %fusion.29.right_ref), custom_call_target="tpu_custom_call" | custom-call | tf_op jit(solution)/shard_map/pallas_call | solution.py:1313
  1235.1 9.0 all-to-all-start.2
  1262.6 4.9 fusion.215
  1291.1 28.7 %all-to-all-done.2 = bf16[16,448,256]{2,1,0:T(8,128)(2,1)} async-done(((bf16[16,448,256]{2,1,0:T(8,128)(2,1)}), bf16[16,448,256]{2,1,0:T(8,128)(2,1)}, u32[]{:S(2)}, u32[]{:S(2)}) %all-to-all-start.2) | async-done | bytes 3670048 | tf_op jit(solution)/shard_map/all_to_all | solution.py:1913
  1319.8 5.7 bitcast_convert_fusion
  (484 shorter events, 217.0 us)
Async XLA Ops:
  78.9 21.1 %collective-permute-start = (bf16[9,128,1152]{2,1,0:T(8,128)(2,1)}, bf16[9,128,1152]{2,1,0:T(8,128)(2,1)}, u32[]{:S(2)}, u32[]{:S(2)}) collective-permute-start(bf16[9,128,1152]{2,1,0:T(8,128)(2,1)} %constant_dynamic-slice_fusion.2), channel_id=1, source_target_pairs={{0,1},{1,0},{2,3},{3,2},{4,5},{5,4},{6,7},{7,6},{8,9},{9,8},{10,11... | collective-permute-start | bytes 7962632 | tf_op jit(solution)/shard_map/ppermute | solution.py:1441
  81.6 63.4 %all-to-all-start = ((bf16[16,2,72,512]{3,2,1,0:T(8,128)(2,1)}), bf16[16,2,72,512]{3,2,1,0:T(8,128)(2,1)S(1)}, u32[]{:S(2)}, u32[]{:S(2)}) async-start(bf16[16,2,72,512]{3,2,1,0:T(8,128)(2,1)} %copy.347), calls=%async_computation | async-start | bytes 4718592 | tf_op jit(solution)/shard_map/all_to_all | solution.py:1637
  89.1 500.0 %all-gather.3.cloned.1.call-start = ((), (), s32[]{:S(2)}) async-start(), calls=%async_computation.4 | async-start | bytes 3342336 | tf_op jit(solution)/shard_map/all_gather | solution.py:1635
  143.1 163.3 %copy-start.43 = (bf16[256,8,72]{0,2,1:T(8,128)(2,1)S(1)}, bf16[256,8,72]{0,2,1:T(8,128)(2,1)}, u32[]{:S(2)}) copy-start(bf16[256,8,72]{0,2,1:T(8,128)(2,1)} %copy.350) | copy-start | bytes 884740
  308.5 8.9 collective-permute-start.1
  308.6 746.3 %all-gather.5.cloned.1.call-start = ((), (), s32[]{:S(2)}) async-start(), calls=%async_computation.5 | async-start | bytes 4386816 | tf_op jit(solution)/shard_map/all_gather | solution.py:1712
  309.1 17.2 %copy-start.109 = (f32[64]{0:T(128)}, f32[64]{0:T(128)S(1)}, u32[]{:S(2)}) copy-start(f32[64]{0:T(128)S(1)} %fusion.178) | copy-start | bytes 772
  314.4 81.2 %collective-permute-start.4 = (bf16[512,4096]{1,0:T(8,128)(2,1)}, bf16[512,4096]{1,0:T(8,128)(2,1)}, u32[]{:S(2)}, u32[]{:S(2)}) collective-permute-start(bf16[512,4096]{1,0:T(8,128)(2,1)} %pad.72), channel_id=1, source_target_pairs={{0,1},{1,0},{2,3},{3,2},{4,5},{5,4},{6,7},{7,6},{8,9},{9,8},{10,11... | collective-permute-start | bytes 12582920 | tf_op jit(solution)/shard_map/ppermute | solution.py:1441
  317.0 12.1 collective-permute-start.3
  325.7 2.2 collective-permute-start.2
  326.4 264.8 %copy-start.16 = (bf16[64,4096]{1,0:T(8,128)(2,1)}, bf16[64,4096]{1,0:T(8,128)(2,1)S(1)}, u32[]{:S(2)}) copy-start(bf16[64,4096]{1,0:T(8,128)(2,1)S(1)} %multiply_convert_fusion.1) | copy-start | bytes 1572868
  577.3 20.3 %collective-permute-start.5 = (bf16[128,4096]{1,0:T(8,128)(2,1)S(1)}, bf16[128,4096]{1,0:T(8,128)(2,1)}, u32[]{:S(2)}, u32[]{:S(2)}) collective-permute-start(bf16[128,4096]{1,0:T(8,128)(2,1)S(1)} %bitcast.263), channel_id=1, source_target_pairs={{0,1},{1,0},{2,3},{3,2},{4,5},{5,4},{6,7},{7,6},{8,9},{9,8},{10,11... | collective-permute-start | bytes 3145736 | tf_op jit(solution)/shard_map/ppermute | solution.py:1441
  597.4 647.8 %reduce-scatter.2.cloned.1.call-start = ((), (), s32[]{:S(2)}) async-start(), calls=%async_computation.6 | async-start | bytes 3342336 | tf_op jit(solution)/shard_map/reduce_scatter | solution.py:1801
  605.6 37.8 %copy-start.84 = (f32[2,4,64]{2,1,0:T(4,128)S(1)}, f32[2,4,64]{2,1,0:T(4,128)}, u32[]{:S(2)}) copy-start(f32[2,4,64]{2,1,0:T(4,128)} %copy-done.83) | copy-start | bytes 6148
  605.6 37.8 %copy-start.89 = (f32[2,4,64]{2,1,0:T(4,128)S(1)}, f32[2,4,64]{2,1,0:T(4,128)}, u32[]{:S(2)}) copy-start(f32[2,4,64]{2,1,0:T(4,128)} %fusion.144) | copy-start | bytes 6148
  653.3 4.3 collective-permute-start.6
  847.2 66.8 %copy-start.12 = (bf16[128,4096]{1,0:T(8,128)(2,1)S(1)}, bf16[128,4096]{1,0:T(8,128)(2,1)}, u32[]{:S(2)}) copy-start(bf16[128,4096]{1,0:T(8,128)(2,1)} %copy-done.11) | copy-start | bytes 3145732
  847.2 66.8 %copy-start.53 = (bf16[2,96,256]{2,1,0:T(8,128)(2,1)S(1)}, bf16[2,96,256]{2,1,0:T(8,128)(2,1)}, u32[]{:S(2)}) copy-start(bf16[2,96,256]{2,1,0:T(8,128)(2,1)} %copy-done.52) | copy-start | bytes 294916
  847.2 66.8 %copy-start.103 = (f32[256]{0:T(256)S(1)}, f32[256]{0:T(256)}, u32[]{:S(2)}) copy-start(f32[256]{0:T(256)} %copy-done.102) | copy-start | bytes 3076
  913.9 2.8 collective-permute-start.7
  928.8 11.3 collective-permute-start.8
  935.3 94.7 %collective-permute-start.10 = (bf16[16,2,72,512]{3,2,1,0:T(8,128)(2,1)}, bf16[16,2,72,512]{3,2,1,0:T(8,128)(2,1)}, u32[]{:S(2)}, u32[]{:S(2)}) collective-permute-start(bf16[16,2,72,512]{3,2,1,0:T(8,128)(2,1)} %slice.180), channel_id=1, source_target_pairs={{0,1},{1,0},{2,3},{3,2},{4,5},{5,4},{6,7},{7,6},{8,9},{9,8},{10,11... | collective-permute-start | bytes 7077896 | tf_op jit(solution)/shard_map/ppermute | solution.py:1441
  939.8 121.1 %collective-permute-start.12 = (bf16[16,448,256]{2,1,0:T(8,128)(2,1)}, bf16[16,448,256]{2,1,0:T(8,128)(2,1)}, u32[]{:S(2)}, u32[]{:S(2)}) collective-permute-start(bf16[16,448,256]{2,1,0:T(8,128)(2,1)} %slice.187), channel_id=1, source_target_pairs={{0,1},{1,0},{2,3},{3,2},{4,5},{5,4},{6,7},{7,6},{8,9},{9,8},{10,11... | collective-permute-start | bytes 11010056 | tf_op jit(solution)/shard_map/ppermute | solution.py:1441
  945.7 49.0 %slice-start.4 = ((s8[5308416]{0:T(1024)(128)(4,1)}), s8[1114112]{0:T(1024)(128)(4,1)S(1)}, s32[]{:S(2)}) async-start(s8[5308416]{0:T(1024)(128)(4,1)} %bitcast.275), calls=%async_computation.11 | async-start | bytes 2228224
  968.5 26.3 %slice-start.5 = ((s8[5308416]{0:T(1024)(128)(4,1)}), s8[4194304]{0:T(1024)(128)(4,1)S(1)}, s32[]{:S(2)}) async-start(s8[5308416]{0:T(1024)(128)(4,1)} %bitcast.275), calls=%async_computation.12 | async-start | bytes 8388608
  992.9 7.1 collective-permute-start.9
  1034.5 200.6 %all-to-all-start.1 = ((bf16[16,144,512]{2,1,0:T(8,128)(2,1)}), bf16[16,144,512]{2,1,0:T(8,128)(2,1)}, u32[]{:S(2)}, u32[]{:S(2)}) async-start(bf16[16,144,512]{2,1,0:T(8,128)(2,1)} %bitcast.268), calls=%async_computation.1 | async-start | bytes 4718592 | tf_op jit(solution)/shard_map/all_to_all | solution.py:1873
  1059.4 7.6 collective-permute-start.11
  1235.1 84.7 %all-to-all-start.2 = ((bf16[16,448,256]{2,1,0:T(8,128)(2,1)}), bf16[16,448,256]{2,1,0:T(8,128)(2,1)}, u32[]{:S(2)}, u32[]{:S(2)}) async-start(bf16[16,448,256]{2,1,0:T(8,128)(2,1)} %add_convert_fusion), calls=%async_computation.2 | async-start | bytes 7340032 | tf_op jit(solution)/shard_map/all_to_all | solution.py:1913
  1249.7 34.7 %collective-permute-start.15 = (f32[4096]{0:T(1024)S(1)}, f32[4096]{0:T(1024)S(1)}, u32[]{:S(2)}, u32[]{:S(2)}) collective-permute-start(f32[4096]{0:T(1024)S(1)} %slice.207), channel_id=1, source_target_pairs={{0,1},{1,0},{2,3},{3,2},{4,5},{5,4},{6,7},{7,6},{8,9},{9,8},{10,11... | collective-permute-start | bytes 49160 | tf_op jit(solution)/shard_map/ppermute | solution.py:1441
  1269.5 16.3 %collective-permute-start.14 = (bf16[64,4096]{1,0:T(8,128)(2,1)}, bf16[64,4096]{1,0:T(8,128)(2,1)}, u32[]{:S(2)}, u32[]{:S(2)}) collective-permute-start(bf16[64,4096]{1,0:T(8,128)(2,1)} %get-tuple-element.351), channel_id=1, source_target_pairs={{0,1},{1,0},{2,3},{3,2},{4,5},{5,4},{6,7},{7,6},{8,9},{9,8},{10,11... | collective-permute-start | bytes 1572872 | tf_op jit(solution)/shard_map/ppermute | solution.py:1441
  1272.3 15.4 %collective-permute-start.13 = (bf16[64,4096]{1,0:T(8,128)(2,1)}, bf16[64,4096]{1,0:T(8,128)(2,1)}, u32[]{:S(2)}, u32[]{:S(2)}) collective-permute-start(bf16[64,4096]{1,0:T(8,128)(2,1)} %get-tuple-element.353), channel_id=1, source_target_pairs={{0,1},{1,0},{2,3},{3,2},{4,5},{5,4},{6,7},{7,6},{8,9},{9,8},{10,11... | collective-permute-start | bytes 1572872 | tf_op jit(solution)/shard_map/ppermute | solution.py:1441
  (117 other events, 458.3 us)
Sparse Core Ops, SparseCore 0:
  308.8 88.5 all-gather.2
  597.5 83.0 all-gather.4
  932.1 166.5 reduce-scatter.1

commit v3 on v2

--- a/solution.py
+++ b/solution.py
@@ -514,8 +514,8 @@
 
 
 class Arrivals:
-    def __init__(self, n, x_ref, slots, sent, landed, local):
-        self.n, self.layers = n, n // 4
+    def __init__(self, n, x_ref, slots, sent, landed, local, reach=None):
+        self.n, self.layers, self.reach = n, n // 4, reach
         self.x_ref, self.slots, self.sent, self.landed = x_ref, slots, sent, landed
         self.me, self.z, self.a, self.b, self.step_a, self.step_b = place()
         self.partners = neighbours(self.layers)
@@ -525,6 +525,13 @@
 
     def at(self, layer, of_a, of_b):
         return layer * 4 + of_a * self.step_a + of_b * self.step_b
+
+    def wanted(self, slot, layer):
+        if self.reach is None:
+            return slot >= 0
+        return jnp.where(
+            layer < self.layers // 2, slot < self.reach, slot >= self.n - self.reach
+        )
 
     def send(self, slot, device, way, source=None):
         return pltpu.make_async_remote_copy(
@@ -563,11 +570,11 @@
         self.own.start()
         me, x_ref = self.me, self.x_ref
 
-        @pl.when(self.up)
+        @pl.when(self.up & self.wanted(me, self.z + 1))
         def _():
             self.send(me, self.to_up, 0, x_ref).start()
 
-        @pl.when(self.down)
+        @pl.when(self.down & self.wanted(me, self.z - 1))
         def _():
             self.send(me, self.to_down, 1, x_ref).start()
 
@@ -577,20 +584,21 @@
 
     def take(self, i):
         layer, over_a, over_b, slot = self.block(i)
-
-        @pl.when(i > 0)
+        here = (i > 0) & self.wanted(slot, self.z)
+
+        @pl.when(here)
         def _():
             self.send(slot, self.to_b, 3).wait_recv()
 
-        @pl.when((i > 0) & (over_b == 0))
+        @pl.when(here & (over_b == 0))
         def _():
             @pl.when(over_a == 0)
             def _():
-                @pl.when((layer < self.z) & self.up)
+                @pl.when((layer < self.z) & self.up & self.wanted(slot, self.z + 1))
                 def _():
                     self.send(slot, self.to_up, 0).start()
 
-                @pl.when((layer > self.z) & self.down)
+                @pl.when((layer > self.z) & self.down & self.wanted(slot, self.z - 1))
                 def _():
                     self.send(slot, self.to_down, 1).start()
 
@@ -603,15 +611,22 @@
     def drain(self):
         def body(layer, _):
             slot = self.at(layer, self.a, self.b)
-            self.send(slot, self.to_a, 2).wait_send()
-            self.send(slot, self.to_b, 3).wait_send()
-            self.send(self.at(layer, 1 - self.a, self.b), self.to_b, 3).wait_send()
-
-            @pl.when((layer <= self.z) & self.up)
+            beyond = self.at(layer, 1 - self.a, self.b)
+
+            @pl.when(self.wanted(slot, self.z))
+            def _():
+                self.send(slot, self.to_a, 2).wait_send()
+                self.send(slot, self.to_b, 3).wait_send()
+
+            @pl.when(self.wanted(beyond, self.z))
+            def _():
+                self.send(beyond, self.to_b, 3).wait_send()
+
+            @pl.when((layer <= self.z) & self.up & self.wanted(slot, self.z + 1))
             def _():
                 self.send(slot, self.to_up, 0).wait_send()
 
-            @pl.when((layer >= self.z) & self.down)
+            @pl.when((layer >= self.z) & self.down & self.wanted(slot, self.z - 1))
             def _():
                 self.send(slot, self.to_down, 1).wait_send()
 
@@ -654,9 +669,9 @@
     )(x)
 
 
-def gather_beside_kernel(n, x_ref, y_ref, o_ref, y_out, sent, landed, local, *semaphores):
+def gather_beside_kernel(n, reach, x_ref, y_ref, o_ref, y_out, sent, landed, local, *semaphores):
     beside = Beside(n, 1, ((y_ref, y_out),), sent, landed, local)
-    arrivals = Arrivals(n, x_ref, o_ref, *semaphores)
+    arrivals = Arrivals(n, x_ref, o_ref, *semaphores, reach=reach)
     arrivals.start(beside)
 
     def body(i, _):
@@ -669,11 +684,11 @@
     arrivals.drain()
 
 
-def gathered_beside(x, y, collective_id):
+def gathered_beside(x, y, collective_id, reach=None):
     n = lax.axis_size("seq")
     anywhere = pl.BlockSpec(memory_space=pl.ANY)
     return pl.pallas_call(
-        functools.partial(gather_beside_kernel, n),
+        functools.partial(gather_beside_kernel, n, reach),
         out_shape=[
             jax.ShapeDtypeStruct((n,) + x.shape, x.dtype),
             jax.ShapeDtypeStruct(y.shape, y.dtype),
@@ -791,14 +806,17 @@
     x_ref,
     w_gate_ref,
     w_up_ref,
-    w_down_ref,
+    down_mine_ref,
+    down_other_ref,
     features_ref,
     gate_ref,
     up_ref,
     slots,
     terms_ref,
-    dunits_ref,
-    ddown_ref,
+    dunits_mine,
+    dunits_other,
+    ddown_mine,
+    ddown_other,
     x_buf,
     features_buf,
     gate_buf,
@@ -812,8 +830,7 @@
     units_buf,
     load_sem,
     store_sem,
-    down_sem,
-    units_sem,
+    out_sem,
     *semaphores,
 ):
     arrivals = Arrivals(n, x_ref, slots, *semaphores)
@@ -821,8 +838,11 @@
     gate_sum[...] = jnp.zeros_like(gate_sum)
     up_sum[...] = jnp.zeros_like(up_sum)
     down_sum[...] = jnp.zeros_like(down_sum)
-    out_width = w_down_ref.shape[1]
-    tile = 1024
+    units, cols = down_mine_ref.shape[1:]
+    room = hidden_grad.shape[1] // 2
+    out_width = n * cols
+    several = 4
+    tile = several * cols
     chunks, chunk = terms_ref.shape[0], terms_ref.shape[3]
 
     def stores(pair):
@@ -864,10 +884,16 @@
         hidden_grad[...] = jnp.zeros_like(hidden_grad)
 
         def back_tile(t, _):
-            columns = pl.ds(pl.multiple_of(t * tile, tile), tile)
-            hidden_grad[...] += product_nt(
-                pair_rows(x_buf[buf, :, :, columns]), w_down_ref[:, columns]
-            )
+            for i, held in enumerate((down_mine_ref, down_other_ref)):
+                hidden_grad[:, i * room : i * room + units] += sum(
+                    product_nt(
+                        pair_rows(
+                            x_buf[buf, :, :, pl.ds(pl.multiple_of(t * tile + j * cols, cols), cols)]
+                        ),
+                        held[t * several + j],
+                    )
+                    for j in range(several)
+                )
             return 0
 
         lax.fori_loop(0, out_width // tile, back_tile, 0)
@@ -900,58 +926,57 @@
 
         def down_tile(t, _):
             columns = pl.ds(pl.multiple_of(t * tile, tile), tile)
-            down_sum[:, columns] += product(hidden_t, pair_rows(x_buf[buf, :, :, columns]))
+            x = pair_rows(x_buf[buf, :, :, columns])
+            for i in range(2):
+                down_sum[i, :, columns] += product(hidden_t[i * room : i * room + units], x)
             return 0
 
         lax.fori_loop(0, out_width // tile, down_tile, 0)
         return 0
 
     lax.fori_loop(0, n // 2, body, 0)
-    share = out_width // n
-
-    def down_store(j):
-        return pltpu.make_async_copy(
-            down_buf.at[j % 2], ddown_ref.at[j], down_sem.at[j % 2]
-        )
-
-    def down_out(j, _):
+    def grad_stores(j):
+        return [
+            pltpu.make_async_copy(source, target.at[j], out_sem.at[j % 2, i])
+            for i, (source, target) in enumerate(
+                (
+                    (down_buf.at[j % 2, 0], ddown_mine),
+                    (down_buf.at[j % 2, 1], ddown_other),
+                    (units_buf.at[j % 2, 0], dunits_mine),
+                    (units_buf.at[j % 2, 1], dunits_other),
+                )
+            )
+        ]
+
+    def grads_out(j, _):
         @pl.when(j >= 2)
         def _():
-            down_store(j - 2).wait()
-
-        columns = pl.ds(pl.multiple_of(j * share, share), share)
-        down_buf[j % 2] = down_sum[:, columns].astype(jnp.bfloat16)
-        down_store(j).start()
+            for store in grad_stores(j - 2):
+                store.wait()
+
+        columns = pl.ds(pl.multiple_of(j * cols, cols), cols)
+        down_buf[j % 2] = down_sum[:, :, columns].astype(jnp.bfloat16)
+        owned = units_buf.shape[3]
+        owner = pl.ds(pl.multiple_of(j * owned, 8), owned)
+        for i in range(2):
+            for k, total in enumerate((gate_sum, up_sum)):
+                units_buf[j % 2, i, k] = total[owner, i * room : (i + 1) * room].astype(
+                    jnp.bfloat16
+                )
+        for store in grad_stores(j):
+            store.start()
         return 0
 
-    lax.fori_loop(0, n, down_out, 0)
-
-    def units_store(j):
-        return pltpu.make_async_copy(units_buf.at[j % 2], dunits_ref.at[j], units_sem.at[j % 2])
-
-    def units_out(j, _):
-        @pl.when(j >= 2)
-        def _():
-            units_store(j - 2).wait()
-
-        owned = units_buf.shape[2]
-        owner = pl.ds(pl.multiple_of(j * owned, 8), owned)
-        for i, total in enumerate((gate_sum, up_sum)):
-            units_buf[j % 2, i] = total[owner].astype(jnp.bfloat16)
-        units_store(j).start()
-        return 0
-
-    lax.fori_loop(0, n, units_out, 0)
-    units_store(n - 2).wait()
-    units_store(n - 1).wait()
-    down_store(n - 2).wait()
-    down_store(n - 1).wait()
+    lax.fori_loop(0, n, grads_out, 0)
+    for j in (n - 2, n - 1):
+        for store in grad_stores(j):
+            store.wait()
     for store in stores(n // 2 - 1):
         store.wait()
     arrivals.drain()
 
 
-def gathered_back(x, w_gate, w_up, w_down, features, gate, up, chunks, collective_id):
+def gathered_back(x, w_gate, w_up, mine, other, features, gate, up, chunks, collective_id):
     n = lax.axis_size("seq")
     rows, out_width = x.shape
     width, units = w_gate.shape
@@ -963,11 +988,13 @@
         out_shape=[
             jax.ShapeDtypeStruct((n,) + x.shape, low),
             jax.ShapeDtypeStruct((chunks, n, rows, width // chunks), low),
-            jax.ShapeDtypeStruct((n, 2, width // n, units), low),
-            jax.ShapeDtypeStruct((n, units, out_width // n), low),
+            jax.ShapeDtypeStruct((n, 2, width // n, units // 2), low),
+            jax.ShapeDtypeStruct((n, 2, width // n, units // 2), low),
+            jax.ShapeDtypeStruct(mine.shape, low),
+            jax.ShapeDtypeStruct(mine.shape, low),
         ],
-        in_specs=[anywhere] + [in_vmem] * 3 + [anywhere] * 3,
-        out_specs=[anywhere] * 4,
+        in_specs=[anywhere] + [in_vmem] * 4 + [anywhere] * 3,
+        out_specs=[anywhere] * 6,
         scratch_shapes=[
             pltpu.VMEM((2, 2, rows, out_width), low),
             pltpu.VMEM((2, 2, rows, width), low),
@@ -977,22 +1004,21 @@
             pltpu.VMEM((2 * rows, units), exact),
             pltpu.VMEM((width, units), exact),
             pltpu.VMEM((width, units), exact),
-            pltpu.VMEM((units, out_width), exact),
-            pltpu.VMEM((2, units, out_width // n), low),
-            pltpu.VMEM((2, 2, width // n, units), low),
+            pltpu.VMEM((2, mine.shape[1], out_width), exact),
+            pltpu.VMEM((2, 2) + mine.shape[1:], low),
+            pltpu.VMEM((2, 2, 2, width // n, units // 2), low),
             pltpu.SemaphoreType.DMA((2, 2, 4)),
             pltpu.SemaphoreType.DMA((2, chunks)),
-            pltpu.SemaphoreType.DMA((2,)),
-            pltpu.SemaphoreType.DMA((2,)),
+            pltpu.SemaphoreType.DMA((2, 4)),
         ]
         + gather_semaphores(n),
         compiler_params=pltpu.CompilerParams(
             collective_id=collective_id, has_side_effects=True, vmem_limit_bytes=60 * 2**20
         ),
-    )(x, w_gate, w_up, w_down, features, gate, up)
-
-
-def scatter_kernel(n, chunks, p_ref, o_ref, from_b, from_a, from_down, from_up, *semaphores, fill=None):
+    )(x, w_gate, w_up, mine, other, features, gate, up)
+
+
+def scatter_kernel(n, chunks, p_ref, o_ref, from_b, from_a, from_down, from_up, *semaphores, fill=None, work=None):
     layers = n // 4
     me, z, a, b, step_a, step_b = place()
     partners = neighbours(layers)
@@ -1131,6 +1157,8 @@
 
     def step(t, _):
         when_chunk(t + 1, fill_and_send)
+        if work is not None:
+            work(t)
         when_chunk(t, send_a)
         when_chunk(t - 1, join_line)
         inner = (z > 0) & (z < layers - 1)
@@ -1197,37 +1225,39 @@
     )(terms)
 
 
-def down_kernel(n, chunks, hidden_ref, w_down_ref, o_ref, p_ref, *scratch):
-    cols = w_down_ref.shape[1] // chunks
+def down_kernel(n, hidden_ref, mine_ref, other_ref, o_ref, p_ref, *scratch):
+    units = mine_ref.shape[1]
+    room = hidden_ref.shape[2] // 2
 
     def fill(c):
-        columns = pl.ds(pl.multiple_of(c * cols, cols), cols)
-
         def body(pair, _):
             owners = pl.ds(2 * pair, 2)
-            terms = product(pair_rows(hidden_ref[owners]), w_down_ref[:, columns])
-            p_ref[c, owners] = terms.astype(p_ref.dtype).reshape(2, -1, cols)
+            terms = sum(
+                product(pair_rows(hidden_ref[owners, :, pl.ds(i * room, units)]), held[c])
+                for i, held in enumerate((mine_ref, other_ref))
+            )
+            p_ref[c, owners] = terms.astype(p_ref.dtype).reshape((2,) + p_ref.shape[2:])
             return 0
 
         lax.fori_loop(0, n // 2, body, 0)
 
-    scatter_kernel(n, chunks, p_ref, o_ref, *scratch, fill=fill)
-
-
-def scattered_down(hidden, w_down, chunks, collective_id):
+    scatter_kernel(n, n, p_ref, o_ref, *scratch, fill=fill)
+
+
+def scattered_down(hidden, mine, other, collective_id):
     n, rows = hidden.shape[:2]
-    block = (rows, w_down.shape[1] // chunks)
+    block = (rows, mine.shape[2])
     return pl.pallas_call(
-        functools.partial(down_kernel, n, chunks),
-        out_shape=jax.ShapeDtypeStruct((chunks,) + block, hidden.dtype),
-        in_specs=[pl.BlockSpec(memory_space=pltpu.VMEM)] * 2,
+        functools.partial(down_kernel, n),
+        out_shape=jax.ShapeDtypeStruct((n,) + block, hidden.dtype),
+        in_specs=[pl.BlockSpec(memory_space=pltpu.VMEM)] * 3,
         out_specs=pl.BlockSpec(memory_space=pltpu.VMEM),
-        scratch_shapes=[pltpu.VMEM((chunks, n) + block, hidden.dtype)]
-        + scatter_scratch(chunks, n, block, hidden.dtype),
+        scratch_shapes=[pltpu.VMEM((n, n) + block, hidden.dtype)]
+        + scatter_scratch(n, n, block, hidden.dtype),
         compiler_params=pltpu.CompilerParams(
             collective_id=collective_id, has_side_effects=True, vmem_limit_bytes=60 * 2**20
         ),
-    )(hidden, w_down)
+    )(hidden, mine, other)
 
 
 class Beside:
@@ -1287,9 +1317,15 @@
             own.wait()
 
 
-def vision_kernel(n, chunks, spans, left_ref, right_ref, o_ref, p_ref, *scratch):
+def vision_kernel(n, chunks, spans, scaling, *refs):
+    left_ref, right_ref, *attention = refs[:9]
+    o_ref, *grads = refs[9:13]
+    p_ref, *scratch = refs[13:]
     cols = right_ref.shape[1] // chunks
     shard = left_ref.shape[1] // n
+    tile = 128
+    for total in grads[1:]:
+        total[...] = jnp.zeros_like(total)
 
     def fill(c):
         def body(t, _):
@@ -1304,23 +1340,33 @@
 
         lax.fori_loop(0, cols // 128, body, 0)
 
-    scatter_kernel(n, chunks, p_ref, o_ref, *scratch, fill=fill)
-
-
-def scattered_vision(left, right, spans, chunks, collective_id):
+    tiles = attention[0].shape[0] // tile
+    assert tiles <= chunks + n // 4
+
+    def work(t):
+        @pl.when(t < tiles)
+        def _():
+            attend_back_tile(scaling, tile, jnp.minimum(t, tiles - 1), *attention, *grads)
+
+    scatter_kernel(n, chunks, p_ref, o_ref, *scratch, fill=fill, work=work)
+
+
+def scattered_vision(left, right, attention, scaling, spans, chunks, collective_id):
     n = lax.axis_size("seq")
     block = (left.shape[1] // n, right.shape[1] // chunks)
+    in_vmem = pl.BlockSpec(memory_space=pltpu.VMEM)
     return pl.pallas_call(
-        functools.partial(vision_kernel, n, chunks, spans),
-        out_shape=jax.ShapeDtypeStruct((chunks,) + block, left.dtype),
-        in_specs=[pl.BlockSpec(memory_space=pltpu.VMEM)] * 2,
-        out_specs=pl.BlockSpec(memory_space=pltpu.VMEM),
+        functools.partial(vision_kernel, n, chunks, spans, scaling),
+        out_shape=[jax.ShapeDtypeStruct((chunks,) + block, left.dtype)]
+        + [jax.ShapeDtypeStruct(x.shape, jnp.float32) for x in attention[:3]],
+        in_specs=[in_vmem] * 9,
+        out_specs=[in_vmem] * 4,
         scratch_shapes=[pltpu.VMEM((chunks, n) + block, left.dtype)]
         + scatter_scratch(chunks, n, block, left.dtype),
         compiler_params=pltpu.CompilerParams(
             collective_id=collective_id, has_side_effects=True, vmem_limit_bytes=60 * 2**20
         ),
-    )(left, right)
+    )(left, right, *attention)
 
 
 def exchange_kernel(n, groups, *refs):
@@ -1468,26 +1514,22 @@
     lse_ref[...] = peak + jnp.log(total)
 
 
-def attend_back_kernel(
-    scaling, q_ref, k_ref, v_ref, g_ref, qid_ref, kid_ref, lse_ref, dq_ref, dk_ref, dv_ref
-):
-    @pl.when(pl.program_id(0) == 0)
-    def _():
-        dk_ref[...] = jnp.zeros_like(dk_ref)
-        dv_ref[...] = jnp.zeros_like(dv_ref)
-
-    scores = product_nt(q_ref[...], k_ref[...]) * scaling
-    scores = jnp.where(qid_ref[...] == kid_ref[...], scores, -1e30)
-    probability = jnp.exp(scores - lse_ref[...])
-    dprob = product_nt(g_ref[...], v_ref[...])
+def attend_back_tile(scaling, tile, t, q_ref, k_ref, v_ref, g_ref, qid_ref, kid_ref, lse_ref, *grads):
+    dq_ref, dk_ref, dv_ref = grads
+    rows = pl.ds(pl.multiple_of(t * tile, tile), tile)
+    query, grad = q_ref[rows], g_ref[rows]
+    scores = product_nt(query, k_ref[...]) * scaling
+    scores = jnp.where(qid_ref[rows] == kid_ref[...], scores, -1e30)
+    probability = jnp.exp(scores - lse_ref[rows])
+    dprob = product_nt(grad, v_ref[...])
     inner = jnp.sum(probability * dprob, axis=1, keepdims=True)
     low = (probability * (dprob - inner)).astype(jnp.bfloat16)
-    dq_ref[...] = product(low, k_ref[...]) * scaling
-    dk_ref[...] += product_tn(low, q_ref[...]) * scaling
-    dv_ref[...] += product_tn(probability.astype(jnp.bfloat16), g_ref[...])
-
-
-def attention_calls(queries, window, width, tile, scaling):
+    dq_ref[rows] = product(low, k_ref[...]) * scaling
+    dk_ref[...] += product_tn(low, query) * scaling
+    dv_ref[...] += product_tn(probability.astype(jnp.bfloat16), grad)
+
+
+def attention_call(queries, window, width, tile, scaling):
     tiled = lambda columns: pl.BlockSpec((tile, columns), lambda i: (i, 0))
     whole = lambda rows, columns: pl.BlockSpec((rows, columns), lambda i: (0, 0))
     params = pltpu.CompilerParams(vmem_limit_bytes=56 * 2**20)
@@ -1513,32 +1555,7 @@
             transcendentals=queries * window,
         ),
     )
-    backward = pl.pallas_call(
-        functools.partial(attend_back_kernel, scaling),
-        grid=(queries // tile,),
-        in_specs=[
-            tiled(width),
-            whole(window, width),
-            whole(window, width),
-            tiled(width),
-            tiled(1),
-            whole(1, window),
-            tiled(1),
-        ],
-        out_specs=[tiled(width), whole(window, width), whole(window, width)],
-        out_shape=[
-            jax.ShapeDtypeStruct((queries, width), jnp.float32),
-            jax.ShapeDtypeStruct((window, width), jnp.float32),
-            jax.ShapeDtypeStruct((window, width), jnp.float32),
-        ],
-        compiler_params=params,
-        cost_estimate=pl.CostEstimate(
-            flops=10 * queries * window * width,
-            bytes_accessed=2 * (6 * window + 4 * queries) * 128,
-            transcendentals=queries * window,
-        ),
-    )
-    return forward, backward
+    return forward
 
 
 def padded_columns(matrix, width):
@@ -1622,7 +1639,7 @@
 
     head_shard = compact([split_heads(w, heads) for w in (q_weight, k_weight, v_weight)])
     normed_half, head_weight = gathered_beside(
-        my_half(normed_in), jnp.concatenate([head_shard] * 2, axis=0), 2
+        my_half(normed_in), jnp.concatenate([head_shard] * 2, axis=0), 2, reach=window // rows
     )
 
     unit_weights = jnp.stack([gate_proj, up_proj]).reshape(2, shard, n, proj_units)
@@ -1658,7 +1675,7 @@
     )
     query_ids = lax.dynamic_slice_in_dim(key_ids, query_start, queries, 0)[:, None]
     key_ids = key_ids[None, :]
-    attend, attend_back = attention_calls(queries, window, lanes, rows, scaling)
+    attend = attention_call(queries, window, lanes, rows, scaling)
     attended_one, lse_one = attend(query_one, key_one, value_one, query_ids, key_ids)
     attended_low = join_heads(
         exchanged([attended_one.reshape(heads, rows, lanes)], 3)[0][:, :, :HD]
@@ -1677,14 +1694,12 @@
     )
     vision, down_mine = gathered_beside(vision_shard, down_proj.reshape(n, proj_units, -1), 17)
     vision = vision.reshape(width, -1)
-    down_mine = down_mine.transpose(1, 0, 2).reshape(proj_units, out_width)
+    down_other = swapped(down_mine)
     w_up = vision[:, :hidden_units]
     w_down_t = vision[:, hidden_pad : hidden_pad + hidden_units]
     w_out_t = vision[:, 2 * hidden_pad :]
     unit_weights = unit_weights.transpose(1, 0, 2, 3).reshape(2, width, unit_lanes)
     w_gate, w_up_proj = jnp.concatenate([unit_weights, swapped(unit_weights)], axis=2)
-    down_mine = jnp.pad(down_mine, ((0, unit_lanes - proj_units), (0, 0)))
-    w_down_proj = jnp.concatenate([down_mine, swapped(down_mine)], axis=0)
 
     attn_part = product_nt(attended_low, w_out_t)
     attn_sum = attn_part + swapped(attn_part)
@@ -1702,8 +1717,7 @@
     def joined_chunks(sums):
         return sums.transpose(1, 0, 2).reshape(half, -1)
 
-    out_chunks = out_width // 256
-    proj_out_low = joined_chunks(scattered_down(proj_hidden, w_down_proj, out_chunks, 5))
+    proj_out_low = joined_chunks(scattered_down(proj_hidden, down_mine, down_other, 5))
     proj_out_half = proj_out_low.astype(jnp.float32)
     proj_out = in_order(proj_out_low, swapped(proj_out_low), 0).astype(jnp.float32)
     qkv_shard, _ = lax.optimization_barrier(
@@ -1782,11 +1796,17 @@
     ctx_back = ctx_kept + swapped(ctx_sent).astype(jnp.float32)
     ctx_pull = jax.vjp(rms_norm, proj_out_half, ctx_gain)[1]
     proj_out_grad, ctx_gain_part = ctx_pull(ctx_back)
-    _, feat_terms, unit_grads, down_grads = gathered_back(
+    ctx_grads = jnp.concatenate([ctx_keys_grad, ctx_values_grad], axis=1)
+    self_grads = jnp.concatenate([self_keys_grad, self_values_grad], axis=1)
+    r_part = product_tn(context_low, ctx_grads) + first_block * product_tn(lat_normed, self_grads)
+    r_part, proj_out_grad = lax.optimization_barrier((r_part.astype(low), proj_out_grad))
+    r_grad = lax.psum_scatter(r_part, "seq", scatter_dimension=0, tiled=True).astype(jnp.float32)
+    _, feat_terms, units_mine, units_other, downs_mine, downs_other = gathered_back(
         proj_out_grad.astype(low),
         w_gate,
         w_up_proj,
-        w_down_proj,
+        down_mine,
+        down_other,
         features_all,
         proj_gate,
         proj_up,
@@ -1795,23 +1815,14 @@
     )
 
     query_part = ctx_query_term + first_block * self_query_term
-    ctx_grads = jnp.concatenate([ctx_keys_grad, ctx_values_grad], axis=1)
-    self_grads = jnp.concatenate([self_keys_grad, self_values_grad], axis=1)
-    r_part = product_tn(context_low, ctx_grads) + first_block * product_tn(lat_normed, self_grads)
-    r_grad = lax.psum_scatter(r_part.astype(low), "seq", scatter_dimension=0, tiled=True).astype(
-        jnp.float32
-    )
-
     feat_half = joined_chunks(scattered_sum(feat_terms, 11))
 
     proj_in_grad = in_order(feat_half, swapped(feat_half), 0).astype(jnp.float32)
     def core_sum(mine, other):
         return (mine.astype(jnp.float32) + swapped(other).astype(jnp.float32)).astype(low)
 
-    down_blocks = core_sum(
-        down_grads[:, :proj_units], down_grads[:, unit_lanes : unit_lanes + proj_units]
-    )
-    unit_blocks = core_sum(unit_grads[..., :unit_lanes], unit_grads[..., unit_lanes:])
+    down_blocks = core_sum(downs_mine, downs_other)
+    unit_blocks = core_sum(units_mine, units_other)
     unit_blocks = unit_blocks.reshape(n, 2 * shard, unit_lanes)
 
     mlp_out_grad = feat_grad.astype(jnp.float32) + proj_in_grad
@@ -1840,12 +1851,16 @@
         axis=1,
     )
     spans = (0, hidden_pad // 128, 2 * hidden_pad // 128)
-    vision_grad = scattered_vision(vision_left, vision_right, spans, vision_chunks, 18)
-
     attended_grad = product(attn_out_low, w_out_t).astype(low)
     grad_one = exchanged([wide(split_heads(attended_grad, heads))], 12)[0].reshape(queries, lanes)
-    dq, dk, dv = attend_back(
-        query_one, key_one, value_one, grad_one, query_ids, key_ids, lse_one
+    vision_grad, dq, dk, dv = scattered_vision(
+        vision_left,
+        vision_right,
+        (query_one, key_one, value_one, grad_one, query_ids, key_ids, lse_one),
+        scaling,
+        spans,
+        vision_chunks,
+        18,
     )
     dq_window = lax.dynamic_update_slice_in_dim(
         jnp.zeros((window, lanes), jnp.float32), dq, query_start, 0
@@ -1893,8 +1908,11 @@
         down_bias_part,
         ctx_gain_part,
     )
-    joined_smalls = jnp.concatenate(smalls)
-    joined_smalls = jnp.concatenate([joined_smalls, query_part.reshape(-1)])
+    pieces = [
+        jnp.pad(small, (0, -small.shape[0] % 1024)) for small in smalls + (query_part.reshape(-1),)
+    ]
+    begins = [sum(p.shape[0] for p in pieces[:i]) for i in range(len(pieces))]
+    joined_smalls = jnp.concatenate(pieces)
     length = joined_smalls.shape[0]
     per_device = -(-length // (n * 1024)) * 1024
     joined_smalls = jnp.pad(joined_smalls, (0, n * per_device - length))
@@ -1924,13 +1942,12 @@
     ro_width = ro_weight.shape[1] // n
     ro_columns = lax.dynamic_slice_in_dim(lat_grad, me * ro_width, ro_width, 1)
     ro_weight_grad = product_tn(pooled_late, ro_columns)
-    small_sums, begin = [], 0
-    for small in smalls:
-        small_sums.append(small_sum[begin : begin + small.shape[0]])
-        begin += small.shape[0]
+    small_sums = [
+        small_sum[begin : begin + small.shape[0]] for begin, small in zip(begins, smalls)
+    ]
     ctx_gain_grad = small_sums[9] + swapped(small_sums[9])
 
-    query_sum = small_sum[begin : begin + query_part.size].reshape(lat_rows, -1)
+    query_sum = small_sum[begins[-1] : begins[-1] + query_part.size].reshape(lat_rows, -1)
     lat_queries_grad = query_sum.astype(low)
     rq_rows = rq_weight.shape[0] // n
     rq_weight_grad = product_tn(

time: 1340 us -> 1290 us (0.963)
  Pallas kernels: 972 us -> 946 us
  local copies, waits for them, and re-layouts: 117 us -> 91.9 us
    pallas_call x5 -> x4, Pallas kernels: 522 us -> 506 us  [the longest x2 206 us: gathered_beside(): pl.pallas_call(functools.partial(gather_beside_kernel, n, reach), out_sha...]
  transfers between devices with their start and end apart: 22 -> 22, of which waited for: 4 -> 4; matrix products, arithmetic and copies ran while one was open for 19% -> 17% of each run, Pallas kernels for 57% -> 70%
where the time goes in v3:
time: 1290 us
  Pallas kernels  946 us (73%)
  local copies, waits for them, and re-layouts  91.9 us (7%)
  other arithmetic  79.2 us (6%)
  matrix products  79 us (6%)
  waiting for transfers between devices  44.7 us (3%)
  starting transfers between devices  29.3 us (2%)
  between operations  15.9 us (1%)
    pallas_call x2, Pallas kernels, gathered_beside(): pl.pallas_call(functools.partial(gather_beside_kernel, n, reach), out_sha...  206 us
    pallas_call x1, Pallas kernels, gathered_back(): pl.pallas_call(functools.partial(units_back_kernel, n), out_shape=[jax.Sh...  178 us
    pallas_call x1, Pallas kernels, scattered_down(): pl.pallas_call(functools.partial(down_kernel, n), out_shape=jax.ShapeDtyp...  170 us
    pallas_call x1, Pallas kernels, scattered_vision(): pl.pallas_call(functools.partial(vision_kernel, n, chunks, spans, scaling...  130 us
    pallas_call x1, Pallas kernels, gathered_units(): pl.pallas_call(functools.partial(units_kernel, n), out_shape=[jax.ShapeDt...  69.5 us
    pallas_call x1, Pallas kernels, scattered_sum(): pl.pallas_call(functools.partial(scatter_kernel, n, chunks), out_shape=ja...  64.8 us
    pallas_call x3, Pallas kernels, exchanged(): pl.pallas_call(functools.partial(exchange_kernel, n, groups), out_shape=[...  61.7 us
    pallas_call x2, Pallas kernels, reduced(): pl.pallas_call(functools.partial(reduce_kernel, n, combine), out_shape=ja...  51.4 us
  transfers between devices with their start and end apart: 22, of which 4 were waited for; matrix products, arithmetic and copies ran while one was open for 17% of the time, Pallas kernels for 70%

profile of v3, /device:TPU:14, one launch (start us, length us, event | category | flops | bytes accessed | tf_op | source)
XLA Modules:
  0.0 1286.0 jit_solution(15977167968796973314)
XLA Ops:
  17.4 45.9 %shard_map.492 = (bf16[16,128,1152]{2,1,0:T(8,128)(2,1)}, bf16[16,72,256]{2,1,0:T(8,128)(2,1)}) custom-call(bf16[128,1152]{1,0:T(8,128)(2,1)} %copy.341.x_ref, bf16[16,72,256]{2,1,0:T(8,128)(2,1)} %pad_maximum_fusion.4.y_ref), custom_call_target="tpu_custom_call" | custom-call | tf_op jit(solution)/shard_map/pallas_call | solution.py:690
  66.2 3.5 constant_dynamic-slice_fusion.2
  72.4 7.7 all-to-all-start
  101.2 15.1 %shard_map.493 = (bf16[2048,128]{1,0:T(8,128)(2,1)}, f32[2048,1]{1,0:T(8,128)}) custom-call(bf16[2048,128]{1,0:T(8,128)(2,1)} %constant_dynamic-slice_fusion.1.q_ref.refs_2_, bf16[2304,128]{1,0:T(8,128)(2,1)} %get-tuple-element.307.k_ref.refs_3_, bf16[2304,128]{1,0:T(8,128)(2,1)} %get-tuple-element.306.v_ref.refs_4_, s32[2048,1]{1,0:T(8,128)} %copy.344.qid_ref.refs_6_, ...), custom_call_target="tpu_custom_call" | custom-call | flops 2415919104 | bytes 2228224 | tf_op jit(solution)/shard_map/pallas_call | solution.py:1679
  116.2 23.2 %shard_map.494 = bf16[8,256,128]{2,1,0:T(8,128)(2,1)} custom-call(bf16[8,256,128]{2,1,0:T(8,128)(2,1)} %bitcast.303), custom_call_target="tpu_custom_call" | custom-call | tf_op jit(solution)/shard_map/pallas_call | solution.py:1412
  144.1 159.8 %shard_map.495 = (bf16[16,72,4928]{2,1,0:T(8,128)(2,1)}, bf16[16,448,256]{2,1,0:T(8,128)(2,1)}) custom-call(bf16[72,4928]{1,0:T(8,128)(2,1)} %fusion.127.x_ref, bf16[16,448,256]{2,1,0:T(8,128)(2,1)} %bitcast.275), custom_call_target="tpu_custom_call" | custom-call | tf_op jit(solution)/shard_map/pallas_call | solution.py:690
  309.9 6.5 multiply_convert_fusion
  316.4 5.6 fusion.205
  324.7 4.9 convolution_convert_fusion.1
  336.6 4.1 fusion.34
  340.7 69.5 %shard_map.496 = (bf16[16,128,1152]{2,1,0:T(8,128)(2,1)}, f32[16,128,1024]{2,1,0:T(8,128)}, f32[16,128,1024]{2,1,0:T(8,128)}, bf16[16,128,1024]{2,1,0:T(8,128)(2,1)}) custom-call(bf16[128,1152]{1,0:T(8,128)(2,1)} %copy.352.x_ref, bf16[1152,1024]{1,0:T(8,128)(2,1)} %get-tuple-element.303.w_gate_ref, bf16[1152,1024]{1,0:T(8,128)(2,1)} %get-tuple-element.302.w_up_ref), custom_call_target="tpu_custom_call" | custom-call | tf_op jit(solution)/shard_map/pallas_call | solution.py:784
  410.2 170.2 %shard_map.497 = bf16[16,128,256]{2,1,0:T(8,128)(2,1)} custom-call(bf16[16,128,1024]{2,1,0:T(8,128)(2,1)} %get-tuple-element.81.hidden_ref, bf16[16,448,256]{2,1,0:T(8,128)(2,1)} %get-tuple-element.82.mine_ref.down_mine_ref, bf16[16,448,256]{2,1,0:T(8,128)(2,1)} %collective-permute-done.4.other_ref.down_other_ref), custom_call_target="tpu_custom_call" | custom-call | tf_op jit(solution)/shard_map/pallas_call | solution.py:1250
  601.2 28.9 %shard_map.498 = f32[16,32,128]{2,1,0:T(8,128)} custom-call(f32[16,32,128]{2,1,0:T(8,128)} %select_maximum_fusion.2.x_ref), custom_call_target="tpu_custom_call" | custom-call | tf_op jit(solution)/shard_map/pallas_call | solution.py:1460
  652.7 3.6 fusion.46
  659.4 177.7 %shard_map.499 = (bf16[16,128,4096]{2,1,0:T(8,128)(2,1)}, bf16[9,16,128,128]{3,2,1,0:T(8,128)(2,1)}, bf16[16,2,72,512]{3,2,1,0:T(8,128)(2,1)}, bf16[16,2,72,512]...) custom-call(bf16[128,4096]{1,0:T(8,128)(2,1)} %add_add_fusion.x_ref, ...), custom_call_target="tpu_custom_call" | custom-call | tf_op jit(solution)/shard_map/pallas_call | solution.py:986
  837.1 64.8 %shard_map.500 = bf16[9,128,128]{2,1,0:T(8,128)(2,1)} custom-call(bf16[9,16,128,128]{3,2,1,0:T(8,128)(2,1)} %get-tuple-element.88.p_ref), custom_call_target="tpu_custom_call" | custom-call | tf_op jit(solution)/shard_map/pallas_call | solution.py:1216
  907.3 6.8 convert_reduce_fusion.1
  914.1 4.3 fusion.208
  931.7 15.6 %shard_map.501 = bf16[8,256,128]{2,1,0:T(8,128)(2,1)} custom-call(bf16[8,256,128]{2,1,0:T(8,128)(2,1)} %pad.102.refs_0_), custom_call_target="tpu_custom_call" | custom-call | tf_op jit(solution)/shard_map/pallas_call | solution.py:1412
  949.8 130.0 %shard_map.502 = (bf16[13,72,384]{2,1,0:T(8,128)(2,1)}, f32[2048,128]{1,0:T(8,128)}, f32[2304,128]{1,0:T(8,128)}, f32[2304,128]{1,0:T(8,128)}) custom-call(bf16[3,1152,256]{2,1,0:T(8,128)(2,1)} %pad_maximum_fusion.3.refs_0_, bf16[256,4992]{1,0:T(8,128)(2,1)} %fusion.29.refs_1_, bf16[2048,128]{1,0:T(8,128)(2,1)} %constant_dynamic-slice_fusion.1.q_ref.refs_2_, ...), custom_call_target="tpu_custom_call" | custom-call | tf_op jit(solution)/shard_map/pallas_call | solution.py:1358
  1087.9 6.0 collective-permute-done.9
  1096.8 22.9 %shard_map.503 = (bf16[16,72,256]{2,1,0:T(8,128)(2,1)}, bf16[8,256,256]{2,1,0:T(8,128)(2,1)}) custom-call(bf16[16,72,256]{2,1,0:T(8,128)(2,1)} %bitcast.301, bf16[8,256,256]{2,1,0:T(8,128)(2,1)} %add_convert_fusion.3.refs_1_), custom_call_target="tpu_custom_call" | custom-call | tf_op jit(solution)/shard_map/pallas_call | solution.py:1412
  1119.7 4.5 add_convert_fusion.2
  1124.2 8.2 all-to-all-start.1
  1139.8 4.4 fusion.209
  1147.6 6.2 add_convert_fusion
  1161.0 22.5 %shard_map.504 = f32[16,40,128]{2,1,0:T(8,128)} custom-call(f32[16,40,128]{2,1,0:T(8,128)} %bitcast.283), custom_call_target="tpu_custom_call" | custom-call | tf_op jit(solution)/shard_map/pallas_call | solution.py:1460
  1183.5 8.1 all-to-all-start.2
  1203.9 3.4 unstack.29
  1210.6 4.9 fusion.214
  1238.8 34.8 %all-to-all-done.2 = bf16[16,448,256]{2,1,0:T(8,128)(2,1)} async-done(((bf16[16,448,256]{2,1,0:T(8,128)(2,1)}), bf16[16,448,256]{2,1,0:T(8,128)(2,1)}, u32[]{:S(2)}, u32[]{:S(2)}) %all-to-all-start.2) | async-done | bytes 3670048 | tf_op jit(solution)/shard_map/all_to_all | solution.py:1931
  1273.6 5.7 bitcast_convert_fusion
  (478 shorter events, 191.1 us)
Async XLA Ops:
  69.7 21.9 %collective-permute-start = (bf16[9,128,1152]{2,1,0:T(8,128)(2,1)}, bf16[9,128,1152]{2,1,0:T(8,128)(2,1)}, u32[]{:S(2)}, u32[]{:S(2)}) collective-permute-start(bf16[9,128,1152]{2,1,0:T(8,128)(2,1)} %constant_dynamic-slice_fusion.2), channel_id=1, source_target_pairs={{0,1},{1,0},{2,3},{3,2},{4,5},{5,4},{6,7},{7,6},{8,9},{9,8},{10,11... | collective-permute-start | bytes 7962632 | tf_op jit(solution)/shard_map/ppermute | solution.py:1487
  72.4 71.7 %all-to-all-start = ((bf16[16,2,72,512]{3,2,1,0:T(8,128)(2,1)}), bf16[16,2,72,512]{3,2,1,0:T(8,128)(2,1)S(1)}, u32[]{:S(2)}, u32[]{:S(2)}) async-start(bf16[16,2,72,512]{3,2,1,0:T(8,128)(2,1)} %copy.342), calls=%async_computation | async-start | bytes 4718592 | tf_op jit(solution)/shard_map/all_to_all | solution.py:1654
  80.1 501.7 %all-gather.3.cloned.1.call-start = ((), (), s32[]{:S(2)}) async-start(), calls=%async_computation.4 | async-start | bytes 3342336 | tf_op jit(solution)/shard_map/all_gather | solution.py:1652
  80.8 1059.0 %all-gather.5.cloned.1.call-start = ((), (), s32[]{:S(2)}) async-start(), calls=%async_computation.5 | async-start | bytes 4386816 | tf_op jit(solution)/shard_map/all_gather | solution.py:1726
  144.1 159.9 %copy-start.36 = (bf16[256,8,72]{0,2,1:T(8,128)(2,1)S(1)}, bf16[256,8,72]{0,2,1:T(8,128)(2,1)}, u32[]{:S(2)}) copy-start(bf16[256,8,72]{0,2,1:T(8,128)(2,1)} %copy.345) | copy-start | bytes 884740
  306.1 3.1 collective-permute-start.1
  306.9 277.0 %copy-start.13 = (bf16[64,4096]{1,0:T(8,128)(2,1)}, bf16[64,4096]{1,0:T(8,128)(2,1)S(1)}, u32[]{:S(2)}) copy-start(bf16[64,4096]{1,0:T(8,128)(2,1)S(1)} %multiply_convert_fusion.1) | copy-start | bytes 1572868
  308.7 27.9 %collective-permute-start.3 = (bf16[2,1152,512]{2,1,0:T(8,128)(2,1)}, bf16[2,1152,512]{2,1,0:T(8,128)(2,1)}, u32[]{:S(2)}, u32[]{:S(2)}) collective-permute-start(bf16[2,1152,512]{2,1,0:T(8,128)(2,1)} %bitcast.21), channel_id=1, source_target_pairs={{0,1},{1,0},{2,3},{3,2},{4,5},{5,4},{6,7},{7,6},{8,9},{9,8},{10,11... | collective-permute-start | bytes 7077896 | tf_op jit(solution)/shard_map/ppermute | solution.py:1487
  309.2 101.0 %collective-permute-start.4 = (bf16[16,448,256]{2,1,0:T(8,128)(2,1)}, bf16[16,448,256]{2,1,0:T(8,128)(2,1)}, u32[]{:S(2)}, u32[]{:S(2)}) collective-permute-start(bf16[16,448,256]{2,1,0:T(8,128)(2,1)} %get-tuple-element.82.mine_ref.down_mine_ref), channel_id=1, source_target_pairs={{0,1},{1,0},{2,3},{3,2},{4,5},{5,4},{6,7},{7,6},{8,9},{9,8},{10,11... | collective-permute-start | bytes 11010056 | tf_op jit(solution)/shard_map/ppermute | solution.py:1487
  322.1 11.9 collective-permute-start.2
  324.7 262.0 %copy-start.31 = (bf16[64,2,4,96]{3,2,1,0:T(4,128)(2,1)}, bf16[64,2,4,96]{3,2,1,0:T(4,128)(2,1)S(1)}, u32[]{:S(2)}) copy-start(bf16[64,2,4,96]{3,2,1,0:T(4,128)(2,1)S(1)} %reshape.403) | copy-start | bytes 294916
  581.7 8.2 collective-permute-start.5
  587.8 606.0 %reduce-scatter.2.cloned.1.call-start = ((), (), s32[]{:S(2)}) async-start(), calls=%async_computation.6 | async-start | bytes 3342336 | tf_op jit(solution)/shard_map/reduce_scatter | solution.py:1803
  599.2 36.6 %copy-start.19 = (bf16[64,2,4,96]{3,2,1,0:T(4,128)(2,1)S(1)}, bf16[64,2,4,96]{3,2,1,0:T(4,128)(2,1)}, u32[]{:S(2)}) copy-start(bf16[64,2,4,96]{3,2,1,0:T(4,128)(2,1)} %reshape.408) | copy-start | bytes 294916
  645.6 7.1 collective-permute-start.6
  837.1 66.1 %copy-start.28 = (bf16[2,4,64,256]{3,2,1,0:T(8,128)(2,1)S(1)}, bf16[2,4,64,256]{3,2,1,0:T(8,128)(2,1)}, u32[]{:S(2)}) copy-start(bf16[2,4,64,256]{3,2,1,0:T(8,128)(2,1)} %copy-done.27) | copy-start | bytes 786436
  837.1 66.1 %copy-start.58 = (bf16[256,192]{0,1:T(8,128)(2,1)S(1)}, bf16[256,192]{0,1:T(8,128)(2,1)}, u32[]{:S(2)}) copy-start(bf16[256,192]{0,1:T(8,128)(2,1)} %copy-done.57) | copy-start | bytes 294916
  903.2 3.1 collective-permute-start.7
  905.7 241.9 %collective-permute-start.12 = (bf16[16,448,256]{2,1,0:T(8,128)(2,1)}, bf16[16,448,256]{2,1,0:T(8,128)(2,1)}, u32[]{:S(2)}, u32[]{:S(2)}) collective-permute-start(bf16[16,448,256]{2,1,0:T(8,128)(2,1)} %get-tuple-element.100), channel_id=1, source_target_pairs={{0,1},{1,0},{2,3},{3,2},{4,5},{5,4},{6,7},{7,6},{8,9},{9,8},{10,11... | collective-permute-start | bytes 11010056 | tf_op jit(solution)/shard_map/ppermute | solution.py:1487
  906.2 213.5 %collective-permute-start.10 = (bf16[16,2,72,512]{3,2,1,0:T(8,128)(2,1)}, bf16[16,2,72,512]{3,2,1,0:T(8,128)(2,1)}, u32[]{:S(2)}, u32[]{:S(2)}) collective-permute-start(bf16[16,2,72,512]{3,2,1,0:T(8,128)(2,1)} %get-tuple-element.96), channel_id=1, source_target_pairs={{0,1},{1,0},{2,3},{3,2},{4,5},{5,4},{6,7},{7,6},{8,9},{9,8},{10,11... | collective-permute-start | bytes 7077896 | tf_op jit(solution)/shard_map/ppermute | solution.py:1487
  906.3 16.9 %copy-start.20 = (bf16[128,1152]{0,1:T(8,128)(2,1)}, bf16[128,1152]{0,1:T(8,128)(2,1)S(1)}, u32[]{:S(2)}) copy-start(bf16[128,1152]{0,1:T(8,128)(2,1)S(1)} %get-tuple-element.323) | copy-start | bytes 884740
  918.4 2.1 collective-permute-start.8
  927.7 19.6 %copy-start.26 = (bf16[1,1152,256]{2,1,0:T(8,128)(2,1)S(1)}, bf16[1,1152,256]{2,1,0:T(8,128)(2,1)}, u32[]{:S(2)}) copy-start(bf16[1,1152,256]{2,1,0:T(8,128)(2,1)} %get-tuple-element.311) | copy-start | bytes 1769476
  949.7 135.6 %slice-start.4 = ((s8[5308416]{0:T(1024)(128)(4,1)}), s8[1114112]{0:T(1024)(128)(4,1)S(1)}, s32[]{:S(2)}) async-start(s8[5308416]{0:T(1024)(128)(4,1)} %bitcast.271), calls=%async_computation.11 | async-start | bytes 2228224
  1082.8 11.1 collective-permute-start.9
  1087.9 31.8 %copy-start.82 = (f32[8,256]{1,0:T(8,128)}, f32[8,256]{1,0:T(8,128)S(1)}, u32[]{:S(2)}) copy-start(f32[8,256]{1,0:T(8,128)S(1)} %dynamic_update_slice.7) | copy-start | bytes 24580
  1124.2 59.2 %all-to-all-start.1 = ((bf16[16,144,512]{2,1,0:T(8,128)(2,1)}), bf16[16,144,512]{2,1,0:T(8,128)(2,1)}, u32[]{:S(2)}, u32[]{:S(2)}) async-start(bf16[16,144,512]{2,1,0:T(8,128)(2,1)} %bitcast.264), calls=%async_computation.1 | async-start | bytes 4718592 | tf_op jit(solution)/shard_map/all_to_all | solution.py:1888
  1144.2 9.6 collective-permute-start.11
  1183.5 90.1 %all-to-all-start.2 = ((bf16[16,448,256]{2,1,0:T(8,128)(2,1)}), bf16[16,448,256]{2,1,0:T(8,128)(2,1)}, u32[]{:S(2)}, u32[]{:S(2)}) async-start(bf16[16,448,256]{2,1,0:T(8,128)(2,1)} %add_convert_fusion), calls=%async_computation.2 | async-start | bytes 7340032 | tf_op jit(solution)/shard_map/all_to_all | solution.py:1931
  1197.7 34.5 %collective-permute-start.15 = (f32[4096]{0:T(1024)}, f32[4096]{0:T(1024)}, u32[]{:S(2)}, u32[]{:S(2)}) collective-permute-start(f32[4096]{0:T(1024)} %slice.191), channel_id=1, source_target_pairs={{0,1},{1,0},{2,3},{3,2},{4,5},{5,4},{6,7},{7,6},{8,9},{9,8},{10,11... | collective-permute-start | bytes 49160 | tf_op jit(solution)/shard_map/ppermute | solution.py:1487
  1217.4 16.1 %collective-permute-start.14 = (bf16[64,4096]{1,0:T(8,128)(2,1)}, bf16[64,4096]{1,0:T(8,128)(2,1)}, u32[]{:S(2)}, u32[]{:S(2)}) collective-permute-start(bf16[64,4096]{1,0:T(8,128)(2,1)} %get-tuple-element.361), channel_id=1, source_target_pairs={{0,1},{1,0},{2,3},{3,2},{4,5},{5,4},{6,7},{7,6},{8,9},{9,8},{10,11... | collective-permute-start | bytes 1572872 | tf_op jit(solution)/shard_map/ppermute | solution.py:1487
  1220.3 15.2 %collective-permute-start.13 = (bf16[64,4096]{1,0:T(8,128)(2,1)}, bf16[64,4096]{1,0:T(8,128)(2,1)}, u32[]{:S(2)}, u32[]{:S(2)}) collective-permute-start(bf16[64,4096]{1,0:T(8,128)(2,1)} %get-tuple-element.363), channel_id=1, source_target_pairs={{0,1},{1,0},{2,3},{3,2},{4,5},{5,4},{6,7},{7,6},{8,9},{9,8},{10,11... | collective-permute-start | bytes 1572872 | tf_op jit(solution)/shard_map/ppermute | solution.py:1487
  (112 other events, 429.9 us)
Sparse Core Ops, SparseCore 0:
  84.2 121.9 all-gather.2
  587.9 80.5 all-gather.4
  906.4 142.0 reduce-scatter.1

commit v4 on v3

--- a/solution.py
+++ b/solution.py
@@ -1646,11 +1646,9 @@
     unit_weights = jnp.pad(unit_weights, ((0, 0),) * 3 + ((0, unit_lanes - proj_units),))
     ctx_width = rk_weight.shape[1]
     ctx_shard = jnp.concatenate([rk_weight, rv_weight], axis=1)
-    unit_weights, normed_half, head_weight, ctx_shard = lax.optimization_barrier(
-        (unit_weights.transpose(2, 0, 1, 3), normed_half, head_weight, ctx_shard)
-    )
-    w_ctx = lax.all_gather(ctx_shard, "seq", axis=0, tiled=True)
-    w_ctxkey, w_ctxval = w_ctx[:, :ctx_width], w_ctx[:, ctx_width:]
+    unit_weights, normed_half, head_weight = lax.optimization_barrier(
+        (unit_weights.transpose(2, 0, 1, 3), normed_half, head_weight)
+    )
     unit_weights = lax.all_to_all(unit_weights, "seq", 0, 0)
     normed_half = lax.dynamic_slice_in_dim(normed_half, window_start // rows, window // rows, 0)
     normed_window = in_order(
@@ -1693,7 +1691,9 @@
         (unit_weights, vision_shard, attended_low, down_proj)
     )
     vision, down_mine = gathered_beside(vision_shard, down_proj.reshape(n, proj_units, -1), 17)
-    vision = vision.reshape(width, -1)
+    vision, ctx_shard = lax.optimization_barrier((vision.reshape(width, -1), ctx_shard))
+    w_ctx = lax.all_gather(ctx_shard, "seq", axis=0, tiled=True)
+    w_ctxkey, w_ctxval = w_ctx[:, :ctx_width], w_ctx[:, ctx_width:]
     down_other = swapped(down_mine)
     w_up = vision[:, :hidden_units]
     w_down_t = vision[:, hidden_pad : hidden_pad + hidden_units]
@@ -1815,6 +1815,7 @@
     )
 
     query_part = ctx_query_term + first_block * self_query_term
+    r_grad, feat_terms = lax.optimization_barrier((r_grad, feat_terms))
     feat_half = joined_chunks(scattered_sum(feat_terms, 11))
 
     proj_in_grad = in_order(feat_half, swapped(feat_half), 0).astype(jnp.float32)

time: 1290 us -> 1290 us (level)
  waiting for transfers between devices: 44.7 us -> 27.1 us
    pallas_call x1, Pallas kernels: 178 us -> 194 us  [gathered_back(): pl.pallas_call(functools.partial(units_back_kernel, n), out_shape=[jax.Sh...]
  transfers between devices with their start and end apart: 22 -> 22, of which waited for: 4 -> 6; matrix products, arithmetic and copies ran while one was open for 17% -> 15% of each run, Pallas kernels for 70% -> 56%
where the time goes in v4:
time: 1290 us; the launch traced here: 1280 us
  Pallas kernels  945 us (73%)
  local copies, waits for them, and re-layouts  99.5 us (8%)
  matrix products  84.1 us (7%)
  other arithmetic  79.6 us (6%)
  starting transfers between devices  31.3 us (2%)
  waiting for transfers between devices  27.1 us (2%)
  between operations  16 us (1%)
    pallas_call x2, Pallas kernels, gathered_beside(): pl.pallas_call(functools.partial(gather_beside_kernel, n, reach), out_sha...  206 us
    pallas_call x1, Pallas kernels, gathered_back(): pl.pallas_call(functools.partial(units_back_kernel, n), out_shape=[jax.Sh...  194 us
    pallas_call x1, Pallas kernels, scattered_down(): pl.pallas_call(functools.partial(down_kernel, n), out_shape=jax.ShapeDtyp...  176 us
    pallas_call x1, Pallas kernels, scattered_vision(): pl.pallas_call(functools.partial(vision_kernel, n, chunks, spans, scaling...  118 us
    pallas_call x1, Pallas kernels, scattered_sum(): pl.pallas_call(functools.partial(scatter_kernel, n, chunks), out_shape=ja...  68.3 us
    pallas_call x1, Pallas kernels, gathered_units(): pl.pallas_call(functools.partial(units_kernel, n), out_shape=[jax.ShapeDt...  61.6 us
    pallas_call x2, Pallas kernels, reduced(): pl.pallas_call(functools.partial(reduce_kernel, n, combine), out_shape=ja...  53.8 us
    pallas_call x3, Pallas kernels, exchanged(): pl.pallas_call(functools.partial(exchange_kernel, n, groups), out_shape=[...  53.5 us
  transfers between devices with their start and end apart: 22, of which 6 were waited for; matrix products, arithmetic and copies ran while one was open for 15% of the time, Pallas kernels for 56%

profile of v4, /device:TPU:14, one launch (start us, length us, event | category | flops | bytes accessed | tf_op | source)
XLA Modules:
  0.0 1282.3 jit_solution(11237209692536794983)
XLA Ops:
  17.5 45.9 %shard_map.492 = (bf16[16,128,1152]{2,1,0:T(8,128)(2,1)}, bf16[16,72,256]{2,1,0:T(8,128)(2,1)}) custom-call(bf16[128,1152]{1,0:T(8,128)(2,1)} %copy.341.x_ref, bf16[16,72,256]{2,1,0:T(8,128)(2,1)} %pad_maximum_fusion.4.y_ref), custom_call_target="tpu_custom_call" | custom-call | tf_op jit(solution)/shard_map/pallas_call | solution.py:690
  65.5 3.5 constant_dynamic-slice_fusion.2
  71.7 7.7 all-to-all-start
  100.5 14.5 %shard_map.493 = (bf16[2048,128]{1,0:T(8,128)(2,1)}, f32[2048,1]{1,0:T(8,128)}) custom-call(bf16[2048,128]{1,0:T(8,128)(2,1)} %constant_dynamic-slice_fusion.1.q_ref.refs_2_, bf16[2304,128]{1,0:T(8,128)(2,1)} %get-tuple-element.313.k_ref.refs_3_, bf16[2304,128]{1,0:T(8,128)(2,1)} %get-tuple-element.312.v_ref.refs_4_, s32[2048,1]{1,0:T(8,128)} %copy.344.qid_ref.refs_6_, ...), custom_call_target="tpu_custom_call" | custom-call | flops 2415919104 | bytes 2228224 | tf_op jit(solution)/shard_map/pallas_call | solution.py:1677
  115.0 16.5 %shard_map.494 = bf16[8,256,128]{2,1,0:T(8,128)(2,1)} custom-call(bf16[8,256,128]{2,1,0:T(8,128)(2,1)} %bitcast.299), custom_call_target="tpu_custom_call" | custom-call | tf_op jit(solution)/shard_map/pallas_call | solution.py:1412
  136.6 160.0 %shard_map.495 = (bf16[16,72,4928]{2,1,0:T(8,128)(2,1)}, bf16[16,448,256]{2,1,0:T(8,128)(2,1)}) custom-call(bf16[72,4928]{1,0:T(8,128)(2,1)} %fusion.127.x_ref, bf16[16,448,256]{2,1,0:T(8,128)(2,1)} %bitcast.271), custom_call_target="tpu_custom_call" | custom-call | tf_op jit(solution)/shard_map/pallas_call | solution.py:690
  304.6 6.1 multiply_convert_fusion
  310.7 4.5 fusion.205
  318.6 4.2 fusion.34
  322.7 61.6 %shard_map.496 = (bf16[16,128,1152]{2,1,0:T(8,128)(2,1)}, f32[16,128,1024]{2,1,0:T(8,128)}, f32[16,128,1024]{2,1,0:T(8,128)}, bf16[16,128,1024]{2,1,0:T(8,128)(2,1)}) custom-call(bf16[128,1152]{1,0:T(8,128)(2,1)} %copy.352.x_ref, bf16[1152,1024]{1,0:T(8,128)(2,1)} %get-tuple-element.309.w_gate_ref, bf16[1152,1024]{1,0:T(8,128)(2,1)} %get-tuple-element.308.w_up_ref), custom_call_target="tpu_custom_call" | custom-call | tf_op jit(solution)/shard_map/pallas_call | solution.py:784
  384.4 175.6 %shard_map.497 = bf16[16,128,256]{2,1,0:T(8,128)(2,1)} custom-call(bf16[16,128,1024]{2,1,0:T(8,128)(2,1)} %get-tuple-element.85.hidden_ref, bf16[16,448,256]{2,1,0:T(8,128)(2,1)} %get-tuple-element.86.mine_ref.down_mine_ref, bf16[16,448,256]{2,1,0:T(8,128)(2,1)} %collective-permute-done.4.other_ref.down_other_ref), custom_call_target="tpu_custom_call" | custom-call | tf_op jit(solution)/shard_map/pallas_call | solution.py:1250
  561.3 4.0 convolution_convert_fusion.2
  566.1 5.0 convolution_convert_fusion.1
  588.9 22.2 %shard_map.498 = f32[16,32,128]{2,1,0:T(8,128)} custom-call(f32[16,32,128]{2,1,0:T(8,128)} %select_maximum_fusion.2.x_ref), custom_call_target="tpu_custom_call" | custom-call | tf_op jit(solution)/shard_map/pallas_call | solution.py:1460
  641.4 3.6 fusion.46
  648.0 193.7 %shard_map.499 = (bf16[16,128,4096]{2,1,0:T(8,128)(2,1)}, bf16[9,16,128,128]{3,2,1,0:T(8,128)(2,1)}, bf16[16,2,72,512]{3,2,1,0:T(8,128)(2,1)}, bf16[16,2,72,512]...) custom-call(bf16[128,4096]{1,0:T(8,128)(2,1)} %add_add_fusion.x_ref, ...), custom_call_target="tpu_custom_call" | custom-call | tf_op jit(solution)/shard_map/pallas_call | solution.py:986
  851.3 68.3 %shard_map.500 = bf16[9,128,128]{2,1,0:T(8,128)(2,1)} custom-call(bf16[9,16,128,128]{3,2,1,0:T(8,128)(2,1)} %get-tuple-element.94.p_ref), custom_call_target="tpu_custom_call" | custom-call | tf_op jit(solution)/shard_map/pallas_call | solution.py:1216
  920.8 4.0 collective-permute-start.7
  924.7 4.7 add_convert_fusion.2
  929.5 6.3 convert_reduce_fusion.1
  949.3 14.0 %shard_map.501 = bf16[8,256,128]{2,1,0:T(8,128)(2,1)} custom-call(bf16[8,256,128]{2,1,0:T(8,128)(2,1)} %pad.102.refs_0_), custom_call_target="tpu_custom_call" | custom-call | tf_op jit(solution)/shard_map/pallas_call | solution.py:1412
  965.8 117.8 %shard_map.502 = (bf16[13,72,384]{2,1,0:T(8,128)(2,1)}, f32[2048,128]{1,0:T(8,128)}, f32[2304,128]{1,0:T(8,128)}, f32[2304,128]{1,0:T(8,128)}) custom-call(bf16[3,1152,256]{2,1,0:T(8,128)(2,1)} %pad_maximum_fusion.3.refs_0_, bf16[256,4992]{1,0:T(8,128)(2,1)} %fusion.29.refs_1_, bf16[2048,128]{1,0:T(8,128)(2,1)} %constant_dynamic-slice_fusion.1.q_ref.refs_2_, ...), custom_call_target="tpu_custom_call" | custom-call | tf_op jit(solution)/shard_map/pallas_call | solution.py:1358
  1089.9 4.9 convolution_convert_fusion
  1096.3 23.1 %shard_map.503 = (bf16[16,72,256]{2,1,0:T(8,128)(2,1)}, bf16[8,256,256]{2,1,0:T(8,128)(2,1)}) custom-call(bf16[16,72,256]{2,1,0:T(8,128)(2,1)} %bitcast.297, bf16[8,256,256]{2,1,0:T(8,128)(2,1)} %add_convert_fusion.3.refs_1_), custom_call_target="tpu_custom_call" | custom-call | tf_op jit(solution)/shard_map/pallas_call | solution.py:1412
  1119.4 5.4 all-to-all-start.1
  1132.2 4.6 fusion.209
  1136.8 5.0 add_convert_fusion
  1155.0 31.5 %shard_map.504 = f32[16,40,128]{2,1,0:T(8,128)} custom-call(f32[16,40,128]{2,1,0:T(8,128)} %bitcast.279), custom_call_target="tpu_custom_call" | custom-call | tf_op jit(solution)/shard_map/pallas_call | solution.py:1460
  1186.6 9.0 all-to-all-start.2
  1215.4 4.9 fusion.214
  1247.0 22.8 %all-to-all-done.2 = bf16[16,448,256]{2,1,0:T(8,128)(2,1)} async-done(((bf16[16,448,256]{2,1,0:T(8,128)(2,1)}), bf16[16,448,256]{2,1,0:T(8,128)(2,1)}, u32[]{:S(2)}, u32[]{:S(2)}) %all-to-all-start.2) | async-done | bytes 3670048 | tf_op jit(solution)/shard_map/all_to_all | solution.py:1932
  1269.9 5.7 bitcast_convert_fusion
  (460 shorter events, 205.8 us)
Async XLA Ops:
  69.0 22.1 %collective-permute-start = (bf16[9,128,1152]{2,1,0:T(8,128)(2,1)}, bf16[9,128,1152]{2,1,0:T(8,128)(2,1)}, u32[]{:S(2)}, u32[]{:S(2)}) collective-permute-start(bf16[9,128,1152]{2,1,0:T(8,128)(2,1)} %constant_dynamic-slice_fusion.2), channel_id=1, source_target_pairs={{0,1},{1,0},{2,3},{3,2},{4,5},{5,4},{6,7},{7,6},{8,9},{9,8},{10,11... | collective-permute-start | bytes 7962632 | tf_op jit(solution)/shard_map/ppermute | solution.py:1487
  71.7 16.4 %copy-start.31 = (bf16[16,72,256]{2,1,0:T(8,128)(2,1)S(1)}, bf16[16,72,256]{2,1,0:T(8,128)(2,1)}, u32[]{:S(2)}) copy-start(bf16[16,72,256]{2,1,0:T(8,128)(2,1)} %get-tuple-element.77) | copy-start | bytes 1769476
  71.7 63.5 %all-to-all-start = ((bf16[16,2,72,512]{3,2,1,0:T(8,128)(2,1)}), bf16[16,2,72,512]{3,2,1,0:T(8,128)(2,1)S(1)}, u32[]{:S(2)}, u32[]{:S(2)}) async-start(bf16[16,2,72,512]{3,2,1,0:T(8,128)(2,1)} %copy.342), calls=%async_computation | async-start | bytes 4718592 | tf_op jit(solution)/shard_map/all_to_all | solution.py:1652
  79.4 496.9 %all-gather.3.cloned.1.call-start = ((), (), s32[]{:S(2)}) async-start(), calls=%async_computation.4 | async-start | bytes 3342336 | tf_op jit(solution)/shard_map/all_gather | solution.py:1695
  136.6 160.1 %copy-start.33 = (bf16[256,8,72]{0,2,1:T(8,128)(2,1)S(1)}, bf16[256,8,72]{0,2,1:T(8,128)(2,1)}, u32[]{:S(2)}) copy-start(bf16[256,8,72]{0,2,1:T(8,128)(2,1)} %copy.345) | copy-start | bytes 884740
  298.8 3.0 collective-permute-start.1
  299.1 16.4 %copy-start.97 = (f32[64]{0:T(128)}, f32[64]{0:T(128)S(1)}, u32[]{:S(2)}) copy-start(f32[64]{0:T(128)S(1)} %fusion.177) | copy-start | bytes 772
  300.7 17.8 %collective-permute-start.3 = (bf16[2,1152,512]{2,1,0:T(8,128)(2,1)}, bf16[2,1152,512]{2,1,0:T(8,128)(2,1)}, u32[]{:S(2)}, u32[]{:S(2)}) collective-permute-start(bf16[2,1152,512]{2,1,0:T(8,128)(2,1)} %bitcast.21), channel_id=1, source_target_pairs={{0,1},{1,0},{2,3},{3,2},{4,5},{5,4},{6,7},{7,6},{8,9},{9,8},{10,11... | collective-permute-start | bytes 7077896 | tf_op jit(solution)/shard_map/ppermute | solution.py:1487
  301.2 83.1 %collective-permute-start.4 = (bf16[16,448,256]{2,1,0:T(8,128)(2,1)}, bf16[16,448,256]{2,1,0:T(8,128)(2,1)}, u32[]{:S(2)}, u32[]{:S(2)}) collective-permute-start(bf16[16,448,256]{2,1,0:T(8,128)(2,1)} %get-tuple-element.86.mine_ref.down_mine_ref), channel_id=1, source_target_pairs={{0,1},{1,0},{2,3},{3,2},{4,5},{5,4},{6,7},{7,6},{8,9},{9,8},{10,11... | collective-permute-start | bytes 11010056 | tf_op jit(solution)/shard_map/ppermute | solution.py:1487
  301.4 548.3 %reduce-scatter.2.cloned.1.call-start = ((), (), s32[]{:S(2)}) async-start(), calls=%async_computation.5 | async-start | bytes 3342336 | tf_op jit(solution)/shard_map/reduce_scatter | solution.py:1803
  315.3 2.1 collective-permute-start.2
  315.7 245.6 %copy-start.11 = (bf16[64,4096]{1,0:T(8,128)(2,1)}, bf16[64,4096]{1,0:T(8,128)(2,1)S(1)}, u32[]{:S(2)}) copy-start(bf16[64,4096]{1,0:T(8,128)(2,1)S(1)} %multiply_convert_fusion.1) | copy-start | bytes 1572868
  561.3 12.1 collective-permute-start.5
  635.0 6.4 collective-permute-start.6
  648.0 484.3 %all-gather.5.cloned.1.call-start = ((), (), s32[]{:S(2)}) async-start(), calls=%async_computation.6 | async-start | bytes 4386816 | tf_op jit(solution)/shard_map/all_gather | solution.py:1726
  648.0 193.9 %copy-start.55 = (bf16[72,576]{1,0:T(8,128)(2,1)S(1)}, bf16[72,576]{1,0:T(8,128)(2,1)}, u32[]{:S(2)}) copy-start(bf16[72,576]{1,0:T(8,128)(2,1)} %param.36) | copy-start | bytes 248836
  648.0 193.9 %copy-start.57 = (bf16[72,576]{1,0:T(8,128)(2,1)S(1)}, bf16[72,576]{1,0:T(8,128)(2,1)}, u32[]{:S(2)}) copy-start(bf16[72,576]{1,0:T(8,128)(2,1)} %param.35) | copy-start | bytes 248836
  648.0 193.9 %copy-start.59 = (bf16[72,576]{1,0:T(8,128)(2,1)S(1)}, bf16[72,576]{1,0:T(8,128)(2,1)}, u32[]{:S(2)}) copy-start(bf16[72,576]{1,0:T(8,128)(2,1)} %param.33) | copy-start | bytes 248836
  841.8 82.9 %collective-permute-start.10 = (bf16[16,2,72,512]{3,2,1,0:T(8,128)(2,1)}, bf16[16,2,72,512]{3,2,1,0:T(8,128)(2,1)}, u32[]{:S(2)}, u32[]{:S(2)}) collective-permute-start(bf16[16,2,72,512]{3,2,1,0:T(8,128)(2,1)} %get-tuple-element.102), channel_id=1, source_target_pairs={{0,1},{1,0},{2,3},{3,2},{4,5},{5,4},{6,7},{7,6},{8,9},{9,8},{10,11... | collective-permute-start | bytes 7077896 | tf_op jit(solution)/shard_map/ppermute | solution.py:1487
  849.1 287.7 %collective-permute-start.12 = (bf16[16,448,256]{2,1,0:T(8,128)(2,1)}, bf16[16,448,256]{2,1,0:T(8,128)(2,1)}, u32[]{:S(2)}, u32[]{:S(2)}) collective-permute-start(bf16[16,448,256]{2,1,0:T(8,128)(2,1)} %get-tuple-element.106), channel_id=1, source_target_pairs={{0,1},{1,0},{2,3},{3,2},{4,5},{5,4},{6,7},{7,6},{8,9},{9,8},{10,11... | collective-permute-start | bytes 11010056 | tf_op jit(solution)/shard_map/ppermute | solution.py:1487
  920.8 8.7 collective-permute-start.7
  929.5 12.8 copy-start.18
  937.5 2.1 collective-permute-start.8
  945.4 18.0 %copy-start.24 = (bf16[1,1152,256]{2,1,0:T(8,128)(2,1)S(1)}, bf16[1,1152,256]{2,1,0:T(8,128)(2,1)}, u32[]{:S(2)}) copy-start(bf16[1,1152,256]{2,1,0:T(8,128)(2,1)} %get-tuple-element.317) | copy-start | bytes 1769476
  1087.3 7.7 collective-permute-start.9
  1119.4 67.2 %all-to-all-start.1 = ((bf16[16,144,512]{2,1,0:T(8,128)(2,1)}), bf16[16,144,512]{2,1,0:T(8,128)(2,1)}, u32[]{:S(2)}, u32[]{:S(2)}) async-start(bf16[16,144,512]{2,1,0:T(8,128)(2,1)} %bitcast.262), calls=%async_computation.2 | async-start | bytes 4718592 | tf_op jit(solution)/shard_map/all_to_all | solution.py:1889
  1136.8 11.0 collective-permute-start.11
  1186.6 83.2 %all-to-all-start.2 = ((bf16[16,448,256]{2,1,0:T(8,128)(2,1)}), bf16[16,448,256]{2,1,0:T(8,128)(2,1)}, u32[]{:S(2)}, u32[]{:S(2)}) async-start(bf16[16,448,256]{2,1,0:T(8,128)(2,1)} %add_convert_fusion), calls=%async_computation.3 | async-start | bytes 7340032 | tf_op jit(solution)/shard_map/all_to_all | solution.py:1932
  1202.5 38.2 %collective-permute-start.15 = (f32[4096]{0:T(1024)S(1)}, f32[4096]{0:T(1024)S(1)}, u32[]{:S(2)}, u32[]{:S(2)}) collective-permute-start(f32[4096]{0:T(1024)S(1)} %slice.191), channel_id=1, source_target_pairs={{0,1},{1,0},{2,3},{3,2},{4,5},{5,4},{6,7},{7,6},{8,9},{9,8},{10,11... | collective-permute-start | bytes 49160 | tf_op jit(solution)/shard_map/ppermute | solution.py:1487
  1208.7 13.7 %slice-start = ((s8[6291456]{0:T(1024)(128)(4,1)}), s8[2097152]{0:T(1024)(128)(4,1)S(1)}, s32[]{:S(2)}) async-start(s8[6291456]{0:T(1024)(128)(4,1)} %bitcast.256), calls=%async_computation.7 | async-start | bytes 4194304
  1221.9 20.1 %collective-permute-start.14 = (bf16[64,4096]{1,0:T(8,128)(2,1)}, bf16[64,4096]{1,0:T(8,128)(2,1)}, u32[]{:S(2)}, u32[]{:S(2)}) collective-permute-start(bf16[64,4096]{1,0:T(8,128)(2,1)} %get-tuple-element.367), channel_id=1, source_target_pairs={{0,1},{1,0},{2,3},{3,2},{4,5},{5,4},{6,7},{7,6},{8,9},{9,8},{10,11... | collective-permute-start | bytes 1572872 | tf_op jit(solution)/shard_map/ppermute | solution.py:1487
  1224.8 19.2 %collective-permute-start.13 = (bf16[64,4096]{1,0:T(8,128)(2,1)}, bf16[64,4096]{1,0:T(8,128)(2,1)}, u32[]{:S(2)}, u32[]{:S(2)}) collective-permute-start(bf16[64,4096]{1,0:T(8,128)(2,1)} %get-tuple-element.369), channel_id=1, source_target_pairs={{0,1},{1,0},{2,3},{3,2},{4,5},{5,4},{6,7},{7,6},{8,9},{9,8},{10,11... | collective-permute-start | bytes 1572872 | tf_op jit(solution)/shard_map/ppermute | solution.py:1487
  (103 other events, 378.3 us)
Sparse Core Ops, SparseCore 0:
  301.4 89.3 all-gather.2
  648.1 142.8 reduce-scatter.1
  842.9 86.3 all-gather.4
